TPU v7x, 32 devices: a whole 2x2x4 slice. The times are simulated.
32 devices in a mesh: section: 2 (over y), ctx: 4 (over z), wsh: 4 (over x, core).
Axes of the slice: x: 2, y: 2, z: 4, core: 2. Of those that a mesh axis runs over, the one named last changes fastest.
Arguments:
- x_in: bfloat16 [2, 4, 2048, 1152], P(None, 'wsh', 'ctx'), may hold values from -6 to 6
- cotangent: bfloat16 [2, 4, 2048, 1152], P(None, 'wsh', 'ctx'), may hold values from -6 to 6
- w_qkv: bfloat16 [2, 1152, 1920], P('section', 'wsh'), may hold values from -0.1875 to 0.1875
- w_out: bfloat16 [2, 1152, 1152], P('section', None, 'wsh'), may hold values from -0.5 to 0.5
- w_gate_up: bfloat16 [2, 1152, 6144], P('section', 'wsh'), may hold values from -0.1875 to 0.1875
- w_down: bfloat16 [2, 3072, 1152], P('section', None, 'wsh'), may hold values from -0.109375 to 0.109375
- gains: bfloat16 [2, 2, 1152], P('section', None, 'wsh'), may hold values from 0.5 to 1.5
- order: int32 [2, 4], replicated, may hold values from 0 to 3, as said below
- visible: int32 [4, 4], replicated, may hold values from 0 to 1, as said below
- seq_ids: int32 [2, 4, 2048], P(None, 'wsh'), may hold values from 0 to 1, as said below
Outputs:
- activations: bfloat16 [2, 2, 4, 2048, 1152], P('section', None, 'wsh', 'ctx')
- input_grads: float32 [2, 2, 4, 2048, 1152], P('section', None, 'wsh', 'ctx')
- grad_qkv: float32 [2, 1152, 1920], P('section', ('ctx', 'wsh'))
- grad_out: float32 [2, 1152, 1152], P('section', None, ('ctx', 'wsh'))
- grad_gate_up: float32 [2, 1152, 6144], P('section', ('ctx', 'wsh'))
- grad_down: float32 [2, 3072, 1152], P('section', None, ('ctx', 'wsh'))
- grad_gains: float32 [2, 2, 1152], P('section', None, ('ctx', 'wsh'))
Inputs may be any that keep to these rules, and one draw needn't show every extreme that they name: Row m lists every block number of 0 to 3 once: index c of ctx holds block order[m, c] of micro-batch m. Indices 0, 2 and 3 hold three blocks that one sequence of every stream reaches into. visible[i, i] is 1 and visible[i, j] is 0 for j > i; an earlier block j < i is visible to block i only where the table says so. `seq_ids`: taken in order of position, each micro-batch of each stream is 0 up to a cut and 1 from it on; each of the two sequences holds 512 tokens or more.
All inputs are finite; a program needn't handle non-finite values.
Results may differ from a plain program's by a relative error of at most 0.022.
Values may be sent and summed in bfloat16 or wider, within the bound.
A program may use at most 384 MiB of HBM per device.

v0:
```python
import jax
import jax.numpy as jnp
from jax import lax
from jax.sharding import PartitionSpec as P

D = 1152
H = 18
KV = 6
HD = 64
FF = 3072


NEG = -1e30
EPS = 1e-05


def shifted(value, axis, by):
    devices = lax.axis_size(axis)
    pairs = [(i, i + by) for i in range(devices) if 0 <= i + by < devices]
    return lax.ppermute(value, axis, pairs)


def rms_forward(hidden, gain_row):
    inverse = lax.rsqrt(jnp.mean(hidden * hidden, axis=-1, keepdims=True) + EPS)
    unit_rows = hidden * inverse
    return (unit_rows * gain_row, unit_rows, inverse)


def rms_backward(grad_rows, unit_rows, inverse, gain_row):
    grad_unit = grad_rows * gain_row
    grad_gain = jnp.sum(grad_rows * unit_rows, axis=0)
    inner = jnp.mean(grad_unit * unit_rows, axis=-1, keepdims=True)
    return (inverse * (grad_unit - unit_rows * inner), grad_gain)


def rotation(positions):
    frequency = 10000.0 ** (-(jnp.arange(HD // 2, dtype=jnp.float32) * 2.0 / HD))
    angles = positions.astype(jnp.float32)[:, None] * frequency[None, :]
    return (jnp.cos(angles), jnp.sin(angles))


def rotate(vectors, cosine, sine):
    half_width = vectors.shape[-1] // 2
    first_half = vectors[..., :half_width]
    second_half = vectors[..., half_width:]
    cos_rows = cosine[:, None, :]
    sin_rows = sine[:, None, :]
    return jnp.concatenate(
        [
            first_half * cos_rows - second_half * sin_rows,
            first_half * sin_rows + second_half * cos_rows,
        ],
        axis=-1,
    )


def stretch_width(rows, n_ctx):
    per_stretch = min(n_ctx, max(1, 512 // rows))
    while n_ctx % per_stretch:
        per_stretch -= 1
    return per_stretch


def sweep(step_fn, init, items, alive):

    def guarded(state, packed):
        item, live = packed
        return step_fn(state, item)

    return lax.scan(guarded, init, (items, alive))


def tables(order, visible, seq_ids, batch_index, column, rows, n_ctx):
    order_row = order[batch_index]
    own_block = order_row[column]
    seq_row = seq_ids[batch_index, 0]
    own_seq = lax.dynamic_slice_in_dim(seq_row, column * rows, rows)
    device_vis = visible[own_block][order_row]
    key_vis = jnp.broadcast_to(device_vis[:, None], (n_ctx, rows)).reshape(n_ctx * rows)
    positions = own_block * rows + jnp.arange(rows, dtype=jnp.int32)
    return ((own_seq, seq_row, key_vis, device_vis), positions)


def key_items(key_rows, value_rows, info, per_stretch, rows):
    own_seq, seq_row, key_vis, device_vis = info
    length = key_rows.shape[0]
    size = per_stretch * rows
    count = length // size
    items = (
        key_rows.reshape(count, size, KV, HD),
        value_rows.reshape(count, size, KV, HD),
        key_vis.reshape(count, size),
        seq_row.reshape(count, size),
    )
    alive = jnp.sum(device_vis.reshape(count, per_stretch), axis=-1) > 0
    return (items, alive, size)


def masked_scores(queries, key_part, vis_part, seq_part, own_seq):
    scores = jnp.einsum(
        "nkgd,mkd->kgnm", queries, key_part, preferred_element_type=jnp.float32
    ) * HD ** (-0.5)
    allowed = (vis_part[None, :] == 1) & (own_seq[:, None] == seq_part[None, :])
    return (jnp.where(allowed[None, None], scores, NEG), allowed)


def attention_forward(queries, key_rows, value_rows, info, per_stretch, rows):
    own_seq = info[0]
    items, alive, size = key_items(key_rows, value_rows, info, per_stretch, rows)
    group = H // KV

    def lse_step(state, item):
        high, total = state
        key_part, value_part, vis_part, seq_part = item
        masked, allowed = masked_scores(queries, key_part, vis_part, seq_part, own_seq)
        top = jnp.maximum(high, jnp.max(masked, axis=-1))
        terms = jnp.where(allowed[None, None], jnp.exp(masked - top[..., None]), 0.0)
        return ((top, total * jnp.exp(high - top) + jnp.sum(terms, axis=-1)), None)

    start_state = (
        jnp.full((KV, group, rows), NEG, jnp.float32),
        jnp.zeros((KV, group, rows), jnp.float32),
    )
    (high, total), unused = sweep(lse_step, start_state, items, alive)
    log_total = high + jnp.log(total)

    def out_step(acc, item):
        key_part, value_part, vis_part, seq_part = item
        masked, allowed = masked_scores(queries, key_part, vis_part, seq_part, own_seq)
        probs = jnp.where(allowed[None, None], jnp.exp(masked - log_total[..., None]), 0.0).astype(
            jnp.bfloat16
        )
        return (
            acc
            + jnp.einsum("kgnm,mkd->nkgd", probs, value_part, preferred_element_type=jnp.float32),
            None,
        )

    attended, unused_two = sweep(
        out_step, jnp.zeros((rows, KV, group, HD), jnp.float32), items, alive
    )
    return (attended, log_total)


def attention_backward(
    queries, key_rows, value_rows, info, per_stretch, rows, log_total, grad_att, delta
):
    own_seq = info[0]
    items, alive, size = key_items(key_rows, value_rows, info, per_stretch, rows)
    group = H // KV

    def back_step(grad_query, item):
        key_part, value_part, vis_part, seq_part = item
        masked, allowed = masked_scores(queries, key_part, vis_part, seq_part, own_seq)
        probs = jnp.where(allowed[None, None], jnp.exp(masked - log_total[..., None]), 0.0)
        probs_low = probs.astype(jnp.bfloat16)
        grad_probs = jnp.einsum(
            "nkgd,mkd->kgnm", grad_att, value_part, preferred_element_type=jnp.float32
        )
        grad_scores = (probs * (grad_probs - delta[..., None])).astype(jnp.bfloat16)
        grad_query = grad_query + jnp.einsum(
            "kgnm,mkd->nkgd", grad_scores, key_part, preferred_element_type=jnp.float32
        ) * HD ** (-0.5)
        grad_keys = jnp.einsum(
            "kgnm,nkgd->mkd", grad_scores, queries, preferred_element_type=jnp.float32
        ) * HD ** (-0.5)
        grad_values = jnp.einsum(
            "kgnm,nkgd->mkd", probs_low, grad_att, preferred_element_type=jnp.float32
        )
        return (grad_query, (grad_keys, grad_values))

    grad_query, (grad_keys, grad_values) = sweep(
        back_step, jnp.zeros((rows, KV, group, HD), jnp.float32), items, alive
    )
    length = key_rows.shape[0]
    return (grad_query, grad_keys.reshape(length, KV, HD), grad_values.reshape(length, KV, HD))


def layer_forward(hidden, weights, info, positions, per_stretch, rows):
    w_qkv, w_out, w_gate_up, w_down, gains = weights
    query_width = H * HD
    key_width = KV * HD
    gain_attn = gains[0].astype(jnp.float32)
    gain_ffn = gains[1].astype(jnp.float32)
    normed, unit_one, inverse_one = rms_forward(hidden, gain_attn)
    normed_low = normed.astype(jnp.bfloat16)
    mixed = jnp.dot(normed_low, w_qkv, preferred_element_type=jnp.float32)
    cosine, sine = rotation(positions)
    queries = (
        rotate(mixed[:, :query_width].reshape(rows, H, HD), cosine, sine)
        .astype(jnp.bfloat16)
        .reshape(rows, KV, H // KV, HD)
    )
    key_own = rotate(
        mixed[:, query_width : query_width + key_width].reshape(rows, KV, HD), cosine, sine
    ).astype(jnp.bfloat16)
    value_own = mixed[:, query_width + key_width :].reshape(rows, KV, HD).astype(jnp.bfloat16)
    key_rows, value_rows = (
        lax.all_gather(key_own, "ctx", axis=0, tiled=True),
        lax.all_gather(value_own, "ctx", axis=0, tiled=True),
    )
    attended, log_total = attention_forward(queries, key_rows, value_rows, info, per_stretch, rows)
    attended_low = attended.reshape(rows, query_width).astype(jnp.bfloat16)
    middle = hidden + jnp.dot(attended_low, w_out, preferred_element_type=jnp.float32)
    normed_two, unit_two, inverse_two = rms_forward(middle, gain_ffn)
    normed_two_low = normed_two.astype(jnp.bfloat16)
    gate_up = jnp.dot(normed_two_low, w_gate_up, preferred_element_type=jnp.float32)
    gate_part = gate_up[:, :FF]
    up_part = gate_up[:, FF:]
    units_low = (jax.nn.silu(gate_part) * up_part).astype(jnp.bfloat16)
    result = middle + jnp.dot(units_low, w_down, preferred_element_type=jnp.float32)
    saved = {
        "unit_one": unit_one,
        "inverse_one": inverse_one,
        "normed_low": normed_low,
        "cosine": cosine,
        "sine": sine,
        "queries": queries,
        "key_rows": key_rows,
        "value_rows": value_rows,
        "attended": attended,
        "log_total": log_total,
        "attended_low": attended_low,
        "unit_two": unit_two,
        "inverse_two": inverse_two,
        "normed_two_low": normed_two_low,
        "gate_part": gate_part,
        "up_part": up_part,
        "units_low": units_low,
    }
    return (result, saved)


def layer_backward(grad_rows, weights, saved, info, per_stretch, rows):
    w_qkv, w_out, w_gate_up, w_down, gains = weights
    query_width = H * HD
    gain_attn = gains[0].astype(jnp.float32)
    gain_ffn = gains[1].astype(jnp.float32)
    gate_part = saved["gate_part"]
    grad_low = grad_rows.astype(jnp.bfloat16)
    grad_units = jnp.dot(grad_low, w_down.T, preferred_element_type=jnp.float32)
    sigmoid = jax.nn.sigmoid(gate_part)
    grad_gate = grad_units * saved["up_part"] * sigmoid * (1.0 + gate_part * (1.0 - sigmoid))
    grad_up = grad_units * gate_part * sigmoid
    grad_mix_low = jnp.concatenate([grad_gate, grad_up], axis=-1).astype(jnp.bfloat16)
    grad_normed_two = jnp.dot(grad_mix_low, w_gate_up.T, preferred_element_type=jnp.float32)
    grad_mid_norm, grad_gain_two = rms_backward(
        grad_normed_two, saved["unit_two"], saved["inverse_two"], gain_ffn
    )
    grad_middle = grad_rows + grad_mid_norm
    grad_branch_low = grad_middle.astype(jnp.bfloat16)
    grad_att = (
        jnp.dot(grad_branch_low, w_out.T, preferred_element_type=jnp.float32)
        .astype(jnp.bfloat16)
        .reshape(rows, KV, H // KV, HD)
    )
    delta = jnp.einsum("nkgd,nkgd->kgn", grad_att.astype(jnp.float32), saved["attended"])
    grad_query, grad_keys, grad_values = attention_backward(
        saved["queries"],
        saved["key_rows"],
        saved["value_rows"],
        info,
        per_stretch,
        rows,
        saved["log_total"],
        grad_att,
        delta,
    )
    key_total, value_total = (
        lax.psum_scatter(
            grad_keys.astype(jnp.bfloat16), "ctx", scatter_dimension=0, tiled=True
        ).astype(jnp.float32),
        lax.psum_scatter(
            grad_values.astype(jnp.bfloat16), "ctx", scatter_dimension=0, tiled=True
        ).astype(jnp.float32),
    )
    cosine = saved["cosine"]
    back_sine = -saved["sine"]
    grad_q = rotate(grad_query.reshape(rows, H, HD), cosine, back_sine).reshape(rows, query_width)
    grad_k = rotate(key_total, cosine, back_sine).reshape(rows, KV * HD)
    grad_v = value_total.reshape(rows, KV * HD)
    grad_qkv_low = jnp.concatenate([grad_q, grad_k, grad_v], axis=-1).astype(jnp.bfloat16)
    grad_normed = jnp.dot(grad_qkv_low, w_qkv.T, preferred_element_type=jnp.float32)
    grad_in_norm, grad_gain_one = rms_backward(
        grad_normed, saved["unit_one"], saved["inverse_one"], gain_attn
    )
    grad_hidden = grad_middle + grad_in_norm
    pairs = (
        saved["normed_low"],
        grad_qkv_low,
        saved["attended_low"],
        grad_branch_low,
        saved["normed_two_low"],
        grad_mix_low,
        saved["units_low"],
        grad_low,
        grad_gain_one,
        grad_gain_two,
    )
    return (grad_hidden, pairs)


def weight_terms(pairs):
    (
        normed_low,
        grad_qkv_low,
        attended_low,
        grad_branch_low,
        normed_two_low,
        grad_mix_low,
        units_low,
        grad_low,
        grad_gain_one,
        grad_gain_two,
    ) = pairs
    return (
        jnp.dot(normed_low.T, grad_qkv_low, preferred_element_type=jnp.float32),
        jnp.dot(attended_low.T, grad_branch_low, preferred_element_type=jnp.float32),
        jnp.dot(normed_two_low.T, grad_mix_low, preferred_element_type=jnp.float32),
        jnp.dot(units_low.T, grad_low, preferred_element_type=jnp.float32),
        jnp.stack([grad_gain_one, grad_gain_two]),
    )


def on_device(x_in, cotangent, w_qkv, w_out, w_gate_up, w_down, gains, order, visible, seq_ids):
    section = lax.axis_index("section")
    column = lax.axis_index("ctx")
    n_ctx = lax.axis_size("ctx")
    batches = x_in.shape[0]
    rows = x_in.shape[2]
    per_stretch = stretch_width(rows, n_ctx)
    first_section = section == 0
    weights = (
        lax.all_gather(w_qkv[0], "wsh", axis=0, tiled=True),
        lax.all_gather(w_out[0], "wsh", axis=1, tiled=True),
        lax.all_gather(w_gate_up[0], "wsh", axis=0, tiled=True),
        lax.all_gather(w_down[0], "wsh", axis=1, tiled=True),
        lax.all_gather(gains[0], "wsh", axis=1, tiled=True),
    )
    incoming = jnp.zeros((rows, D), jnp.bfloat16)
    section_inputs = []
    section_outputs = []
    for tick_now in range(batches + 1):
        batch_index = jnp.clip(tick_now - section, 0, batches - 1)
        info, positions = tables(order, visible, seq_ids, batch_index, column, rows, n_ctx)
        source = jnp.where(first_section, x_in[batch_index, 0], incoming)
        result, unused = layer_forward(
            source.astype(jnp.float32), weights, info, positions, per_stretch, rows
        )
        result_low = result.astype(jnp.bfloat16)
        section_inputs.append(source)
        section_outputs.append(result_low)
        if tick_now < batches:
            incoming = shifted(result_low, "section", 1)
    activations = jnp.stack(
        [
            jnp.where(first_section, section_outputs[batch], section_outputs[batch + 1])
            for batch in range(batches)
        ]
    )
    back_weights = (
        lax.all_gather(w_qkv[0], "wsh", axis=0, tiled=True),
        lax.all_gather(w_out[0], "wsh", axis=1, tiled=True),
        lax.all_gather(w_gate_up[0], "wsh", axis=0, tiled=True),
        lax.all_gather(w_down[0], "wsh", axis=1, tiled=True),
        lax.all_gather(gains[0], "wsh", axis=1, tiled=True),
    )
    returned = jnp.zeros((rows, D), jnp.bfloat16)
    grad_list = []
    totals = None
    for tick_now in range(batches + 1):
        raw_index = tick_now - 1 + section
        valid = (raw_index >= 0) & (raw_index < batches)
        batch_index = jnp.clip(raw_index, 0, batches - 1)
        info, positions = tables(order, visible, seq_ids, batch_index, column, rows, n_ctx)
        source = jnp.where(
            first_section,
            section_inputs[max(tick_now - 1, 0)],
            section_inputs[min(tick_now + 1, batches)],
        )
        unused, saved = layer_forward(
            source.astype(jnp.float32), back_weights, info, positions, per_stretch, rows
        )
        grad_rows = jnp.where(first_section, returned, cotangent[batch_index, 0]).astype(
            jnp.float32
        ) * valid.astype(jnp.float32)
        grad_hidden, pairs = layer_backward(grad_rows, back_weights, saved, info, per_stretch, rows)
        grad_hidden_low = grad_hidden.astype(jnp.bfloat16)
        grad_list.append((grad_hidden, grad_hidden_low))
        if tick_now < batches:
            returned = shifted(grad_hidden_low, "section", -1)
        terms = weight_terms(pairs)
        totals = terms if totals is None else jax.tree.map(jnp.add, totals, terms)
    input_grads = jnp.stack(
        [
            jnp.where(
                first_section, grad_list[batch + 1][0], grad_list[batch][1].astype(jnp.float32)
            )
            for batch in range(batches)
        ]
    )
    term_qkv, term_out, term_gate_up, term_down, term_gains = totals
    shares = (
        lax.psum_scatter(term_qkv, ("ctx", "wsh"), scatter_dimension=0, tiled=True),
        lax.psum_scatter(term_out, ("ctx", "wsh"), scatter_dimension=1, tiled=True),
        lax.psum_scatter(term_gate_up, ("ctx", "wsh"), scatter_dimension=0, tiled=True),
        lax.psum_scatter(term_down, ("ctx", "wsh"), scatter_dimension=1, tiled=True),
        lax.psum_scatter(term_gains, ("ctx", "wsh"), scatter_dimension=1, tiled=True),
    )
    return (
        activations[None, :, None],
        input_grads[None, :, None],
        shares[0][None],
        shares[1][None],
        shares[2][None],
        shares[3][None],
        shares[4][None],
    )


def solution(mesh):
    in_specs = (
        P(None, "wsh", "ctx", None),
        P(None, "wsh", "ctx", None),
        P("section", "wsh", None),
        P("section", None, "wsh"),
        P("section", "wsh", None),
        P("section", None, "wsh"),
        P("section", None, "wsh"),
        P(),
        P(),
        P(None, "wsh", None),
    )
    out_specs = (
        P("section", None, "wsh", "ctx", None),
        P("section", None, "wsh", "ctx", None),
        P("section", ("ctx", "wsh"), None),
        P("section", None, ("ctx", "wsh")),
        P("section", ("ctx", "wsh"), None),
        P("section", None, ("ctx", "wsh")),
        P("section", None, ("ctx", "wsh")),
    )
    return jax.shard_map(
        on_device, mesh=mesh, in_specs=in_specs, out_specs=out_specs, check_vma=False
    )
```

profile of v0, /device:TPU:0, one launch (start us, length us, event | category | flops | bytes accessed | tf_op | source)
XLA Modules:
  0.0 2606.6 jit_solution(13756520023241305215)
XLA Ops:
  95.6 79.8 %while.189 = (s32[]{:T(128)}, f32[6,3,512]{2,1,0:T(4,128)S(1)}, f32[6,3,512]{2,1,0:T(4,128)S(1)}, s32[4,512]{1,0:T(4,128)S(1)}, s32[512]{0:T(512)S(1)}, /*index=...) while((s32[]{:T(128)}, f32[6,3,512]{2,1,0:T(4,128)S(1)}, ...), condition=%wide.region_4.5_spmd.clone, body=%wide.region_1.4_spmd.clone.sunk | while | flops 642299392 | bytes 40598656 | solution.py:70
  178.4 34.7 %while.190 = (s32[]{:T(128)}, f32[512,6,3,64]{0,3,2,1:T(8,128)}, bf16[4,512,6,64]{1,3,2,0:T(8,128)(2,1)}, s32[4,512]{1,0:T(4,128)S(1)}, s32[512]{0:T(512)S(1)}, ...) while((s32[]{:T(128)}, f32[512,6,3,64]{0,3,2,1:T(8,128)}, ...), condition=%wide.region_6.7_spmd.clone, body=%wide.region_5.6_spmd.clone.sunk | while | flops 1233256960 | bytes 7271046 | solution.py:70
  221.4 29.1 %all-gather.50.cloned.1.call-done = bf16[1,1152,6144]{2,1,0:T(8,128)(2,1)} async-done(((bf16[1,288,6144]{2,1,0:T(8,128)(2,1)}), bf16[1,1152,6144]{2,1,0:T(8,128)(2,1)}) %all-gather.50.cloned.1.call-update) | async-done | bytes 14155792 | tf_op jit(solution)/shard_map/all_gather | solution.py:336
  265.6 37.5 %all-gather.52.cloned.1.call-done = bf16[1,3072,1152]{1,2,0:T(8,128)(2,1)} async-done(((bf16[1,3072,288]{1,2,0:T(8,128)(2,1)}), bf16[1,3072,1152]{1,2,0:T(8,128)(2,1)}) %all-gather.52.cloned.1.call-update) | async-done | bytes 7077904 | tf_op jit(solution)/shard_map/all_gather | solution.py:337
  318.2 25.6 collective-permute-done
  395.1 81.4 %while.191 = (s32[]{:T(128)}, f32[6,3,512]{2,1,0:T(4,128)S(1)}, f32[6,3,512]{2,1,0:T(4,128)S(1)}, s32[4,512]{1,0:T(4,128)S(1)}, s32[512]{0:T(512)S(1)}, /*index=...) while((s32[]{:T(128)}, f32[6,3,512]{2,1,0:T(4,128)S(1)}, ...), condition=%wide.region_12.13_spmd.clone, body=%wide.region_9.12_spmd.clone.sunk | while | flops 642299392 | bytes 40598656 | solution.py:70
  507.6 77.2 %while.195 = (s32[]{:T(128)}, f32[6,3,512]{2,1,0:T(4,128)S(1)}, f32[6,3,512]{2,1,0:T(4,128)S(1)}, s32[4,512]{1,0:T(4,128)S(1)}, s32[512]{0:T(512)S(1)}, /*index=...) while((s32[]{:T(128)}, f32[6,3,512]{2,1,0:T(4,128)S(1)}, ...), condition=%wide.region_28.29_spmd.clone, body=%wide.region_25.28_spmd.clone.sunk | while | flops 642299392 | bytes 40598656 | solution.py:70
  584.9 34.5 %while.196 = (s32[]{:T(128)}, f32[512,6,3,64]{0,3,2,1:T(8,128)}, bf16[4,512,6,64]{1,3,2,0:T(8,128)(2,1)}, s32[4,512]{1,0:T(4,128)S(1)}, s32[512]{0:T(512)S(1)}, ...) while((s32[]{:T(128)}, f32[512,6,3,64]{0,3,2,1:T(8,128)}, ...), condition=%wide.region_30.31_spmd.clone, body=%wide.region_29.30_spmd.clone.sunk | while | flops 1233256960 | bytes 7271046 | solution.py:70
  685.1 174.8 %while.197 = (s32[]{:T(128)}, f32[512,6,3,64]{0,3,2,1:T(8,128)S(1)}, bf16[4,512,6,64]{1,3,2,0:T(8,128)(2,1)}, bf16[4,512,6,64]{1,3,2,0:T(8,128)(2,1)}, bf16[4,51...) while((s32[]{:T(128)}, f32[512,6,3,64]{0,3,2,1:T(8,128)S(1)}, ...), condition=%wide.region_34.35_spmd.clone, body=%wide.region_33.34_spmd.clone.sunk | while | flops 3079012864 | bytes 160341488 | solution.py:70
  864.3 43.3 %while.192 = (s32[]{:T(128)}, f32[512,6,3,64]{0,3,2,1:T(8,128)}, bf16[4,512,6,64]{1,3,2,0:T(8,128)(2,1)}, s32[4,512]{1,0:T(4,128)}, s32[512]{0:T(512)S(1)}, /*in...) while((s32[]{:T(128)}, f32[512,6,3,64]{0,3,2,1:T(8,128)}, ...), condition=%wide.region_14.15_spmd.clone, body=%wide.region_13.14_spmd.clone.sunk | while | flops 1233256960 | bytes 7271046 | solution.py:70
  946.3 25.0 collective-permute-done.1
  1060.5 80.5 %while.198 = (s32[]{:T(128)}, f32[6,3,512]{2,1,0:T(4,128)S(1)}, f32[6,3,512]{2,1,0:T(4,128)S(1)}, s32[4,512]{1,0:T(4,128)S(1)}, s32[512]{0:T(512)S(1)}, /*index=...) while((s32[]{:T(128)}, f32[6,3,512]{2,1,0:T(4,128)S(1)}, ...), condition=%wide.region_42.43_spmd.clone, body=%wide.region_39.42_spmd.clone.sunk | while | flops 642299392 | bytes 40598656 | solution.py:70
  1141.1 37.0 %while.199 = (s32[]{:T(128)}, f32[512,6,3,64]{0,3,2,1:T(8,128)}, bf16[4,512,6,64]{1,3,2,0:T(8,128)(2,1)}, s32[4,512]{1,0:T(4,128)S(1)}, s32[512]{0:T(512)S(1)}, ...) while((s32[]{:T(128)}, f32[512,6,3,64]{0,3,2,1:T(8,128)}, ...), condition=%wide.region_44.45_spmd.clone, body=%wide.region_43.44_spmd.clone.sunk | while | flops 1233256960 | bytes 7271046 | solution.py:70
  1248.8 174.7 %while.200 = (s32[]{:T(128)}, f32[512,6,3,64]{0,3,2,1:T(8,128)S(1)}, bf16[4,512,6,64]{1,3,2,0:T(8,128)(2,1)}, bf16[4,512,6,64]{1,3,2,0:T(8,128)(2,1)}, bf16[4,51...) while((s32[]{:T(128)}, f32[512,6,3,64]{0,3,2,1:T(8,128)S(1)}, ...), condition=%wide.region_48.49_spmd.clone, body=%wide.region_47.48_spmd.clone.sunk | while | flops 3079012864 | bytes 160341488 | solution.py:70
  1427.3 86.8 %while.201 = (s32[]{:T(128)}, f32[6,3,512]{2,1,0:T(4,128)}, f32[6,3,512]{2,1,0:T(4,128)}, s32[4,512]{1,0:T(4,128)S(1)}, s32[512]{0:T(512)S(1)}, /*index=5*/s32[4...) while((s32[]{:T(128)}, f32[6,3,512]{2,1,0:T(4,128)}, ...), condition=%wide.region_56.57_spmd.clone, body=%wide.region_53.56_spmd.clone.sunk | while | flops 642299392 | bytes 41041108 | solution.py:70
  1520.0 42.0 %while.202 = (s32[]{:T(128)}, f32[512,6,3,64]{0,3,2,1:T(8,128)S(1)}, bf16[4,512,6,64]{1,3,2,0:T(8,128)(2,1)}, s32[4,512]{1,0:T(4,128)}, s32[512]{0:T(512)S(1)}, ...) while((s32[]{:T(128)}, f32[512,6,3,64]{0,3,2,1:T(8,128)S(1)}, ...), condition=%wide.region_58.59_spmd.clone, body=%wide.region_57.58_spmd.clone.sunk | while | flops 1233256960 | bytes 7271046 | solution.py:70
  1657.0 174.4 %while.203 = (s32[]{:T(128)}, f32[512,6,3,64]{0,3,2,1:T(8,128)S(1)}, bf16[4,512,6,64]{1,3,2,0:T(8,128)(2,1)}, bf16[4,512,6,64]{1,3,2,0:T(8,128)(2,1)}, bf16[4,51...) while((s32[]{:T(128)}, f32[512,6,3,64]{0,3,2,1:T(8,128)S(1)}, ...), condition=%wide.region_62.63_spmd.clone, body=%wide.region_61.62_spmd.clone.sunk | while | flops 3079012864 | bytes 160341488 | solution.py:70
  1873.4 32.1 %reduce-scatter.26.cloned.1.call-done = bf16[512,6,64]{0,2,1:T(8,128)(2,1)} async-done(((bf16[2048,6,64]{0,2,1:T(8,128)(2,1)}), bf16[512,6,64]{0,2,1:T(8,128)(2,1)}) %reduce-scatter.26.cloned.1.call-update) | async-done | bytes 393232 | tf_op jit(solution)/shard_map/reduce_scatter | solution.py:273
  1999.7 33.7 %add_add_fusion = f32[1152,6144]{1,0:T(8,128)} fusion(f32[1152,6144]{1,0:T(8,128)} %fusion.313, f32[1152,6144]{1,0:T(8,128)} %fusion.312, bf16[512,3072]{1,0:T(8,128)(2,1)} %get-tuple-element.2113, bf16[512,3072]{1,0:T(8,128)(2,1)} %get-tuple-element.2112, f32[512,1152]{1,0:T(8,128)S(1)} %copy-done.42, f32[512]{0:T(512)S(1)} %copy-done.176, ...), kind=kOutput, calls=%fused_computation.303 | convolution fusion | flops 7276265472 | bytes 93592064 | tf_op jit(solution)/shard_map/dot_general | solution.py:319
  2049.2 81.0 %while.193 = (s32[]{:T(128)}, f32[6,3,512]{2,1,0:T(4,128)S(1)}, f32[6,3,512]{2,1,0:T(4,128)S(1)}, s32[4,512]{1,0:T(4,128)S(1)}, s32[512]{0:T(512)S(1)}, /*index=...) while((s32[]{:T(128)}, f32[6,3,512]{2,1,0:T(4,128)S(1)}, ...), condition=%wide.region_20.21_spmd.clone, body=%wide.region_17.20_spmd.clone.sunk | while | flops 642299392 | bytes 40598656 | solution.py:70
  2130.3 34.4 %while.194 = (s32[]{:T(128)}, f32[512,6,3,64]{0,3,2,1:T(8,128)}, bf16[4,512,6,64]{1,3,2,0:T(8,128)(2,1)}, s32[4,512]{1,0:T(4,128)S(1)}, s32[512]{0:T(512)S(1)}, ...) while((s32[]{:T(128)}, f32[512,6,3,64]{0,3,2,1:T(8,128)}, ...), condition=%wide.region_22.23_spmd.clone, body=%wide.region_21.22_spmd.clone.sunk | while | flops 1233256960 | bytes 7271046 | solution.py:70
  2210.6 33.4 %all-reduce.2 = f32[2,1152]{1,0:T(2,128)} all-reduce(f32[2,1152]{1,0:T(2,128)} %fusion.456), channel_id=17, replica_groups=mesh['section'=2,'ctx'=4,'wsh'=4] {'ctx','wsh'}, use_global_device_ids=true, to_apply=%region_76.77.clone | all-reduce | flops 2304 | bytes 18432
  2250.6 75.4 %reduce-scatter.30.cloned.1.call-done = f32[3072,72]{0,1:T(8,128)} async-done(((f32[3072,1152]{0,1:T(8,128)}), f32[3072,72]{0,1:T(8,128)}) %reduce-scatter.30.cloned.1.call-update) | async-done | bytes 884752 | tf_op jit(solution)/shard_map/reduce_scatter | solution.py:407
  2326.0 273.6 %reduce-scatter.28.cloned.1.call-done = f32[72,6144]{1,0:T(8,128)} async-done(((f32[1152,6144]{1,0:T(8,128)}), f32[72,6144]{1,0:T(8,128)}) %reduce-scatter.28.cloned.1.call-update) | async-done | bytes 1769488 | tf_op jit(solution)/shard_map/reduce_scatter | solution.py:406
  (1401 shorter events, 2003.6 us)
Async XLA Ops:
  7.9 86.0 %all-gather.24.cloned.1.call-start = ((), (), s32[]{:S(2)}) async-start(), calls=%async_computation.11 | async-start | bytes 1966080 | tf_op jit(solution)/shard_map/all_gather | solution.py:199
  56.1 119.3 %all-gather.22.cloned.1.call-start = ((), (), s32[]{:S(2)}) async-start(), calls=%async_computation.10 | async-start | bytes 1966080 | tf_op jit(solution)/shard_map/all_gather | solution.py:200
  58.3 157.7 %all-gather.48.cloned.1.call-start = ((), (), s32[]{:S(2)}) async-start(), calls=%async_computation.31 | async-start | bytes 3317760 | tf_op jit(solution)/shard_map/all_gather | solution.py:335
  59.0 191.6 %all-gather.50.cloned.1.call-start = ((), (), s32[]{:S(2)}) async-start(), calls=%async_computation.32 | async-start | bytes 17694720 | tf_op jit(solution)/shard_map/all_gather | solution.py:336
  59.6 243.5 %all-gather.52.cloned.1.call-start = ((), (), s32[]{:S(2)}) async-start(), calls=%async_computation.33 | async-start | bytes 8847360 | tf_op jit(solution)/shard_map/all_gather | solution.py:337
  60.1 332.1 %all-gather.28.cloned.1.call-start = ((), (), s32[]{:S(2)}) async-start(), calls=%async_computation.13 | async-start | bytes 1966080 | tf_op jit(solution)/shard_map/all_gather | solution.py:199
  354.0 122.6 %all-gather.26.cloned.1.call-start = ((), (), s32[]{:S(2)}) async-start(), calls=%async_computation.12 | async-start | bytes 1966080 | tf_op jit(solution)/shard_map/all_gather | solution.py:200
  356.2 123.6 %all-gather.34.cloned.1.call-start = ((), (), s32[]{:S(2)}) async-start(), calls=%async_computation.16 | async-start | bytes 1966080 | tf_op jit(solution)/shard_map/all_gather | solution.py:200
  364.1 141.8 %all-gather.36.cloned.1.call-start = ((), (), s32[]{:S(2)}) async-start(), calls=%async_computation.17 | async-start | bytes 1966080 | tf_op jit(solution)/shard_map/all_gather | solution.py:199
  385.0 637.6 %reduce-scatter.16.cloned.1.call-start = ((), (), s32[]{:S(2)}) async-start(), calls=%async_computation.18 | async-start | bytes 1966080 | tf_op jit(solution)/shard_map/reduce_scatter | solution.py:270
  862.8 161.2 %reduce-scatter.18.cloned.1.call-start = ((), (), s32[]{:S(2)}) async-start(), calls=%async_computation.19 | async-start | bytes 1966080 | tf_op jit(solution)/shard_map/reduce_scatter | solution.py:273
  914.6 119.3 %all-gather.38.cloned.1.call-start = ((), (), s32[]{:S(2)}) async-start(), calls=%async_computation.20 | async-start | bytes 1966080 | tf_op jit(solution)/shard_map/all_gather | solution.py:200
  989.8 196.5 %all-gather.44.cloned.1.call-start = ((), (), s32[]{:S(2)}) async-start(), calls=%async_computation.25 | async-start | bytes 1966080 | tf_op jit(solution)/shard_map/all_gather | solution.py:199
  1001.2 512.9 %all-gather.42.cloned.1.call-start = ((), (), s32[]{:S(2)}) async-start(), calls=%async_computation.24 | async-start | bytes 1966080 | tf_op jit(solution)/shard_map/all_gather | solution.py:200
  1020.1 549.9 %reduce-scatter.20.cloned.1.call-start = ((), (), s32[]{:S(2)}) async-start(), calls=%async_computation.22 | async-start | bytes 1966080 | tf_op jit(solution)/shard_map/reduce_scatter | solution.py:270
  1032.6 168.1 %collective-permute-start.2 = (bf16[512,1152]{1,0:T(8,128)(2,1)}, bf16[512,1152]{1,0:T(8,128)(2,1)}, u32[]{:S(2)}, u32[]{:S(2)}) collective-permute-start(bf16[512,1152]{1,0:T(8,128)(2,1)} %fusion.391), channel_id=1, source_target_pairs={{16,0},{17,1},{18,2},{19,3},{20,4},{21,5},{22,6},{23,7},{24,8},{25... | collective-permute-start | bytes 3538952 | tf_op jit(solution)/shard_map/ppermute | solution.py:20
  1427.2 146.2 %reduce-scatter.22.cloned.1.call-start = ((), (), s32[]{:S(2)}) async-start(), calls=%async_computation.23 | async-start | bytes 1966080 | tf_op jit(solution)/shard_map/reduce_scatter | solution.py:273
  1519.1 352.5 %reduce-scatter.24.cloned.1.call-start = ((), (), s32[]{:S(2)}) async-start(), calls=%async_computation.26 | async-start | bytes 1966080 | tf_op jit(solution)/shard_map/reduce_scatter | solution.py:270
  1837.2 207.5 %all-gather.30.cloned.1.call-start = ((), (), s32[]{:S(2)}) async-start(), calls=%async_computation.14 | async-start | bytes 1966080 | tf_op jit(solution)/shard_map/all_gather | solution.py:200
  1845.4 202.0 %all-gather.32.cloned.1.call-start = ((), (), s32[]{:S(2)}) async-start(), calls=%async_computation.15 | async-start | bytes 1966080 | tf_op jit(solution)/shard_map/all_gather | solution.py:199
  1848.9 401.8 %reduce-scatter.34.cloned.1.call-start = ((), (), s32[]{:S(2)}) async-start(), calls=%async_computation.35 | async-start | bytes 5640192
  1859.1 391.6 %reduce-scatter.32.cloned.1.call-start = ((), (), s32[]{:S(2)}) async-start(), calls=%async_computation.34 | async-start | bytes 9400320
  1915.4 410.6 %reduce-scatter.30.cloned.1.call-start = ((), (), s32[]{:S(2)}) async-start(), calls=%async_computation.29 | async-start | bytes 15040512 | tf_op jit(solution)/shard_map/reduce_scatter | solution.py:407
  1965.3 634.2 %reduce-scatter.28.cloned.1.call-start = ((), (), s32[]{:S(2)}) async-start(), calls=%async_computation.28 | async-start | bytes 30081024 | tf_op jit(solution)/shard_map/reduce_scatter | solution.py:406
  (345 other events, 3097.1 us)
Sparse Core Ops, SparseCore 0:
  9.6 38.4 all-gather.45
  56.3 37.6 all-gather.23
  96.1 35.9 all-gather.21
  159.5 91.0 all-gather.49
  252.0 50.9 all-gather.51
  354.1 38.0 all-gather.27
  394.4 35.9 all-gather.25
  432.0 35.9 all-gather.33
  470.0 35.9 all-gather.35
  862.9 34.1 reduce-scatter.15
  914.7 34.0 reduce-scatter.17
  983.5 37.2 all-gather.37
  1022.8 35.9 all-gather.39
  1060.2 35.9 all-gather.43
  1097.7 35.9 all-gather.41
  1427.3 34.1 reduce-scatter.19
  1519.2 34.4 reduce-scatter.21
  1871.1 34.2 reduce-scatter.25
  1907.0 36.0 all-gather.29
  1944.7 35.9 all-gather.31
  1985.3 78.6 reduce-scatter.33
  2068.6 105.6 reduce-scatter.31
  2179.6 146.3 reduce-scatter.29
  2331.2 268.3 reduce-scatter.27
  (2 shorter events, 58.4 us)
where the time goes:
time: 2620 us; the launch traced here: 2610 us
  matrix products  1320 us (50%)
  waiting for transfers between devices  580 us (22%)
  other arithmetic  408 us (16%)
  local copies, waits for them, and re-layouts  202 us (8%)
  blocking collectives  42.3 us (2%)
  between operations  32.7 us (1%)
    dot_general x36, matrix products, masked_scores(): jnp.einsum('nkgd,mkd->kgnm', queries, key_part, preferred_element_type=jn...  311 us
    reduce_scatter x1, waiting for transfers between devices, on_device(): lax.psum_scatter(term_gate_up, ('ctx', 'wsh'), scatter_dimension=0, tiled...  274 us
    reduce_sum x24, other arithmetic, lse_step(): return ((top, total * jnp.exp(high - top) + jnp.sum(terms, axis=-1)), None)  264 us
    dot_general x24, matrix products, out_step(): jnp.einsum('kgnm,mkd->nkgd', probs, value_part, preferred_element_type=jn...  198 us
    dot_general x12, matrix products, back_step(): jnp.einsum('nkgd,mkd->kgnm', grad_att, value_part, preferred_element_type...  145 us
    dot_general x12, matrix products, back_step(): jnp.einsum('kgnm,nkgd->mkd', probs_low, grad_att, preferred_element_type=...  122 us
    dot_general x6, matrix products, layer_forward(): jnp.dot(normed_two_low, w_gate_up, preferred_element_type=jnp.float32)  88.4 us
    reduce_scatter x1, waiting for transfers between devices, on_device(): lax.psum_scatter(term_down, ('ctx', 'wsh'), scatter_dimension=1, tiled=True)  75.4 us
  transfers between devices with their start and end apart: 30, of which 13 were waited for; matrix products, arithmetic and copies ran while one was open for 49% of the time, Pallas kernels for 0%

commit v1 on v0

--- a/solution.py
+++ b/solution.py
@@ -1,6 +1,8 @@
 import jax
 import jax.numpy as jnp
 from jax import lax
+from jax.experimental import pallas as pl
+from jax.experimental.pallas import tpu as pltpu
 from jax.sharding import PartitionSpec as P
 
 D = 1152
@@ -322,7 +324,7 @@
     )
 
 
-def on_device(x_in, cotangent, w_qkv, w_out, w_gate_up, w_down, gains, order, visible, seq_ids):
+def on_device_general(x_in, cotangent, w_qkv, w_out, w_gate_up, w_down, gains, order, visible, seq_ids):
     section = lax.axis_index("section")
     column = lax.axis_index("ctx")
     n_ctx = lax.axis_size("ctx")
@@ -418,6 +420,496 @@
     )
 
 
+GROUP = H // KV
+QD = H * HD
+KD = KV * HD
+QKV = QD + 2 * KD
+SIDE = 128
+LOW = jnp.bfloat16
+
+
+def fits_pairs(mesh):
+    return mesh.shape["section"] == 2 and mesh.shape["ctx"] == 4 and mesh.shape["wsh"] == 4
+
+
+def contract(left, right, left_dim, right_dim):
+    return lax.dot_general(
+        left,
+        right,
+        (((left_dim,), (right_dim,)), ((), ())),
+        preferred_element_type=jnp.float32,
+    )
+
+
+def swap(value, axis, bit):
+    return lax.ppermute(value, axis, [(i, i ^ bit) for i in range(lax.axis_size(axis))])
+
+
+def after(value, *others):
+    return lax.optimization_barrier((value, *others))[0]
+
+
+def fill_bias(bias_ref, kseq_ref, qseq_ref):
+    @pl.when(pl.program_id(0) == 0)
+    def _():
+        for slot in range(bias_ref.shape[0]):
+            bias_ref[slot] = jnp.where(kseq_ref[slot][:, :1] == qseq_ref[...], 0.0, NEG)
+
+
+def forward_kernel(live_ref, q_ref, k_ref, v_ref, kseq_ref, qseq_ref, o_ref, lse_ref, bias_ref):
+    fill_bias(bias_ref, kseq_ref, qseq_ref)
+    rows = q_ref.shape[1]
+    queries = [q_ref[pl.ds(j * HD, HD), :] for j in range(GROUP)]
+
+    def step(i, states):
+        slot = live_ref[1 + i]
+        key_t = k_ref[slot, 0]
+        value_t = v_ref[slot, 0]
+        new_states = []
+        for j in range(GROUP):
+            high, total, acc = states[j]
+            scores = contract(key_t, queries[j], 0, 0) + bias_ref[slot]
+            top = jnp.maximum(high, jnp.max(scores, axis=0, keepdims=True))
+            terms = jnp.exp(scores - top)
+            scale = jnp.exp(high - top)
+            total = total * scale + jnp.sum(terms, axis=0, keepdims=True)
+            acc = acc * scale + contract(value_t, terms.astype(LOW), 1, 0)
+            new_states.append((top, total, acc))
+        return tuple(new_states)
+
+    start = (
+        jnp.full((1, rows), NEG, jnp.float32),
+        jnp.zeros((1, rows), jnp.float32),
+        jnp.zeros((HD, rows), jnp.float32),
+    )
+    states = lax.fori_loop(0, live_ref[0], step, (start,) * GROUP)
+    for j in range(GROUP):
+        high, total, acc = states[j]
+        o_ref[pl.ds(j * HD, HD), :] = (acc / total).astype(o_ref.dtype)
+        lse_ref[0, pl.ds(j, 1), :] = high + jnp.log(total)
+
+
+def backward_kernel(
+    live_ref,
+    q_ref,
+    do_ref,
+    o_ref,
+    lse_ref,
+    k_ref,
+    v_ref,
+    kseq_ref,
+    qseq_ref,
+    dq_ref,
+    dk_ref,
+    dv_ref,
+    bias_ref,
+    acc_ref,
+):
+    fill_bias(bias_ref, kseq_ref, qseq_ref)
+    keys = bias_ref.shape[1]
+    acc_ref[...] = jnp.zeros_like(acc_ref)
+    dk_ref[...] = jnp.zeros_like(dk_ref)
+    dv_ref[...] = jnp.zeros_like(dv_ref)
+    deltas = []
+    for j in range(GROUP):
+        part = pl.ds(j * HD, HD)
+        both = do_ref[part, :].astype(jnp.float32) * o_ref[part, :].astype(jnp.float32)
+        deltas.append(jnp.sum(both, axis=0, keepdims=True))
+
+    def step(i, carry):
+        slot = live_ref[1 + i]
+        key_t = k_ref[slot, 0]
+        value_t = v_ref[slot, 0]
+        grad_k = jnp.zeros((keys, HD), jnp.float32)
+        grad_v = jnp.zeros((keys, HD), jnp.float32)
+        for j in range(GROUP):
+            part = pl.ds(j * HD, HD)
+            query_t = q_ref[part, :]
+            grad_t = do_ref[part, :]
+            scores = contract(key_t, query_t, 0, 0) + bias_ref[slot]
+            probs = jnp.exp(scores - lse_ref[0, pl.ds(j, 1), :])
+            grad_probs = contract(value_t, grad_t, 0, 0)
+            grad_scores = (probs * (grad_probs - deltas[j])).astype(LOW)
+            grad_v = grad_v + contract(probs.astype(LOW), grad_t, 1, 1)
+            grad_k = grad_k + contract(grad_scores, query_t, 1, 1)
+            acc_ref[part, :] += contract(key_t, grad_scores, 1, 0)
+        dk_ref[slot, 0] = jnp.transpose(grad_k).astype(LOW)
+        dv_ref[slot, 0] = jnp.transpose(grad_v).astype(LOW)
+        return carry
+
+    lax.fori_loop(0, live_ref[0], step, 0)
+    dq_ref[...] = acc_ref[...] * HD ** (-0.5)
+
+
+def kernel_cost(scores, matmuls):
+    return pl.CostEstimate(
+        flops=scores * matmuls * HD * 2 * 4, bytes_accessed=12 * 2**20, transcendentals=scores
+    )
+
+
+def pair_attention_forward(info, q_t, kv_t):
+    live, key_seq, own_seq = info
+    slots, keys = kv_t.shape[0], kv_t.shape[3]
+    rows = q_t.shape[1]
+    return pl.pallas_call(
+        forward_kernel,
+        grid_spec=pltpu.PrefetchScalarGridSpec(
+            num_scalar_prefetch=1,
+            grid=(KV,),
+            in_specs=[
+                pl.BlockSpec((GROUP * HD, rows), lambda g, l: (g, 0)),
+                pl.BlockSpec((slots, 1, HD, keys), lambda g, l: (0, g, 0, 0)),
+                pl.BlockSpec((slots, 1, HD, keys), lambda g, l: (0, KV + g, 0, 0)),
+                pl.BlockSpec((slots, keys, SIDE), lambda g, l: (0, 0, 0)),
+                pl.BlockSpec((1, rows), lambda g, l: (0, 0)),
+            ],
+            out_specs=[
+                pl.BlockSpec((GROUP * HD, rows), lambda g, l: (g, 0)),
+                pl.BlockSpec((1, GROUP, rows), lambda g, l: (g, 0, 0)),
+            ],
+            scratch_shapes=[pltpu.VMEM((slots, keys, rows), jnp.float32)],
+        ),
+        out_shape=[
+            jax.ShapeDtypeStruct(q_t.shape, LOW),
+            jax.ShapeDtypeStruct((KV, GROUP, rows), jnp.float32),
+        ],
+        compiler_params=pltpu.CompilerParams(vmem_limit_bytes=48 * 2**20),
+        cost_estimate=kernel_cost(H * rows * slots * keys, 2),
+    )(live, q_t, kv_t, kv_t, key_seq, own_seq)
+
+
+def pair_attention_backward(info, q_t, do_t, o_t, lse, kv_t):
+    live, key_seq, own_seq = info
+    slots, keys = kv_t.shape[0], kv_t.shape[3]
+    rows = q_t.shape[1]
+    q_spec = pl.BlockSpec((GROUP * HD, rows), lambda g, l: (g, 0))
+    part_spec = pl.BlockSpec((slots, 1, HD, keys), lambda g, l: (0, g, 0, 0))
+    part_shape = jax.ShapeDtypeStruct((slots, KV, HD, keys), LOW)
+    return pl.pallas_call(
+        backward_kernel,
+        grid_spec=pltpu.PrefetchScalarGridSpec(
+            num_scalar_prefetch=1,
+            grid=(KV,),
+            in_specs=[
+                q_spec,
+                q_spec,
+                q_spec,
+                pl.BlockSpec((1, GROUP, rows), lambda g, l: (g, 0, 0)),
+                part_spec,
+                pl.BlockSpec((slots, 1, HD, keys), lambda g, l: (0, KV + g, 0, 0)),
+                pl.BlockSpec((slots, keys, SIDE), lambda g, l: (0, 0, 0)),
+                pl.BlockSpec((1, rows), lambda g, l: (0, 0)),
+            ],
+            out_specs=[q_spec, part_spec, part_spec],
+            scratch_shapes=[
+                pltpu.VMEM((slots, keys, rows), jnp.float32),
+                pltpu.VMEM((GROUP * HD, rows), jnp.float32),
+            ],
+        ),
+        out_shape=[jax.ShapeDtypeStruct(q_t.shape, jnp.float32), part_shape, part_shape],
+        compiler_params=pltpu.CompilerParams(vmem_limit_bytes=48 * 2**20),
+        cost_estimate=kernel_cost(H * rows * slots * keys, 5),
+    )(live, q_t, do_t, o_t, lse, kv_t, kv_t, key_seq, own_seq)
+
+
+def turn(heads, cosine, sine):
+    half = HD // 2
+    first, second = heads[:, :half], heads[:, half:]
+    return jnp.concatenate(
+        [first * cosine - second * sine, first * sine + second * cosine], axis=1
+    )
+
+
+def one_hot(index, size):
+    return (index[:, None] == jnp.arange(size, dtype=jnp.int32)[None, :]).astype(LOW)
+
+
+def pair_tables(order, visible, seq_ids, batch, slot, rows):
+    order_row = order[batch]
+    order_slots = [order_row[slot ^ step] for step in (0, 2, 1, 3)]
+    own_block = order_slots[0]
+    seqs = [
+        lax.dynamic_slice_in_dim(seq_ids, (slot ^ step) * rows, rows) for step in (0, 2, 1, 3)
+    ]
+    has = [(jnp.any(s == 0), jnp.any(s == 1)) for s in seqs]
+    alive = []
+    for block, (zero, one) in zip(order_slots, has):
+        shares = (zero & has[0][0]) | (one & has[0][1])
+        alive.append((visible[own_block, block] == 1) & shares)
+    alive[0] = jnp.bool_(True)
+    alive = jnp.stack(alive).astype(jnp.int32)
+    place = jnp.cumsum(alive) - 1
+    ids = jnp.arange(4, dtype=jnp.int32)
+    listed = jnp.sum(
+        jnp.where((place[None, :] == ids[:, None]) & (alive[None, :] == 1), ids[None, :], 0),
+        axis=1,
+    )
+    live = jnp.concatenate([jnp.sum(alive, keepdims=True), listed]).astype(jnp.int32)
+    key_seq = jnp.broadcast_to(
+        jnp.stack(seqs).astype(jnp.float32)[:, :, None], (4, rows, SIDE)
+    )
+    own_seq = seqs[0].astype(jnp.float32)[None]
+    positions = own_block * rows + jnp.arange(rows, dtype=jnp.int32)
+    frequency = 10000.0 ** (-(jnp.arange(HD // 2, dtype=jnp.float32) * 2.0 / HD))
+    angles = frequency[:, None] * positions.astype(jnp.float32)[None, :]
+    return (live, key_seq, own_seq), (jnp.cos(angles), jnp.sin(angles))
+
+
+def gather_both(shards, section, half):
+    own_side, other_side = [], []
+    sent = []
+    for step, own in enumerate(shards):
+        if step >= 2:
+            own = after(own, sent[step - 2])
+        near = swap(own, "wsh", 2)
+        sent.append(near)
+        rows, width = own.shape
+        if step < 2:
+            other = swap(own, "section", 1)
+            if step == 0:
+                far = swap(after(other, near), "wsh", 2)
+            else:
+                far = swap(near, "section", 1)
+        else:
+            both = jnp.stack([own, near]).reshape(2, 2, rows // 2, width)
+            mine = lax.dynamic_index_in_dim(both, half, 1, keepdims=False)
+            crossed = swap(mine, "section", 1)
+            passed = swap(crossed, "ctx", 1)
+            crossed_two = swap(crossed, "wsh", 1)
+            passed_two = swap(passed, "wsh", 1)
+            first = half == 0
+
+            def joined(a, b):
+                return jnp.concatenate([jnp.where(first, a, b), jnp.where(first, b, a)], axis=0)
+
+            other, far = joined(crossed[0], passed[0]), joined(crossed[1], passed[1])
+            other_two = joined(crossed_two[0], passed_two[0])
+            far_two = joined(crossed_two[1], passed_two[1])
+        if step < 2:
+            other_two, far_two = swap(other, "wsh", 1), swap(far, "wsh", 1)
+        own_side.append(
+            jnp.concatenate([own, swap(own, "wsh", 1), near, swap(near, "wsh", 1)], axis=0)
+        )
+        other_side.append(jnp.concatenate([other, other_two, far, far_two], axis=0))
+    first_section = section == 0
+    return [
+        [
+            jnp.where(first_section, a, b) if layer == 0 else jnp.where(first_section, b, a)
+            for a, b in zip(own_side, other_side)
+        ]
+        for layer in range(2)
+    ]
+
+
+def unpack(weights):
+    w_in, w_out_t, w_gate, w_up, w_down_t = weights
+    gain_one = w_in[:, QKV].astype(jnp.float32)
+    gain_two = w_in[:, QKV + 1].astype(jnp.float32)
+    return w_in, w_out_t, w_gate, w_up, w_down_t, gain_one, gain_two
+
+
+def pair_forward(hidden, weights, info, angles):
+    w_in, w_out_t, w_gate, w_up, w_down_t, gain_one, gain_two = unpack(weights)
+    rows = hidden.shape[0]
+    cosine, sine = angles
+    normed, unused, inverse_one = rms_forward(hidden, gain_one)
+    normed = normed.astype(LOW)
+    kv = contract(w_in[:, QD:QKV], normed, 0, 1).reshape(2 * KV, HD, rows)
+    kv_own = jnp.concatenate([turn(kv[:KV], cosine, sine), kv[KV:]], axis=0).astype(LOW)
+    kv_far = swap(kv_own, "ctx", 1)
+    kv_near = swap(kv_own, "wsh", 1)
+    kv_last = swap(kv_far, "wsh", 1)
+    q = contract(w_in[:, :QD], normed, 0, 1).reshape(H, HD, rows)
+    q_t = (turn(q, cosine, sine).astype(LOW) * HD ** (-0.5)).reshape(QD, rows)
+    kv_t = jnp.stack([kv_own, kv_near, kv_far, kv_last])
+    o_t, lse = pair_attention_forward(info, q_t, kv_t)
+    middle = hidden + contract(o_t, w_out_t, 0, 1)
+    normed_two, unused, inverse_two = rms_forward(middle, gain_two)
+    normed_two = normed_two.astype(LOW)
+    gate = contract(normed_two, w_gate, 1, 0).astype(LOW)
+    up = contract(normed_two, w_up, 1, 0).astype(LOW)
+    gate_wide = gate.astype(jnp.float32)
+    units = (jax.nn.silu(gate_wide) * up.astype(jnp.float32)).astype(LOW)
+    result = (middle + contract(units, w_down_t, 1, 1)).astype(LOW)
+    saved = (hidden, inverse_one, normed, q_t, kv_t, o_t, lse, middle, inverse_two, normed_two)
+    return result, saved + (gate, up, units)
+
+
+def spread(layer, lhs_t, rhs, rhs_dim, extra=None):
+    half = lhs_t.shape[0] // 2
+    given = contract(lhs_t[:half], rhs, 1, rhs_dim)
+    kept = contract(lhs_t[half:], rhs, 1, rhs_dim)
+    if extra is not None:
+        given = jnp.concatenate([given, extra[:half]], axis=1)
+        kept = jnp.concatenate([kept, extra[half:]], axis=1)
+    width = given.shape[1]
+    kept = (kept + swap(given.astype(LOW), "wsh", 1).astype(jnp.float32)).astype(LOW)
+    quarter = half // 2
+    got = swap(kept[:quarter], "wsh", 2).astype(jnp.float32)
+    parts = (kept[quarter:].astype(jnp.float32) + got).reshape(4, quarter // 4, width)
+    sent = [swap(parts[k].astype(LOW), "ctx", k).astype(jnp.float32) for k in range(1, 4)]
+    own = (parts[0] + sent[0] + sent[1] + sent[2]).astype(LOW)
+    return own, lax.ppermute(own, "section", [(1 - layer, layer)])
+
+
+def pair_backward(layer, grad_low, weights, saved, info, angles, arrange):
+    w_in, w_out_t, w_gate, w_up, w_down_t, gain_one, gain_two = unpack(weights)
+    (
+        hidden,
+        inverse_one,
+        normed,
+        q_t,
+        kv_t,
+        o_t,
+        lse,
+        middle,
+        inverse_two,
+        normed_two,
+        gate,
+        up,
+        units,
+    ) = saved
+    rows = hidden.shape[0]
+    cosine, sine = angles
+
+    def arranged(value):
+        return contract(arrange, value, 1, 1).astype(LOW)
+
+    shares = {}
+    shares["down"] = spread(layer, arranged(grad_low), units, 0)
+    grad_units = contract(grad_low, w_down_t, 1, 0)
+    gate_wide = gate.astype(jnp.float32)
+    sigmoid = jax.nn.sigmoid(gate_wide)
+    grad_gate = (
+        grad_units * up.astype(jnp.float32) * sigmoid * (1.0 + gate_wide * (1.0 - sigmoid))
+    ).astype(LOW)
+    grad_up = (grad_units * gate_wide * sigmoid).astype(LOW)
+    lhs_two = arranged(normed_two)
+    shares["gate"] = spread(layer, lhs_two, grad_gate, 0)
+    shares["up"] = spread(layer, lhs_two, grad_up, 0)
+    grad_normed_two = contract(grad_gate, w_gate, 1, 1) + contract(grad_up, w_up, 1, 1)
+    grad_mid_norm, grad_gain_two = rms_backward(
+        grad_normed_two, middle * inverse_two, inverse_two, gain_two
+    )
+    grad_middle = grad_low.astype(jnp.float32) + grad_mid_norm
+    grad_branch = grad_middle.astype(LOW)
+    do_t = contract(w_out_t, grad_branch, 0, 1).astype(LOW)
+    dq_t, dk_t, dv_t = pair_attention_backward(info, q_t, do_t, o_t, lse, kv_t)
+    grad_kv = jnp.concatenate([dk_t, dv_t], axis=1)
+    crossed = swap(jnp.stack([grad_kv[1], grad_kv[3]]), "wsh", 1).astype(jnp.float32)
+    far = (grad_kv[2].astype(jnp.float32) + crossed[1]).astype(LOW)
+    grad_kv = (
+        grad_kv[0].astype(jnp.float32) + crossed[0] + swap(far, "ctx", 1).astype(jnp.float32)
+    )
+    grad_q = turn(dq_t.reshape(H, HD, rows), cosine, -sine).reshape(QD, rows)
+    grad_k = turn(grad_kv[:KV], cosine, -sine).reshape(KD, rows)
+    grad_v = grad_kv[KV:].reshape(KD, rows)
+    grad_mixed = jnp.concatenate([grad_q, grad_k, grad_v], axis=0).astype(LOW)
+    grad_normed = contract(grad_mixed, w_in[:, :QKV], 0, 1)
+    grad_in_norm, grad_gain_one = rms_backward(
+        grad_normed, hidden * inverse_one, inverse_one, gain_one
+    )
+    grad_hidden = (grad_middle + grad_in_norm).astype(LOW)
+    shares["out"] = spread(layer, arranged(grad_branch), o_t, 1)
+    gain_rows = jnp.zeros((SIDE, D), LOW)
+    gain_rows = gain_rows.at[0].set(grad_gain_one.astype(LOW)).at[1].set(grad_gain_two.astype(LOW))
+    shares["in"] = spread(layer, arranged(normed), grad_mixed, 1, arranged(gain_rows))
+    return grad_hidden, shares
+
+
+def on_device_pairs(
+    x_in, cotangent, w_qkv, w_out, w_gate_up, w_down, gains, order, visible, seq_ids
+):
+    section = lax.axis_index("section")
+    column = lax.axis_index("ctx")
+    place = lax.axis_index("wsh")
+    core = place % 2
+    side = place // 2
+    rows = x_in.shape[2]
+    quarter = D // 4
+    share = quarter // 4
+    slot = column % 2 + 2 * core
+    first_section = section == 0
+
+    def partner(index):
+        z, w = index // 4, index % 4
+        if (z < 2) == (w % 2 == 1):
+            return ((z + 2) % 4) * 4 + (w ^ 1)
+        return index
+
+    moves = [(i, partner(i)) for i in range(16)]
+
+    def moved(value):
+        return lax.ppermute(value, ("ctx", "wsh"), moves)
+
+    ids = jnp.arange(D, dtype=jnp.int32)
+    natural = one_hot((place ^ (ids // quarter)) * quarter + ids % quarter, D)
+    given, block, shard = ids // (D // 2), (ids % quarter) // share, ids % share
+    to_core = jnp.where(given == 0, 1 - core, core)
+    to_side = jnp.where((ids % (D // 2)) // quarter == 0, 1 - side, side)
+    to_place = place ^ column ^ block
+    arrange = one_hot(to_place * quarter + (2 * to_side + to_core) * share + shard, D)
+
+    seq_both = jnp.stack([seq_ids[:, 0], swap(seq_ids[:, 0], "wsh", 1)])
+    seq_row = jnp.where(core == column // 2, seq_both[0, section], seq_both[1, section])
+    info, angles = pair_tables(order, visible, seq_row, section, slot, rows)
+
+    gain_columns = jnp.concatenate(
+        [gains[0].T, jnp.zeros((quarter, SIDE - gains.shape[1]), LOW)], axis=1
+    )
+    shards = [
+        jnp.concatenate([w_qkv[0], gain_columns], axis=1),
+        w_out[0].T,
+        w_gate_up[0][:, :FF],
+        w_gate_up[0][:, FF:],
+        w_down[0].T,
+    ]
+    hidden = contract(moved(x_in[section, 0]), natural, 1, 1)
+    weights = gather_both(shards, section, column % 2)
+    result_one, saved_one = pair_forward(hidden, weights[0], info, angles)
+    result_two, saved_two = pair_forward(
+        result_one.astype(jnp.float32), weights[1], info, angles
+    )
+
+    def placed(own_one, own_two):
+        mine = jnp.where(first_section, own_one, own_two)
+        other = swap(jnp.where(first_section, own_two, own_one), "section", 1)
+        both = jnp.concatenate(
+            [jnp.where(first_section, mine, other), jnp.where(first_section, other, mine)], axis=0
+        )
+        both = contract(both, natural, 1, 0).astype(LOW)
+        return moved(both).reshape(2, rows, D)
+
+    activations = placed(result_one, result_two)
+    grad_low = contract(moved(cotangent[section, 0]), natural, 1, 1).astype(LOW)
+    grad_two, shares_two = pair_backward(
+        1, grad_low, weights[1], saved_two, info, angles, arrange
+    )
+    grad_one, shares_one = pair_backward(
+        0, grad_two, weights[0], saved_one, info, angles, arrange
+    )
+    input_grads = placed(grad_one, grad_two).astype(jnp.float32)
+
+    def total(name):
+        one, two = shares_one[name], shares_two[name]
+        return jnp.where(
+            first_section,
+            one[0].astype(jnp.float32) + one[1].astype(jnp.float32),
+            two[0].astype(jnp.float32) + two[1].astype(jnp.float32),
+        )
+
+    term_in = total("in")
+    return (
+        activations[None, :, None],
+        input_grads[None, :, None],
+        term_in[None, :, :QKV],
+        total("out").T[None],
+        jnp.concatenate([total("gate"), total("up")], axis=1)[None],
+        total("down").T[None],
+        term_in[:, QKV : QKV + 2].T[None],
+    )
+
+
 def solution(mesh):
     in_specs = (
         P(None, "wsh", "ctx", None),
@@ -440,6 +932,7 @@
         P("section", None, ("ctx", "wsh")),
         P("section", None, ("ctx", "wsh")),
     )
+    body = on_device_pairs if fits_pairs(mesh) else on_device_general
     return jax.shard_map(
-        on_device, mesh=mesh, in_specs=in_specs, out_specs=out_specs, check_vma=False
-    )
+        body, mesh=mesh, in_specs=in_specs, out_specs=out_specs, check_vma=False
+    )

time: 2620 us -> 1290 us (0.49)
  matrix products: 1320 us -> 250 us
  other arithmetic: 408 us -> 95.4 us
  starting transfers between devices: 11.4 us -> 259 us
  local copies, waits for them, and re-layouts: 202 us -> 62.8 us
  Pallas kernels: 0 us -> 61.1 us
  blocking collectives: 42.3 us -> 0 us
  waiting for transfers between devices: 580 us -> 548 us
    dot_general x153 -> x56, matrix products: 1320 us -> 250 us  [contract(): lax.dot_general(left, right, (((left_dim,), (right_dim,)), ((), ())), pre...]
    ppermute x4 -> x112, waiting for transfers between devices: 64.1 us -> 548 us  [the longest x98 518 us: swap(): lax.ppermute(value, axis, [(i, i ^ bit) for i in range(lax.axis_size(axis...]
    reduce_scatter x8 -> x0, waiting for transfers between devices: 381 us -> none  [the longest x1 274 us: on_device(): lax.psum_scatter(term_gate_up, ('ctx', 'wsh'), scatter_dimension=0, tiled...]
    reduce_sum x29 -> x2, other arithmetic: 269 us -> 0.83 us  [the longest x1 0.71 us: pair_tables(): jnp.sum(alive, keepdims=True)]
    ppermute x4 -> x112, starting transfers between devices: 9.38 us -> 259 us  [the longest x98 208 us: swap(): lax.ppermute(value, axis, [(i, i ^ bit) for i in range(lax.axis_size(axis...]
    all_gather x16 -> x0, waiting for transfers between devices: 133 us -> none  [the longest x6 64.1 us: layer_forward(): lax.all_gather(key_own, 'ctx', axis=0, tiled=True)]
    pallas_call x0 -> x4, Pallas kernels: none -> 61.1 us  [the longest x2 33.9 us: pair_attention_backward(): pl.pallas_call(backward_kernel, grid_spec=pltpu.PrefetchScalarGridSpec(nu...]
    slice x38 -> x29, local copies, waits for them, and re-layouts: 49.3 us -> 11.1 us  [the longest x10 7.36 us: spread(): got = swap(kept[:quarter], 'wsh', 2).astype(jnp.float32)]
  transfers between devices with their start and end apart: 30 -> 112, of which waited for: 13 -> 35; matrix products, arithmetic and copies ran while one was open for 49% -> 24% of each run, Pallas kernels for 0% -> 4%
where the time goes in v1:
time: 1290 us; the launch traced here: 1300 us
  waiting for transfers between devices  548 us (42%)
  starting transfers between devices  259 us (20%)
  matrix products  250 us (19%)
  other arithmetic  95.4 us (7%)
  local copies, waits for them, and re-layouts  62.8 us (5%)
  Pallas kernels  61.1 us (5%)
  between operations  21.2 us (2%)
    ppermute x98, waiting for transfers between devices, swap(): lax.ppermute(value, axis, [(i, i ^ bit) for i in range(lax.axis_size(axis...  518 us
    dot_general x56, matrix products, contract(): lax.dot_general(left, right, (((left_dim,), (right_dim,)), ((), ())), pre...  250 us
    ppermute x98, starting transfers between devices, swap(): lax.ppermute(value, axis, [(i, i ^ bit) for i in range(lax.axis_size(axis...  208 us
    pallas_call x2, Pallas kernels, pair_attention_backward(): pl.pallas_call(backward_kernel, grid_spec=pltpu.PrefetchScalarGridSpec(nu...  33.9 us
    ppermute x4, starting transfers between devices, moved(): return lax.ppermute(value, ('ctx', 'wsh'), moves)  33.9 us
    unnamed x248, local copies, waits for them, and re-layouts  33 us
    ppermute x10, waiting for transfers between devices, spread(): return (own, lax.ppermute(own, 'section', [(1 - layer, layer)]))  29.5 us
    unnamed x26, other arithmetic  28.8 us
  transfers between devices with their start and end apart: 112, of which 35 were waited for; matrix products, arithmetic and copies ran while one was open for 24% of the time, Pallas kernels for 4%

profile of v1, /device:TPU:0, one launch (start us, length us, event | category | flops | bytes accessed | tf_op | source)
XLA Modules:
  0.0 1296.7 jit_solution(10808173047078099882)
XLA Ops:
  57.8 16.3 %collective-permute-start.16 = (bf16[288,1152]{1,0:T(8,128)(2,1)}, bf16[288,1152]{1,0:T(8,128)(2,1)S(1)}, u32[]{:S(2)}, u32[]{:S(2)}) collective-permute-start(bf16[288,1152]{1,0:T(8,128)(2,1)} %collective-permute-done.15), channel_id=1, source_target_pairs={{0,1},{1,0},{2,3},{3,2},{4,5},{5,4},{6,7},{7,6},{8,9},{9,8},{10,11... | collective-permute-start | bytes 1990664 | tf_op jit(solution)/shard_map/ppermute | solution.py:445
  98.7 46.7 %collective-permute-done.7 = bf16[288,2048]{1,0:T(8,128)(2,1)S(1)} collective-permute-done((bf16[288,2048]{1,0:T(8,128)(2,1)}, bf16[288,2048]{1,0:T(8,128)(2,1)S(1)}, u32[]{:S(2)}, u32[]{:S(2)}) %collective-permute-start.7) | collective-permute-done | bytes 1179680 | tf_op jit(solution)/shard_map/ppermute | solution.py:445
  155.0 28.3 %collective-permute-done.20 = bf16[288,3072]{1,0:T(8,128)(2,1)S(1)} collective-permute-done((bf16[288,3072]{1,0:T(8,128)(2,1)S(1)}, bf16[288,3072]{1,0:T(8,128)(2,1)S(1)}, u32[]{:S(2)}, u32[]{:S(2)}) %collective-permute-start.20) | collective-permute-done | bytes 1769504 | tf_op jit(solution)/shard_map/ppermute | solution.py:445
  213.6 17.3 %collective-permute-done.34 = bf16[288,3072]{1,0:T(8,128)(2,1)S(1)} collective-permute-done((bf16[288,3072]{1,0:T(8,128)(2,1)S(1)}, bf16[288,3072]{1,0:T(8,128)(2,1)S(1)}, u32[]{:S(2)}, u32[]{:S(2)}) %collective-permute-start.34) | collective-permute-done | bytes 1769504 | tf_op jit(solution)/shard_map/ppermute | solution.py:445
  255.5 13.7 %shard_map.153 = (bf16[1152,512]{1,0:T(8,128)(2,1)S(1)}, f32[6,3,512]{2,1,0:T(4,128)S(1)}) custom-call(s32[5]{0:T(128)S(1)} %pad_add_fusion.live_ref, bf16[1152,512]{1,0:T(8,128)(2,1)S(1)} %bitcast.216, bf16[4,12,64,512]{3,2,1,0:T(8,128)(2,1)} %pad_maximum_fusion.1.k_ref.v_ref, bf16[4,12,64,512]{3,2,1,0:T(8,128)(2,1)} %pad_maximum_fusion.1.k_ref.v_ref, ...), custom_call_target="tpu_custom_call" | custom-call | flops 19327352832 | bytes 12582912 | tf_op jit(solution)/shard_map/pallas_call | solution.py:554
  298.0 32.2 %collective-permute-done.23 = bf16[2,144,3072]{2,1,0:T(8,128)(2,1)S(1)} collective-permute-done((bf16[2,144,3072]{2,1,0:T(8,128)(2,1)S(1)}, bf16[2,144,3072]{2,1,0:T(8,128)(2,1)S(1)}, u32[]{:S(2)}, u32[]{:S(2)}) %collective-permute-start.23) | collective-permute-done | bytes 1769504 | tf_op jit(solution)/shard_map/ppermute | solution.py:445
  433.0 13.5 %shard_map.154 = (bf16[1152,512]{1,0:T(8,128)(2,1)S(1)}, f32[6,3,512]{2,1,0:T(4,128)S(1)}) custom-call(s32[5]{0:T(128)S(1)} %pad_add_fusion.live_ref, bf16[1152,512]{1,0:T(8,128)(2,1)S(1)} %bitcast.218, bf16[4,12,64,512]{3,2,1,0:T(8,128)(2,1)} %pad_maximum_fusion.2.k_ref.v_ref, bf16[4,12,64,512]{3,2,1,0:T(8,128)(2,1)} %pad_maximum_fusion.2.k_ref.v_ref, ...), custom_call_target="tpu_custom_call" | custom-call | flops 19327352832 | bytes 12582912 | tf_op jit(solution)/shard_map/pallas_call | solution.py:554
  529.7 16.7 %shard_map.155 = (f32[1152,512]{1,0:T(8,128)}, bf16[4,6,64,512]{3,2,1,0:T(8,128)(2,1)S(1)}, bf16[4,6,64,512]{3,2,1,0:T(8,128)(2,1)}) custom-call(s32[5]{0:T(128)S(1)} %pad_add_fusion.live_ref, bf16[1152,512]{1,0:T(8,128)(2,1)S(1)} %bitcast.219, bf16[1152,512]{1,0:T(8,128)(2,1)S(1)} %convolution_convert_fusion.15.do_ref, ...), custom_call_target="tpu_custom_call" | custom-call | flops 48318382080 | bytes 12582912 | tf_op jit(solution)/shard_map/pallas_call | solution.py:588
  569.6 40.2 %collective-permute-start.47 = (bf16[12,64,512]{2,1,0:T(8,128)(2,1)S(1)}, bf16[12,64,512]{2,1,0:T(8,128)(2,1)S(1)}, u32[]{:S(2)}, u32[]{:S(2)}) collective-permute-start(bf16[12,64,512]{2,1,0:T(8,128)(2,1)S(1)} %fusion.129), channel_id=1, source_target_pairs={{0,4},{4,0},{8,12},{12,8},{1,5},{5,1},{9,13},{13,9},{2,6},{6,2},{1... | collective-permute-start | bytes 2359304 | tf_op jit(solution)/shard_map/ppermute | solution.py:445
  610.1 15.2 %collective-permute-start.74 = (bf16[72,1152]{1,0:T(8,128)(2,1)S(1)}, bf16[72,1152]{1,0:T(8,128)(2,1)S(1)}, u32[]{:S(2)}, u32[]{:S(2)}) collective-permute-start(bf16[72,1152]{1,0:T(8,128)(2,1)S(1)} %get-tuple-element.209), channel_id=1, source_target_pairs={{0,12},{4,8},{8,4},{12,0},{1,13},{5,9},{9,5},{13,1},{2,14},{6,10},... | collective-permute-start | bytes 497672 | tf_op jit(solution)/shard_map/ppermute | solution.py:445
  639.0 19.3 %collective-permute-start.44 = (bf16[1024,1152]{1,0:T(8,128)(2,1)}, bf16[1024,1152]{1,0:T(8,128)(2,1)}, u32[]{:S(2)}, u32[]{:S(2)}) collective-permute-start(bf16[1024,1152]{1,0:T(8,128)(2,1)} %fusion.40), channel_id=1, source_target_pairs={{0,0},{1,8},{2,2},{3,10},{4,4},{5,12},{6,6},{7,14},{8,1},{9,9},{10... | collective-permute-start | bytes 7077896 | tf_op jit(solution)/shard_map/ppermute | solution.py:843
  704.1 17.2 %shard_map.156 = (f32[1152,512]{1,0:T(8,128)}, bf16[4,6,64,512]{3,2,1,0:T(8,128)(2,1)S(1)}, bf16[4,6,64,512]{3,2,1,0:T(8,128)(2,1)}) custom-call(s32[5]{0:T(128)S(1)} %pad_add_fusion.live_ref, bf16[1152,512]{1,0:T(8,128)(2,1)S(1)} %bitcast.217, bf16[1152,512]{1,0:T(8,128)(2,1)S(1)} %convolution_convert_fusion.14.do_ref, bf16[1152,512]{1,0:T(8,128)(2,1)S(1)} %copy-done.5, ...), custom_call_target="tpu_custom_call" | custom-call | flops 48318382080 | bytes 12582912 | tf_op jit(solution)/shard_map/pallas_call | solution.py:588
  769.1 27.5 %collective-permute-start.68 = (bf16[72,1152]{1,0:T(8,128)(2,1)S(1)}, bf16[72,1152]{1,0:T(8,128)(2,1)S(1)}, u32[]{:S(2)}, u32[]{:S(2)}) collective-permute-start(bf16[72,1152]{1,0:T(8,128)(2,1)S(1)} %get-tuple-element.206), channel_id=1, source_target_pairs={{0,12},{4,8},{8,4},{12,0},{1,13},{5,9},{9,5},{13,1},{2,14},{6,10},... | collective-permute-start | bytes 497672 | tf_op jit(solution)/shard_map/ppermute | solution.py:445
  822.4 14.0 %collective-permute-done.49 = bf16[12,64,512]{2,1,0:T(8,128)(2,1)S(1)} collective-permute-done((bf16[12,64,512]{2,1,0:T(8,128)(2,1)S(1)}, bf16[12,64,512]{2,1,0:T(8,128)(2,1)S(1)}, u32[]{:S(2)}, u32[]{:S(2)}) %collective-permute-start.49) | collective-permute-done | bytes 786464 | tf_op jit(solution)/shard_map/ppermute | solution.py:445
  859.4 28.2 %collective-permute-done.83 = bf16[288,3072]{1,0:T(8,128)(2,1)} collective-permute-done((bf16[288,3072]{1,0:T(8,128)(2,1)}, bf16[288,3072]{1,0:T(8,128)(2,1)}, u32[]{:S(2)}, u32[]{:S(2)}) %collective-permute-start.83) | collective-permute-done | bytes 1769504 | tf_op jit(solution)/shard_map/ppermute | solution.py:445
  891.5 33.6 %collective-permute-done.107 = bf16[288,3072]{1,0:T(8,128)(2,1)} collective-permute-done((bf16[288,3072]{1,0:T(8,128)(2,1)}, bf16[288,3072]{1,0:T(8,128)(2,1)}, u32[]{:S(2)}, u32[]{:S(2)}) %collective-permute-start.107) | collective-permute-done | bytes 1769504 | tf_op jit(solution)/shard_map/ppermute | solution.py:445
  943.8 33.1 %collective-permute-done.85 = bf16[72,3072]{1,0:T(8,128)(2,1)S(1)} collective-permute-done((bf16[72,3072]{1,0:T(8,128)(2,1)S(1)}, bf16[72,3072]{1,0:T(8,128)(2,1)S(1)}, u32[]{:S(2)}, u32[]{:S(2)}) %collective-permute-start.85) | collective-permute-done | bytes 442400 | tf_op jit(solution)/shard_map/ppermute | solution.py:445
  979.2 24.8 %collective-permute-done.109 = bf16[72,3072]{1,0:T(8,128)(2,1)S(1)} collective-permute-done((bf16[72,3072]{1,0:T(8,128)(2,1)S(1)}, bf16[72,3072]{1,0:T(8,128)(2,1)S(1)}, u32[]{:S(2)}, u32[]{:S(2)}) %collective-permute-start.109) | collective-permute-done | bytes 442400 | tf_op jit(solution)/shard_map/ppermute | solution.py:445
  1055.4 27.0 %collective-permute-done.89 = bf16[288,3072]{1,0:T(8,128)(2,1)} collective-permute-done((bf16[288,3072]{1,0:T(8,128)(2,1)S(1)}, bf16[288,3072]{1,0:T(8,128)(2,1)}, u32[]{:S(2)}, u32[]{:S(2)}) %collective-permute-start.89) | collective-permute-done | bytes 1769504 | tf_op jit(solution)/shard_map/ppermute | solution.py:445
  1086.8 33.5 %collective-permute-done.77 = bf16[288,3072]{1,0:T(8,128)(2,1)} collective-permute-done((bf16[288,3072]{1,0:T(8,128)(2,1)S(1)}, bf16[288,3072]{1,0:T(8,128)(2,1)}, u32[]{:S(2)}, u32[]{:S(2)}) %collective-permute-start.77) | collective-permute-done | bytes 1769504 | tf_op jit(solution)/shard_map/ppermute | solution.py:445
  1123.8 34.3 %collective-permute-done.101 = bf16[288,3072]{1,0:T(8,128)(2,1)S(1)} collective-permute-done((bf16[288,3072]{1,0:T(8,128)(2,1)}, bf16[288,3072]{1,0:T(8,128)(2,1)S(1)}, u32[]{:S(2)}, u32[]{:S(2)}) %collective-permute-start.101) | collective-permute-done | bytes 1769504 | tf_op jit(solution)/shard_map/ppermute | solution.py:445
  1162.5 15.6 %collective-permute-done.90 = bf16[72,3072]{1,0:T(8,128)(2,1)S(1)} collective-permute-done((bf16[72,3072]{1,0:T(8,128)(2,1)S(1)}, bf16[72,3072]{1,0:T(8,128)(2,1)S(1)}, u32[]{:S(2)}, u32[]{:S(2)}) %collective-permute-start.90) | collective-permute-done | bytes 442400 | tf_op jit(solution)/shard_map/ppermute | solution.py:445
  1183.4 32.8 %collective-permute-done.79 = bf16[72,3072]{1,0:T(8,128)(2,1)S(1)} collective-permute-done((bf16[72,3072]{1,0:T(8,128)(2,1)S(1)}, bf16[72,3072]{1,0:T(8,128)(2,1)S(1)}, u32[]{:S(2)}, u32[]{:S(2)}) %collective-permute-start.79) | collective-permute-done | bytes 442400 | tf_op jit(solution)/shard_map/ppermute | solution.py:445
  1220.4 15.9 %collective-permute-done.103 = bf16[72,3072]{1,0:T(8,128)(2,1)S(1)} collective-permute-done((bf16[72,3072]{1,0:T(8,128)(2,1)S(1)}, bf16[72,3072]{1,0:T(8,128)(2,1)S(1)}, u32[]{:S(2)}, u32[]{:S(2)}) %collective-permute-start.103) | collective-permute-done | bytes 442400 | tf_op jit(solution)/shard_map/ppermute | solution.py:445
  (691 shorter events, 678.8 us)
Async XLA Ops:
  4.9 81.0 %collective-permute-start.5 = (bf16[288,2048]{1,0:T(8,128)(2,1)}, bf16[288,2048]{1,0:T(8,128)(2,1)}, u32[]{:S(2)}, u32[]{:S(2)}) collective-permute-start(bf16[288,2048]{1,0:T(8,128)(2,1)} %concatenate.168), channel_id=1, source_target_pairs={{0,16},{16,0},{1,17},{17,1},{2,18},{18,2},{3,19},{19,3},{4,20},{20... | collective-permute-start | bytes 3538952 | tf_op jit(solution)/shard_map/ppermute | solution.py:445
  7.8 69.5 %collective-permute-start.3 = (bf16[288,2048]{1,0:T(8,128)(2,1)}, bf16[288,2048]{1,0:T(8,128)(2,1)}, u32[]{:S(2)}, u32[]{:S(2)}) collective-permute-start(bf16[288,2048]{1,0:T(8,128)(2,1)} %concatenate.168), channel_id=1, source_target_pairs={{0,2},{1,3},{2,0},{3,1},{4,6},{5,7},{6,4},{7,5},{8,10},{9,11},{10,... | collective-permute-start | bytes 3538952 | tf_op jit(solution)/shard_map/ppermute | solution.py:445
  56.5 97.8 %collective-permute-start.26 = (bf16[288,3072]{1,0:T(8,128)(2,1)S(1)}, bf16[288,3072]{1,0:T(8,128)(2,1)S(1)}, u32[]{:S(2)}, u32[]{:S(2)}) collective-permute-start(bf16[288,3072]{1,0:T(8,128)(2,1)S(1)} %get-tuple-element.72), channel_id=1, source_target_pairs={{0,1},{1,0},{2,3},{3,2},{4,5},{5,4},{6,7},{7,6},{8,9},{9,8},{10,11... | collective-permute-start | bytes 5308424 | tf_op jit(solution)/shard_map/ppermute | solution.py:445
  82.2 70.6 %collective-permute-start.27 = (bf16[288,3072]{1,0:T(8,128)(2,1)S(1)}, bf16[288,3072]{1,0:T(8,128)(2,1)S(1)}, u32[]{:S(2)}, u32[]{:S(2)}) collective-permute-start(bf16[288,3072]{1,0:T(8,128)(2,1)S(1)} %get-tuple-element.72), channel_id=1, source_target_pairs={{0,2},{1,3},{2,0},{3,1},{4,6},{5,7},{6,4},{7,5},{8,10},{9,11},{10,... | collective-permute-start | bytes 5308424 | tf_op jit(solution)/shard_map/ppermute | solution.py:445
  96.7 86.6 %collective-permute-start.20 = (bf16[288,3072]{1,0:T(8,128)(2,1)S(1)}, bf16[288,3072]{1,0:T(8,128)(2,1)S(1)}, u32[]{:S(2)}, u32[]{:S(2)}) collective-permute-start(bf16[288,3072]{1,0:T(8,128)(2,1)S(1)} %get-tuple-element.71), channel_id=1, source_target_pairs={{0,2},{1,3},{2,0},{3,1},{4,6},{5,7},{6,4},{7,5},{8,10},{9,11},{10,... | collective-permute-start | bytes 5308424 | tf_op jit(solution)/shard_map/ppermute | solution.py:445
  98.5 92.9 %collective-permute-start.2 = (bf16[288,2048]{1,0:T(8,128)(2,1)}, bf16[288,2048]{1,0:T(8,128)(2,1)S(1)}, u32[]{:S(2)}, u32[]{:S(2)}) collective-permute-start(bf16[288,2048]{1,0:T(8,128)(2,1)} %concatenate.168), channel_id=1, source_target_pairs={{0,1},{1,0},{2,3},{3,2},{4,5},{5,4},{6,7},{7,6},{8,9},{9,8},{10,11... | collective-permute-start | bytes 3538952 | tf_op jit(solution)/shard_map/ppermute | solution.py:445
  253.3 82.8 %collective-permute-start.31 = (bf16[2,144,3072]{2,1,0:T(8,128)(2,1)S(1)}, bf16[2,144,3072]{2,1,0:T(8,128)(2,1)}, u32[]{:S(2)}, u32[]{:S(2)}) collective-permute-start(bf16[2,144,3072]{2,1,0:T(8,128)(2,1)S(1)} %collective-permute-done.29), channel_id=1, source_target_pairs={{0,1},{1,0},{2,3},{3,2},{4,5},{5,4},{6,7},{7,6},{8,9},{9,8},{10,11... | collective-permute-start | bytes 5308424 | tf_op jit(solution)/shard_map/ppermute | solution.py:445
  494.9 72.5 %collective-permute-start.43 = (bf16[512,1152]{1,0:T(8,128)(2,1)}, bf16[512,1152]{1,0:T(8,128)(2,1)}, u32[]{:S(2)}, u32[]{:S(2)}) collective-permute-start(bf16[512,1152]{1,0:T(8,128)(2,1)} %get-tuple-element.242), channel_id=1, source_target_pairs={{0,16},{16,0},{1,17},{17,1},{2,18},{18,2},{3,19},{19,3},{4,20},{20... | collective-permute-start | bytes 3538952 | tf_op jit(solution)/shard_map/ppermute | solution.py:445
  554.7 196.8 %collective-permute-start.94 = (bf16[576,3072]{1,0:T(8,128)(2,1)}, bf16[576,3072]{1,0:T(8,128)(2,1)}, u32[]{:S(2)}, u32[]{:S(2)}) collective-permute-start(bf16[576,3072]{1,0:T(8,128)(2,1)} %convolution_convert_fusion.2), channel_id=1, source_target_pairs={{0,1},{1,0},{2,3},{3,2},{4,5},{5,4},{6,7},{7,6},{8,9},{9,8},{10,11... | collective-permute-start | bytes 10616840 | tf_op jit(solution)/shard_map/ppermute | solution.py:445
  569.6 89.4 %collective-permute-start.47 = (bf16[12,64,512]{2,1,0:T(8,128)(2,1)S(1)}, bf16[12,64,512]{2,1,0:T(8,128)(2,1)S(1)}, u32[]{:S(2)}, u32[]{:S(2)}) collective-permute-start(bf16[12,64,512]{2,1,0:T(8,128)(2,1)S(1)} %fusion.129), channel_id=1, source_target_pairs={{0,4},{4,0},{8,12},{12,8},{1,5},{5,1},{9,13},{13,9},{2,6},{6,2},{1... | collective-permute-start | bytes 2359304 | tf_op jit(solution)/shard_map/ppermute | solution.py:445
  633.8 123.4 %collective-permute-start.82 = (bf16[576,3072]{1,0:T(8,128)(2,1)}, bf16[576,3072]{1,0:T(8,128)(2,1)}, u32[]{:S(2)}, u32[]{:S(2)}) collective-permute-start(bf16[576,3072]{1,0:T(8,128)(2,1)} %convolution_convert_fusion.4), channel_id=1, source_target_pairs={{0,1},{1,0},{2,3},{3,2},{4,5},{5,4},{6,7},{7,6},{8,9},{9,8},{10,11... | collective-permute-start | bytes 10616840 | tf_op jit(solution)/shard_map/ppermute | solution.py:445
  639.0 157.6 %collective-permute-start.106 = (bf16[576,3072]{1,0:T(8,128)(2,1)}, bf16[576,3072]{1,0:T(8,128)(2,1)}, u32[]{:S(2)}, u32[]{:S(2)}) collective-permute-start(bf16[576,3072]{1,0:T(8,128)(2,1)} %convolution_convert_fusion), channel_id=1, source_target_pairs={{0,1},{1,0},{2,3},{3,2},{4,5},{5,4},{6,7},{7,6},{8,9},{9,8},{10,11... | collective-permute-start | bytes 10616840 | tf_op jit(solution)/shard_map/ppermute | solution.py:445
  639.0 157.6 %collective-permute-start.44 = (bf16[1024,1152]{1,0:T(8,128)(2,1)}, bf16[1024,1152]{1,0:T(8,128)(2,1)}, u32[]{:S(2)}, u32[]{:S(2)}) collective-permute-start(bf16[1024,1152]{1,0:T(8,128)(2,1)} %fusion.40), channel_id=1, source_target_pairs={{0,0},{1,8},{2,2},{3,10},{4,4},{5,12},{6,6},{7,14},{8,1},{9,9},{10... | collective-permute-start | bytes 7077896 | tf_op jit(solution)/shard_map/ppermute | solution.py:843
  807.8 208.1 %collective-permute-start.88 = (bf16[576,3072]{1,0:T(8,128)(2,1)}, bf16[576,3072]{1,0:T(8,128)(2,1)}, u32[]{:S(2)}, u32[]{:S(2)}) collective-permute-start(bf16[576,3072]{1,0:T(8,128)(2,1)} %convolution_convert_fusion.3), channel_id=1, source_target_pairs={{0,1},{1,0},{2,3},{3,2},{4,5},{5,4},{6,7},{7,6},{8,9},{9,8},{10,11... | collective-permute-start | bytes 10616840 | tf_op jit(solution)/shard_map/ppermute | solution.py:445
  810.9 76.7 %collective-permute-start.83 = (bf16[288,3072]{1,0:T(8,128)(2,1)}, bf16[288,3072]{1,0:T(8,128)(2,1)}, u32[]{:S(2)}, u32[]{:S(2)}) collective-permute-start(bf16[288,3072]{1,0:T(8,128)(2,1)} %slice.886), channel_id=1, source_target_pairs={{0,2},{1,3},{2,0},{3,1},{4,6},{5,7},{6,4},{7,5},{8,10},{9,11},{10,... | collective-permute-start | bytes 5308424 | tf_op jit(solution)/shard_map/ppermute | solution.py:445
  819.8 105.2 %collective-permute-start.107 = (bf16[288,3072]{1,0:T(8,128)(2,1)}, bf16[288,3072]{1,0:T(8,128)(2,1)}, u32[]{:S(2)}, u32[]{:S(2)}) collective-permute-start(bf16[288,3072]{1,0:T(8,128)(2,1)} %slice.914), channel_id=1, source_target_pairs={{0,2},{1,3},{2,0},{3,1},{4,6},{5,7},{6,4},{7,5},{8,10},{9,11},{10,... | collective-permute-start | bytes 5308424 | tf_op jit(solution)/shard_map/ppermute | solution.py:445
  855.6 75.4 %collective-permute-start.98 = (bf16[72,3072]{1,0:T(8,128)(2,1)S(1)}, bf16[72,3072]{1,0:T(8,128)(2,1)S(1)}, u32[]{:S(2)}, u32[]{:S(2)}) collective-permute-start(bf16[72,3072]{1,0:T(8,128)(2,1)S(1)} %get-tuple-element.189), channel_id=1, source_target_pairs={{0,12},{4,8},{8,4},{12,0},{1,13},{5,9},{9,5},{13,1},{2,14},{6,10},... | collective-permute-start | bytes 1327112 | tf_op jit(solution)/shard_map/ppermute | solution.py:445
  859.4 71.8 %collective-permute-start.97 = (bf16[72,3072]{1,0:T(8,128)(2,1)S(1)}, bf16[72,3072]{1,0:T(8,128)(2,1)S(1)}, u32[]{:S(2)}, u32[]{:S(2)}) collective-permute-start(bf16[72,3072]{1,0:T(8,128)(2,1)S(1)} %get-tuple-element.190), channel_id=1, source_target_pairs={{0,8},{4,12},{8,0},{12,4},{1,9},{5,13},{9,1},{13,5},{2,10},{6,14},... | collective-permute-start | bytes 1327112 | tf_op jit(solution)/shard_map/ppermute | solution.py:445
  931.2 91.8 %collective-permute-start.76 = (bf16[576,3072]{1,0:T(8,128)(2,1)}, bf16[576,3072]{1,0:T(8,128)(2,1)}, u32[]{:S(2)}, u32[]{:S(2)}) collective-permute-start(bf16[576,3072]{1,0:T(8,128)(2,1)} %convolution_convert_fusion.5), channel_id=1, source_target_pairs={{0,1},{1,0},{2,3},{3,2},{4,5},{5,4},{6,7},{7,6},{8,9},{9,8},{10,11... | collective-permute-start | bytes 10616840 | tf_op jit(solution)/shard_map/ppermute | solution.py:445
  1048.6 71.7 %collective-permute-start.77 = (bf16[288,3072]{1,0:T(8,128)(2,1)S(1)}, bf16[288,3072]{1,0:T(8,128)(2,1)}, u32[]{:S(2)}, u32[]{:S(2)}) collective-permute-start(bf16[288,3072]{1,0:T(8,128)(2,1)S(1)} %slice.878), channel_id=1, source_target_pairs={{0,2},{1,3},{2,0},{3,1},{4,6},{5,7},{6,4},{7,5},{8,10},{9,11},{10,... | collective-permute-start | bytes 5308424 | tf_op jit(solution)/shard_map/ppermute | solution.py:445
  1049.3 108.8 %collective-permute-start.101 = (bf16[288,3072]{1,0:T(8,128)(2,1)}, bf16[288,3072]{1,0:T(8,128)(2,1)S(1)}, u32[]{:S(2)}, u32[]{:S(2)}) collective-permute-start(bf16[288,3072]{1,0:T(8,128)(2,1)} %slice.906), channel_id=1, source_target_pairs={{0,2},{1,3},{2,0},{3,1},{4,6},{5,7},{6,4},{7,5},{8,10},{9,11},{10,... | collective-permute-start | bytes 5308424 | tf_op jit(solution)/shard_map/ppermute | solution.py:445
  1050.7 188.6 %collective-permute-start.51 = (bf16[1024,1152]{1,0:T(8,128)(2,1)}, bf16[1024,1152]{1,0:T(8,128)(2,1)S(1)}, u32[]{:S(2)}, u32[]{:S(2)}) collective-permute-start(bf16[1024,1152]{1,0:T(8,128)(2,1)} %fusion.41), channel_id=1, source_target_pairs={{0,0},{1,8},{2,2},{3,10},{4,4},{5,12},{6,6},{7,14},{8,1},{9,9},{10... | collective-permute-start | bytes 7077896 | tf_op jit(solution)/shard_map/ppermute | solution.py:843
  1054.6 188.4 %collective-permute-start.53 = (bf16[288,2048]{1,0:T(8,128)(2,1)S(1)}, bf16[288,2048]{1,0:T(8,128)(2,1)S(1)}, u32[]{:S(2)}, u32[]{:S(2)}) collective-permute-start(bf16[288,2048]{1,0:T(8,128)(2,1)S(1)} %slice.843), channel_id=1, source_target_pairs={{0,2},{1,3},{2,0},{3,1},{4,6},{5,7},{6,4},{7,5},{8,10},{9,11},{10,... | collective-permute-start | bytes 3538952 | tf_op jit(solution)/shard_map/ppermute | solution.py:445
  1084.6 75.1 %collective-permute-start.92 = (bf16[72,3072]{1,0:T(8,128)(2,1)S(1)}, bf16[72,3072]{1,0:T(8,128)(2,1)S(1)}, u32[]{:S(2)}, u32[]{:S(2)}) collective-permute-start(bf16[72,3072]{1,0:T(8,128)(2,1)S(1)} %get-tuple-element.186), channel_id=1, source_target_pairs={{0,12},{4,8},{8,4},{12,0},{1,13},{5,9},{9,5},{13,1},{2,14},{6,10},... | collective-permute-start | bytes 1327112 | tf_op jit(solution)/shard_map/ppermute | solution.py:445
  (202 other events, 4680.5 us)

commit v2 on v1

--- a/solution.py
+++ b/solution.py
@@ -655,50 +655,252 @@
     return (live, key_seq, own_seq), (jnp.cos(angles), jnp.sin(angles))
 
 
-def gather_both(shards, section, half):
-    own_side, other_side = [], []
-    sent = []
-    for step, own in enumerate(shards):
-        if step >= 2:
-            own = after(own, sent[step - 2])
-        near = swap(own, "wsh", 2)
-        sent.append(near)
-        rows, width = own.shape
-        if step < 2:
-            other = swap(own, "section", 1)
-            if step == 0:
-                far = swap(after(other, near), "wsh", 2)
-            else:
-                far = swap(near, "section", 1)
-        else:
-            both = jnp.stack([own, near]).reshape(2, 2, rows // 2, width)
-            mine = lax.dynamic_index_in_dim(both, half, 1, keepdims=False)
-            crossed = swap(mine, "section", 1)
-            passed = swap(crossed, "ctx", 1)
-            crossed_two = swap(crossed, "wsh", 1)
-            passed_two = swap(passed, "wsh", 1)
-            first = half == 0
-
-            def joined(a, b):
-                return jnp.concatenate([jnp.where(first, a, b), jnp.where(first, b, a)], axis=0)
-
-            other, far = joined(crossed[0], passed[0]), joined(crossed[1], passed[1])
-            other_two = joined(crossed_two[0], passed_two[0])
-            far_two = joined(crossed_two[1], passed_two[1])
-        if step < 2:
-            other_two, far_two = swap(other, "wsh", 1), swap(far, "wsh", 1)
-        own_side.append(
-            jnp.concatenate([own, swap(own, "wsh", 1), near, swap(near, "wsh", 1)], axis=0)
-        )
-        other_side.append(jnp.concatenate([other, other_two, far, far_two], axis=0))
-    first_section = section == 0
-    return [
-        [
-            jnp.where(first_section, a, b) if layer == 0 else jnp.where(first_section, b, a)
-            for a, b in zip(own_side, other_side)
+MESH_ID = pl.DeviceIdType.MESH
+PIECE = 1024
+
+
+def stream_partner(column, place):
+    core = place % 2
+    moving = (column < 2) == (core == 1)
+    return moving, lax.rem(column + 2, 4), place + 1 - 2 * core
+
+
+def gather_kernel(*refs):
+    rows_refs, shard_refs = refs[:2], refs[2:6]
+    full_refs, moved_refs = refs[6:11], refs[11:13]
+    send_sem, recv_sem, local_sem = refs[13:16]
+    held_refs, held_rows = refs[16:20], refs[20:22]
+    section = lax.axis_index("section")
+    column = lax.axis_index("ctx")
+    place = lax.axis_index("wsh")
+    half = lax.rem(column, 2)
+    over_x = (section, column, lax.rem(place + 2, 4))
+    over_y = (1 - section, column, place)
+    over_z = (section, column + 1 - 2 * half, place)
+    over_core = (section, column, place + 1 - 2 * lax.rem(place, 2))
+    moving, partner_column, partner_place = stream_partner(column, place)
+    partner = (section, partner_column, partner_place)
+
+    barrier = pltpu.get_barrier_semaphore()
+    for target in (over_x, over_y, over_z, over_core):
+        pl.semaphore_signal(barrier, inc=1, device_id=target, device_id_type=MESH_ID)
+
+    @pl.when(moving)
+    def _():
+        pl.semaphore_signal(barrier, inc=1, device_id=partner, device_id_type=MESH_ID)
+        pl.semaphore_wait(barrier, 5)
+
+    @pl.when(jnp.logical_not(moving))
+    def _():
+        pl.semaphore_wait(barrier, 4)
+
+    in_ref, out_ref, gate_up_ref, down_ref = shard_refs
+    sources = [
+        (in_ref, 0, full_refs[0]),
+        (out_ref, 0, full_refs[1]),
+        (gate_up_ref, 0, full_refs[2]),
+        (gate_up_ref, FF, full_refs[3]),
+        (down_ref, 0, full_refs[4]),
+    ]
+    pieces = []
+    for shard_ref, offset, full_ref in sources:
+        width = full_ref.shape[3]
+        step = PIECE if width % PIECE == 0 else width
+        for first in range(0, width, step):
+            pieces.append((shard_ref, offset + first, full_ref, first, step))
+    count = len(pieces)
+    quarter = shard_refs[0].shape[0]
+    mid = quarter // 2
+
+    def own(k):
+        shard_ref, offset, full_ref, first, step = pieces[k]
+        return shard_ref.at[:, pl.ds(offset, step)]
+
+    def own_half(k):
+        shard_ref, offset, full_ref, first, step = pieces[k]
+        return shard_ref.at[pl.ds(half * mid, mid), pl.ds(offset, step)]
+
+    def full(k, layer, block):
+        shard_ref, offset, full_ref, first, step = pieces[k]
+        return full_ref.at[layer, block, :, pl.ds(first, step)]
+
+    def full_half(k, layer, block, which):
+        shard_ref, offset, full_ref, first, step = pieces[k]
+        return full_ref.at[layer, block, pl.ds(which * mid, mid), pl.ds(first, step)]
+
+    started = {}
+
+    def send(kind, k, source, target, device):
+        copy = pltpu.make_async_remote_copy(
+            src_ref=source,
+            dst_ref=target,
+            send_sem=send_sem.at[kind, k],
+            recv_sem=recv_sem.at[kind, k],
+            device_id=device,
+            device_id_type=MESH_ID,
+        )
+        copy.start()
+        started[kind, k] = copy
+
+    other = 1 - section
+
+    def start_near(k):
+        send(0, k, own(k), full(k, section, 2), over_x)
+
+    def start_cross(k):
+        send(1, k, own_half(k), full_half(k, section, 0, half), over_y)
+
+    def row_copies():
+        return [
+            pltpu.make_async_remote_copy(
+                src_ref=rows_refs[i].at[section, 0],
+                dst_ref=moved_refs[i],
+                send_sem=send_sem.at[11, i],
+                recv_sem=recv_sem.at[11, i],
+                device_id=partner,
+                device_id_type=MESH_ID,
+            )
+            for i in range(2)
         ]
-        for layer in range(2)
+
+    loads = [
+        pltpu.make_async_copy(shard_refs[i], held_refs[i], local_sem.at[count + i])
+        for i in range(4)
     ]
+    row_loads = [
+        pltpu.make_async_copy(
+            rows_refs[i].at[section, 0], held_rows[i], local_sem.at[count + 4 + i]
+        )
+        for i in range(2)
+    ]
+    row_stores = [
+        pltpu.make_async_copy(held_rows[i], moved_refs[i], local_sem.at[count + 4 + i])
+        for i in range(2)
+    ]
+    for copy in loads:
+        copy.start()
+
+    for k in range(2):
+        start_near(k)
+        start_cross(k)
+
+    @pl.when(moving)
+    def _():
+        for copy in row_copies():
+            copy.start()
+
+    @pl.when(jnp.logical_not(moving))
+    def _():
+        for copy in row_loads:
+            copy.start()
+        for copy, store in zip(row_loads, row_stores):
+            copy.wait()
+            store.start()
+
+    for copy in loads:
+        copy.wait()
+    stores = []
+    for k in range(count):
+        shard_ref, offset, full_ref, first, step = pieces[k]
+        held_ref = held_refs[[i for i in range(4) if shard_refs[i] is shard_ref][0]]
+        copy = pltpu.make_async_copy(
+            held_ref.at[:, pl.ds(offset, step)], full(k, section, 0), local_sem.at[k]
+        )
+        copy.start()
+        stores.append(copy)
+        send(5, k, own(k), full(k, section, 1), over_core)
+
+    for k in range(count + 2):
+        if k < count:
+            started[0, k].wait_recv()
+            send(
+                2,
+                k,
+                full_half(k, section, 2, half),
+                full_half(k, section, 2, half),
+                over_y,
+            )
+            send(6, k, full(k, section, 2), full(k, section, 3), over_core)
+            if k + 2 < count:
+                start_near(k + 2)
+            started[1, k].wait_recv()
+            send(
+                3, k, full_half(k, other, 0, half), full_half(k, other, 0, half), over_z
+            )
+            send(
+                7, k, full_half(k, other, 0, half), full_half(k, other, 1, half), over_core
+            )
+            if k + 2 < count:
+                start_cross(k + 2)
+        j = k - 1
+        if 0 <= j < count:
+            started[2, j].wait_recv()
+            send(
+                4, j, full_half(j, other, 2, half), full_half(j, other, 2, half), over_z
+            )
+            send(
+                8, j, full_half(j, other, 2, half), full_half(j, other, 3, half), over_core
+            )
+            started[3, j].wait_recv()
+            send(
+                9,
+                j,
+                full_half(j, other, 0, 1 - half),
+                full_half(j, other, 1, 1 - half),
+                over_core,
+            )
+        j = k - 2
+        if 0 <= j < count:
+            started[4, j].wait_recv()
+            send(
+                10,
+                j,
+                full_half(j, other, 2, 1 - half),
+                full_half(j, other, 3, 1 - half),
+                over_core,
+            )
+    for (kind, k), copy in started.items():
+        if kind >= 5:
+            copy.wait_recv()
+        copy.wait_send()
+    for copy in stores:
+        copy.wait()
+
+    @pl.when(moving)
+    def _():
+        for copy in row_copies():
+            copy.wait()
+
+    @pl.when(jnp.logical_not(moving))
+    def _():
+        for copy in row_stores:
+            copy.wait()
+
+
+def gather_all(rows_in, shards):
+    widths = [shards[0].shape[1], shards[1].shape[1], FF, FF, shards[3].shape[1]]
+    quarter = shards[0].shape[0]
+    batch_rows = rows_in[0].shape[2:]
+    anywhere = pl.BlockSpec(memory_space=pl.ANY)
+    count = sum(w // PIECE if w % PIECE == 0 else 1 for w in widths)
+    outs = pl.pallas_call(
+        gather_kernel,
+        out_shape=[jax.ShapeDtypeStruct((2, 4, quarter, w), LOW) for w in widths]
+        + [jax.ShapeDtypeStruct(batch_rows, LOW)] * 2,
+        in_specs=[anywhere] * 6,
+        out_specs=[anywhere] * 7,
+        scratch_shapes=[
+            pltpu.SemaphoreType.DMA((12, count)),
+            pltpu.SemaphoreType.DMA((12, count)),
+            pltpu.SemaphoreType.DMA((count + 6,)),
+        ]
+        + [pltpu.VMEM(shard.shape, LOW) for shard in shards]
+        + [pltpu.VMEM(batch_rows, LOW)] * 2,
+        compiler_params=pltpu.CompilerParams(collective_id=1, has_side_effects=True),
+    )(*rows_in, *shards)
+    full = outs[:5]
+    weights = [[w[layer].reshape(4 * quarter, -1) for w in full] for layer in range(2)]
+    return weights, outs[5], outs[6]
 
 
 def unpack(weights):
@@ -735,24 +937,331 @@
     return result, saved + (gate, up, units)
 
 
-def spread(layer, lhs_t, rhs, rhs_dim, extra=None):
-    half = lhs_t.shape[0] // 2
-    given = contract(lhs_t[:half], rhs, 1, rhs_dim)
-    kept = contract(lhs_t[half:], rhs, 1, rhs_dim)
-    if extra is not None:
-        given = jnp.concatenate([given, extra[:half]], axis=1)
-        kept = jnp.concatenate([kept, extra[half:]], axis=1)
-    width = given.shape[1]
-    kept = (kept + swap(given.astype(LOW), "wsh", 1).astype(jnp.float32)).astype(LOW)
+TILE = 384
+CROSSED = 22
+PLANE = 11
+
+
+def spread_kernel(
+    lhs_all,
+    rhs_all,
+    out_ref,
+    rhs_peer,
+    lhs_ref,
+    rhs_ref,
+    given_ref,
+    sum_ref,
+    side_ref,
+    block_ref,
+    last_given,
+    last_ref,
+    lhs_sem,
+    peer_send,
+    peer_recv,
+    load_sem,
+    given_send,
+    given_recv,
+    side_send,
+    side_recv,
+    block_send,
+    block_recv,
+    last_send,
+    last_recv,
+):
+    section = lax.axis_index("section")
+    column = lax.axis_index("ctx")
+    place = lax.axis_index("wsh")
+    other = 1 - section
+    over_x = (section, column, lax.rem(place + 2, 4))
+    over_y = (other, column, place)
+    over_core = (section, column, place + 1 - 2 * lax.rem(place, 2))
+    flip_low = column + 1 - 2 * lax.rem(column, 2)
+    flip_high = lax.rem(column + 2, 4)
+    flip_both = lax.rem(flip_low + 2, 4)
+    over_z = [(section, c, place) for c in (flip_low, flip_high, flip_both)]
+
+    barrier = pltpu.get_barrier_semaphore()
+    for target in (over_x, over_y, over_core, *over_z):
+        pl.semaphore_signal(barrier, inc=1, device_id=target, device_id_type=MESH_ID)
+    pl.semaphore_wait(barrier, 6)
+
+    half = lhs_all.shape[2] // 2
+    tokens = lhs_all.shape[3]
     quarter = half // 2
-    got = swap(kept[:quarter], "wsh", 2).astype(jnp.float32)
-    parts = (kept[quarter:].astype(jnp.float32) + got).reshape(4, quarter // 4, width)
-    sent = [swap(parts[k].astype(LOW), "ctx", k).astype(jnp.float32) for k in range(1, 4)]
-    own = (parts[0] + sent[0] + sent[1] + sent[2]).astype(LOW)
-    return own, lax.ppermute(own, "section", [(1 - layer, layer)])
-
-
-def pair_backward(layer, grad_low, weights, saved, info, angles, arrange):
+    share = quarter // 4
+    layers = (section, other)
+
+    def remote(source, target, send_sem, recv_sem, device):
+        return pltpu.make_async_remote_copy(
+            src_ref=source,
+            dst_ref=target,
+            send_sem=send_sem,
+            recv_sem=recv_sem,
+            device_id=device,
+            device_id_type=MESH_ID,
+        )
+
+    def lhs_copies():
+        copies = []
+        for which in range(2):
+            copies.append(
+                pltpu.make_async_copy(
+                    lhs_all.at[layers[which], :, pl.ds(half, half), :],
+                    lhs_ref.at[which, :, :, pl.ds(0, tokens)],
+                    lhs_sem.at[which],
+                )
+            )
+            copies.append(
+                remote(
+                    lhs_all.at[layers[which], :, pl.ds(0, half), :],
+                    lhs_ref.at[which, :, :, pl.ds(tokens, tokens)],
+                    lhs_sem.at[2 + which],
+                    lhs_sem.at[4 + which],
+                    over_core,
+                )
+            )
+        return copies
+
+    def peer_copy(which, tile):
+        return remote(
+            rhs_all.at[layers[which], tile],
+            rhs_peer.at[layers[which], tile],
+            peer_send.at[which, tile],
+            peer_recv.at[which, tile],
+            over_core,
+        )
+
+    def peer_starts(i):
+        for tile in (2 * i, 2 * i + 1, CROSSED + i):
+            for which in range(2):
+                peer_copy(1 - which, tile).start()
+
+    def loads(slot, which, tile):
+        return (
+            pltpu.make_async_copy(
+                rhs_all.at[layers[which], tile],
+                rhs_ref.at[slot, pl.ds(0, tokens)],
+                load_sem.at[slot, 0],
+            ),
+            pltpu.make_async_copy(
+                rhs_peer.at[layers[which], tile],
+                rhs_ref.at[slot, pl.ds(tokens, tokens)],
+                load_sem.at[slot, 1],
+            ),
+        )
+
+    def load_start(slot, which, tile):
+        own, peer = loads(slot, which, tile)
+        own.start()
+        peer_copy(which, tile).wait_recv()
+        peer.start()
+
+    def product(slot, which, tile, kind):
+        for copy in loads(slot, which, tile):
+            copy.wait()
+        return jnp.dot(
+            lhs_ref[which, kind], rhs_ref[slot], preferred_element_type=jnp.float32
+        )
+
+    def crossed_kind(tile):
+        return jnp.where(tile < 16, 0, jnp.where(tile < 21, 1, 2))
+
+    def plane_kind(i):
+        return jnp.where(i < 8, 3, 4)
+
+    def given_copy(tile):
+        slot = lax.rem(tile, 4)
+        return remote(
+            given_ref.at[slot],
+            sum_ref.at[tile],
+            given_send.at[slot],
+            given_recv.at[tile],
+            over_y,
+        )
+
+    def side_copy(unit):
+        return remote(
+            sum_ref.at[unit, pl.ds(0, quarter)],
+            side_ref.at[unit // 2, pl.ds(lax.rem(unit, 2) * quarter, quarter)],
+            side_send.at[unit],
+            side_recv.at[unit],
+            over_x,
+        )
+
+    def block_copy(pair, k):
+        return remote(
+            side_ref.at[pair, pl.ds((k + 1) * 2 * share, 2 * share)],
+            block_ref.at[pair, k],
+            block_send.at[pair, k],
+            block_recv.at[pair, k],
+            over_z[k],
+        )
+
+    def last_copy(i):
+        return remote(
+            last_given.at[i], last_ref.at[i], last_send.at[i], last_recv.at[i], over_y
+        )
+
+    def combine(pair):
+        parts = []
+        for e in range(2):
+            unit = 2 * pair + e
+            side_copy(unit).wait_recv()
+            kept = sum_ref[unit, pl.ds(quarter, quarter)].astype(jnp.float32)
+            got = side_ref[pair, pl.ds(e * quarter, quarter)].astype(jnp.float32)
+            parts.append((kept + got).reshape(4, share, TILE))
+        both = jnp.concatenate(parts, axis=1).reshape(8 * share, TILE)
+        side_ref[pair] = both.astype(LOW)
+        for k in range(3):
+            block_copy(pair, k).start()
+
+    def settle(pair):
+        total = side_ref[pair, pl.ds(0, 2 * share)].astype(jnp.float32)
+        for k in range(3):
+            block_copy(pair, k).wait_recv()
+            total = total + block_ref[pair, k].astype(jnp.float32)
+        return total[:share], total[share:]
+
+    for copy in lhs_copies():
+        copy.start()
+    peer_starts(0)
+    for copy in lhs_copies():
+        copy.wait()
+
+    def within(i, low=0):
+        return (i >= low) & (i < low + PLANE)
+
+    def step(i, carry):
+        @pl.when(i + 1 < PLANE)
+        def _():
+            peer_starts(i + 1)
+
+        @pl.when(i < PLANE)
+        def _():
+            load_start(0, 1, 2 * i)
+            load_start(1, 1, 2 * i + 1)
+            for e in range(2):
+                tile = 2 * i + e
+                value = product(e, 1, tile, crossed_kind(tile))
+                if e == 0:
+                    load_start(2, 1, CROSSED + i)
+                else:
+                    load_start(0, 0, CROSSED + i)
+
+                @pl.when(i >= 2)
+                def _():
+                    given_copy(tile - 4).wait_send()
+
+                given_ref[lax.rem(tile, 4)] = value.astype(LOW)
+                given_copy(tile).start()
+            for e in range(2):
+                unit = CROSSED + 2 * i + e
+                value = product(2 - 2 * e, 1 - e, CROSSED + i, plane_kind(i))
+                sum_ref[unit] = value.astype(LOW)
+                side_copy(unit).start()
+
+        @pl.when(within(i, 1))
+        def _():
+            load_start(1, 0, 2 * i - 2)
+            load_start(2, 0, 2 * i - 1)
+            combine(PLANE + i - 1)
+            for e in range(2):
+                tile = 2 * i - 2 + e
+                value = product(1 + e, 0, tile, crossed_kind(tile))
+                given_copy(tile).wait_recv()
+                sum_ref[tile] = (value + sum_ref[tile].astype(jnp.float32)).astype(LOW)
+                side_copy(tile).start()
+
+        @pl.when(within(i, 2))
+        def _():
+            j = i - 2
+            given, kept = settle(PLANE + j)
+            out_ref[CROSSED + j] = kept
+            last_given[j] = jnp.concatenate(
+                [given, jnp.zeros((last_given.shape[1] - share, TILE), jnp.float32)], axis=0
+            ).astype(LOW)
+            last_copy(j).start()
+            combine(j)
+
+        @pl.when(within(i, 3))
+        def _():
+            j = i - 3
+            first, second = settle(j)
+            out_ref[2 * j] = first
+            out_ref[2 * j + 1] = second
+            last_copy(j).wait_recv()
+            out_ref[CROSSED + j] += last_ref[j].astype(jnp.float32)[:share]
+
+        return carry
+
+    lax.fori_loop(0, PLANE + 3, step, 0)
+
+    def drain(i, carry):
+        for e in range(4):
+            side_copy(4 * i + e).wait_send()
+        for e in range(2):
+            for k in range(3):
+                block_copy(2 * i + e, k).wait_send()
+        last_copy(i).wait_send()
+        for tile in (2 * i, 2 * i + 1, CROSSED + i):
+            for which in range(2):
+                peer_copy(which, tile).wait_send()
+        return carry
+
+    lax.fori_loop(0, PLANE, drain, 0)
+    for e in range(4):
+        given_copy(2 * PLANE - 4 + e).wait_send()
+
+
+def spread_all(lhs, rhs):
+    tiles = rhs.shape[1]
+    half = lhs.shape[2] // 2
+    share = half // 8
+    tokens = lhs.shape[3]
+    dma = pltpu.SemaphoreType.DMA
+    anywhere = pl.BlockSpec(memory_space=pl.ANY)
+    return pl.pallas_call(
+        spread_kernel,
+        out_shape=[
+            jax.ShapeDtypeStruct((tiles, share, TILE), jnp.float32),
+            jax.ShapeDtypeStruct(rhs.shape, LOW),
+        ],
+        in_specs=[anywhere, anywhere],
+        out_specs=[pl.BlockSpec(memory_space=pltpu.VMEM), anywhere],
+        scratch_shapes=[
+            pltpu.VMEM((2, lhs.shape[1], half, 2 * tokens), LOW),
+            pltpu.VMEM((3, 2 * tokens, TILE), LOW),
+            pltpu.VMEM((4, half, TILE), LOW),
+            pltpu.VMEM((4 * PLANE, half, TILE), LOW),
+            pltpu.VMEM((2 * PLANE, half, TILE), LOW),
+            pltpu.VMEM((2 * PLANE, 3, 2 * share, TILE), LOW),
+            pltpu.VMEM((PLANE, share + 8, TILE), LOW),
+            pltpu.VMEM((PLANE, share + 8, TILE), LOW),
+            dma((6,)),
+            dma((2, tiles)),
+            dma((2, tiles)),
+            dma((3, 2)),
+            dma((4,)),
+            dma((CROSSED,)),
+            dma((4 * PLANE,)),
+            dma((4 * PLANE,)),
+            dma((2 * PLANE, 3)),
+            dma((2 * PLANE, 3)),
+            dma((PLANE,)),
+            dma((PLANE,)),
+        ],
+        compiler_params=pltpu.CompilerParams(
+            collective_id=2, has_side_effects=True, vmem_limit_bytes=62 * 2**20
+        ),
+    )(lhs, rhs)[0]
+
+
+def tiled(value):
+    rows, width = value.shape
+    return value.reshape(rows, width // TILE, TILE).transpose(1, 0, 2)
+
+
+def pair_backward(grad_low, weights, saved, info, angles, arrange):
     w_in, w_out_t, w_gate, w_up, w_down_t, gain_one, gain_two = unpack(weights)
     (
         hidden,
@@ -775,8 +1284,6 @@
     def arranged(value):
         return contract(arrange, value, 1, 1).astype(LOW)
 
-    shares = {}
-    shares["down"] = spread(layer, arranged(grad_low), units, 0)
     grad_units = contract(grad_low, w_down_t, 1, 0)
     gate_wide = gate.astype(jnp.float32)
     sigmoid = jax.nn.sigmoid(gate_wide)
@@ -784,9 +1291,6 @@
         grad_units * up.astype(jnp.float32) * sigmoid * (1.0 + gate_wide * (1.0 - sigmoid))
     ).astype(LOW)
     grad_up = (grad_units * gate_wide * sigmoid).astype(LOW)
-    lhs_two = arranged(normed_two)
-    shares["gate"] = spread(layer, lhs_two, grad_gate, 0)
-    shares["up"] = spread(layer, lhs_two, grad_up, 0)
     grad_normed_two = contract(grad_gate, w_gate, 1, 1) + contract(grad_up, w_up, 1, 1)
     grad_mid_norm, grad_gain_two = rms_backward(
         grad_normed_two, middle * inverse_two, inverse_two, gain_two
@@ -810,11 +1314,23 @@
         grad_normed, hidden * inverse_one, inverse_one, gain_one
     )
     grad_hidden = (grad_middle + grad_in_norm).astype(LOW)
-    shares["out"] = spread(layer, arranged(grad_branch), o_t, 1)
-    gain_rows = jnp.zeros((SIDE, D), LOW)
+    gain_rows = jnp.zeros((rows, D), LOW)
     gain_rows = gain_rows.at[0].set(grad_gain_one.astype(LOW)).at[1].set(grad_gain_two.astype(LOW))
-    shares["in"] = spread(layer, arranged(normed), grad_mixed, 1, arranged(gain_rows))
-    return grad_hidden, shares
+    lhs = jnp.stack(
+        [arranged(v) for v in (normed_two, normed, gain_rows, grad_low, grad_branch)]
+    )
+    rhs = jnp.concatenate(
+        [
+            tiled(grad_gate),
+            tiled(grad_up),
+            tiled(grad_mixed.T),
+            jnp.eye(rows, TILE, dtype=LOW)[None],
+            tiled(units),
+            tiled(o_t.T),
+        ],
+        axis=0,
+    )
+    return grad_hidden, lhs, rhs
 
 
 def on_device_pairs(
@@ -860,12 +1376,11 @@
     shards = [
         jnp.concatenate([w_qkv[0], gain_columns], axis=1),
         w_out[0].T,
-        w_gate_up[0][:, :FF],
-        w_gate_up[0][:, FF:],
+        w_gate_up[0],
         w_down[0].T,
     ]
-    hidden = contract(moved(x_in[section, 0]), natural, 1, 1)
-    weights = gather_both(shards, section, column % 2)
+    weights, source, upstream = gather_all([x_in, cotangent], shards)
+    hidden = contract(source, natural, 1, 1)
     result_one, saved_one = pair_forward(hidden, weights[0], info, angles)
     result_two, saved_two = pair_forward(
         result_one.astype(jnp.float32), weights[1], info, angles
@@ -881,32 +1396,30 @@
         return moved(both).reshape(2, rows, D)
 
     activations = placed(result_one, result_two)
-    grad_low = contract(moved(cotangent[section, 0]), natural, 1, 1).astype(LOW)
-    grad_two, shares_two = pair_backward(
-        1, grad_low, weights[1], saved_two, info, angles, arrange
-    )
-    grad_one, shares_one = pair_backward(
-        0, grad_two, weights[0], saved_one, info, angles, arrange
-    )
+    grad_low = contract(upstream, natural, 1, 1).astype(LOW)
+    grad_two, lhs_two, rhs_two = pair_backward(
+        grad_low, weights[1], saved_two, info, angles, arrange
+    )
+    grad_one, lhs_one, rhs_one = pair_backward(
+        grad_two, weights[0], saved_one, info, angles, arrange
+    )
+    shares = spread_all(jnp.stack([lhs_one, lhs_two]), jnp.stack([rhs_one, rhs_two]))
     input_grads = placed(grad_one, grad_two).astype(jnp.float32)
 
-    def total(name):
-        one, two = shares_one[name], shares_two[name]
-        return jnp.where(
-            first_section,
-            one[0].astype(jnp.float32) + one[1].astype(jnp.float32),
-            two[0].astype(jnp.float32) + two[1].astype(jnp.float32),
-        )
-
-    term_in = total("in")
+    def joined(first, count):
+        return shares[first : first + count].transpose(1, 0, 2).reshape(share, count * TILE)
+
+    def joined_t(first, count):
+        return shares[first : first + count].transpose(0, 2, 1).reshape(count * TILE, share)
+
     return (
         activations[None, :, None],
         input_grads[None, :, None],
-        term_in[None, :, :QKV],
-        total("out").T[None],
-        jnp.concatenate([total("gate"), total("up")], axis=1)[None],
-        total("down").T[None],
-        term_in[:, QKV : QKV + 2].T[None],
+        joined(16, 5)[None],
+        joined_t(30, 3)[None],
+        joined(0, 16)[None],
+        joined_t(22, 8)[None],
+        shares[21, :, :2].T[None],
     )
 
 

time: 1290 us -> 1120 us (0.87); the launches traced: 1300 us -> 1100 us
  Pallas kernels: 61.1 us -> 579 us
  waiting for transfers between devices: 548 us -> 45.2 us
  starting transfers between devices: 259 us -> 41.7 us
  local copies, waits for them, and re-layouts: 62.8 us -> 176 us
  matrix products: 250 us -> 172 us
  other arithmetic: 95.4 us -> 67.8 us
    ppermute x98 -> x13, waiting for transfers between devices: 518 us -> 45.1 us  [swap(): lax.ppermute(value, axis, [(i, i ^ bit) for i in range(lax.axis_size(axis...]
    pallas_call x0 -> x2, Pallas kernels: none -> 472 us  [the longest x1 265 us: spread_all(): pl.pallas_call(spread_kernel, out_shape=[jax.ShapeDtypeStruct((tiles, sha...]
    ppermute x98 -> x13, starting transfers between devices: 208 us -> 3.22 us  [swap(): lax.ppermute(value, axis, [(i, i ^ bit) for i in range(lax.axis_size(axis...]
    dot_general x56 -> x36, matrix products: 250 us -> 172 us  [contract(): lax.dot_general(left, right, (((left_dim,), (right_dim,)), ((), ())), pre...]
    reshape x0 -> x10, local copies, waits for them, and re-layouts: none -> 36.2 us  [tiled(): return value.reshape(rows, width // TILE, TILE).transpose(1, 0, 2)]
    slice x21 -> x6, local copies, waits for them, and re-layouts: 10.5 us -> 45.6 us  [the longest x4 43.5 us: gather_all(): w[layer].reshape(4 * quarter, -1)]
    ppermute x10 -> x0, waiting for transfers between devices: 29.5 us -> none  [spread(): return (own, lax.ppermute(own, 'section', [(1 - layer, layer)]))]
    convert_element_type x0 -> x6, local copies, waits for them, and re-layouts: none -> 28.1 us  [the longest x2 9.37 us: pair_backward(): grad_gate = (grad_units * up.astype(jnp.float32) * sigmoid * (1.0 + gate_...]
  transfers between devices with their start and end apart: 112 -> 15, of which waited for: 35 -> 5; matrix products, arithmetic and copies ran while one was open for 24% -> 23% of each run, Pallas kernels for 4% -> 27%
where the time goes in v2:
time: 1120 us; the launch traced here: 1100 us
  Pallas kernels  579 us (52%)
  local copies, waits for them, and re-layouts  176 us (16%)
  matrix products  172 us (15%)
  other arithmetic  67.8 us (6%)
  waiting for transfers between devices  45.2 us (4%)
  starting transfers between devices  41.7 us (4%)
  between operations  20.7 us (2%)
    pallas_call x1, Pallas kernels, spread_all(): pl.pallas_call(spread_kernel, out_shape=[jax.ShapeDtypeStruct((tiles, sha...  265 us
    pallas_call x1, Pallas kernels, gather_all(): pl.pallas_call(gather_kernel, out_shape=[jax.ShapeDtypeStruct((2, 4, quar...  207 us
    dot_general x36, matrix products, contract(): lax.dot_general(left, right, (((left_dim,), (right_dim,)), ((), ())), pre...  172 us
    pallas_call x2, Pallas kernels, pair_attention_backward(): pl.pallas_call(backward_kernel, grid_spec=pltpu.PrefetchScalarGridSpec(nu...  59.8 us
    pallas_call x2, Pallas kernels, pair_attention_forward(): pl.pallas_call(forward_kernel, grid_spec=pltpu.PrefetchScalarGridSpec(num...  48 us
    unnamed x268, local copies, waits for them, and re-layouts  45.4 us
    ppermute x13, waiting for transfers between devices, swap(): lax.ppermute(value, axis, [(i, i ^ bit) for i in range(lax.axis_size(axis...  45.1 us
    slice x4, local copies, waits for them, and re-layouts, gather_all(): w[layer].reshape(4 * quarter, -1)  43.5 us
  transfers between devices with their start and end apart: 15, of which 5 were waited for; matrix products, arithmetic and copies ran while one was open for 23% of the time, Pallas kernels for 27%

profile of v2, /device:TPU:0, one launch (start us, length us, event | category | flops | bytes accessed | tf_op | source)
XLA Modules:
  0.0 1103.0 jit_solution(12937219718127166041)
XLA Ops:
  4.7 206.7 %shard_map.153 = (bf16[2,4,288,2048]{3,2,1,0:T(8,128)(2,1)}, bf16[2,4,288,1152]{3,2,1,0:T(8,128)(2,1)}, bf16[2,4,288,3072]{3,2,1,0:T(8,128)(2,1)}, bf16[2,4,288,...) custom-call(bf16[2,1,512,1152]{3,2,1,0:T(8,128)(2,1)} %refs_0_.1, ...), custom_call_target="tpu_custom_call" | custom-call | tf_op jit(solution)/shard_map/pallas_call | solution.py:886
  214.8 8.3 fusion.175
  247.1 10.6 fusion.174
  263.5 19.2 %fusion.172 = (bf16[1,4,288,3072]{3,2,1,0:T(8,128)(2,1)}, bf16[1,4,288,3072]{3,2,1,0:T(8,128)(2,1)}, bf16[1,4,288,3072]{3,2,1,0:T(8,128)(2,1)}, bf16[1,4,288,3072]{3,2,1,0:T(8,128)(2,1)}) fusion(bf16[2,4,288,3072]{3,2,1,0:T(8,128)(2,1)} %get-tuple-element.79, bf16[2,4,288,3072]{3,2,1,0:T(8,128)(2,1)} %get-tuple-element.77), kind=kLoop, calls=%fused_computation.339 | loop fusion | bytes 56623104 | tf_op jit(solution)/shard_map/slice | solution.py:902
  308.3 24.1 %shard_map.154 = (bf16[1152,512]{1,0:T(8,128)(2,1)S(1)}, f32[6,3,512]{2,1,0:T(4,128)S(1)}) custom-call(s32[5]{0:T(128)S(1)} %pad_add_fusion.live_ref, bf16[1152,512]{1,0:T(8,128)(2,1)S(1)} %bitcast.242, bf16[4,12,64,512]{3,2,1,0:T(8,128)(2,1)} %pad_maximum_fusion.2.k_ref.v_ref, bf16[4,12,64,512]{3,2,1,0:T(8,128)(2,1)} %pad_maximum_fusion.2.k_ref.v_ref, ...), custom_call_target="tpu_custom_call" | custom-call | flops 19327352832 | bytes 12582912 | tf_op jit(solution)/shard_map/pallas_call | solution.py:554
  341.3 6.6 fusion
  348.0 8.5 fusion.102
  364.6 14.7 %collective-permute-done.5 = bf16[12,64,512]{2,1,0:T(8,128)(2,1)} collective-permute-done((bf16[12,64,512]{2,1,0:T(8,128)(2,1)}, bf16[12,64,512]{2,1,0:T(8,128)(2,1)}, u32[]{:S(2)}, u32[]{:S(2)}) %collective-permute-start.5) | collective-permute-done | bytes 786464 | tf_op jit(solution)/shard_map/ppermute | solution.py:445
  400.8 23.9 %shard_map.155 = (bf16[1152,512]{1,0:T(8,128)(2,1)S(1)}, f32[6,3,512]{2,1,0:T(4,128)S(1)}) custom-call(s32[5]{0:T(128)S(1)} %pad_add_fusion.live_ref, bf16[1152,512]{1,0:T(8,128)(2,1)S(1)} %bitcast.246, bf16[4,12,64,512]{3,2,1,0:T(8,128)(2,1)} %pad_maximum_fusion.3.k_ref.v_ref, bf16[4,12,64,512]{3,2,1,0:T(8,128)(2,1)} %pad_maximum_fusion.3.k_ref.v_ref, ...), custom_call_target="tpu_custom_call" | custom-call | flops 19327352832 | bytes 12582912 | tf_op jit(solution)/shard_map/pallas_call | solution.py:554
  439.2 12.4 %fusion.19 = (bf16[512,3072]{1,0:T(8,128)(2,1)S(1)}, bf16[512,3072]{1,0:T(8,128)(2,1)S(1)}, bf16[512,3072]{1,0:T(8,128)(2,1)}) fusion(bf16[512,3072]{1,0:T(8,128)(2,1)} %convolution_convert_fusion.1, bf16[512,3072]{1,0:T(8,128)(2,1)} %convolution_convert_fusion, bf16[512,1152]{1,0:T(8,128)(2,1)S(1)} %copy-done.54, bf16[1152,3072]{1,0:T(8,128)(2,1)} %bitcast.282), kind=kOutput, calls=%fused_computation.33 | convolution fusion | flops 3652190208 | bytes 23986176 | tf_op jit(solution)/shard_map/dot_general | solution.py:436
  451.6 10.2 fusion.185
  461.8 7.0 multiply_reduce_fusion
  472.3 29.9 %shard_map.156 = (f32[1152,512]{1,0:T(8,128)}, bf16[4,6,64,512]{3,2,1,0:T(8,128)(2,1)S(1)}, bf16[4,6,64,512]{3,2,1,0:T(8,128)(2,1)}) custom-call(s32[5]{0:T(128)S(1)} %pad_add_fusion.live_ref, bf16[1152,512]{1,0:T(8,128)(2,1)S(1)} %bitcast.247, bf16[1152,512]{1,0:T(8,128)(2,1)S(1)} %convolution_convert_fusion.5.do_ref, ...), custom_call_target="tpu_custom_call" | custom-call | flops 48318382080 | bytes 12582912 | tf_op jit(solution)/shard_map/pallas_call | solution.py:588
  507.4 8.7 broadcast_select_fusion.6
  563.2 13.5 %collective-permute-done.7 = bf16[512,1152]{1,0:T(8,128)(2,1)S(1)} collective-permute-done((bf16[512,1152]{1,0:T(8,128)(2,1)}, bf16[512,1152]{1,0:T(8,128)(2,1)S(1)}, u32[]{:S(2)}, u32[]{:S(2)}) %collective-permute-start.7) | collective-permute-done | bytes 1179680 | tf_op jit(solution)/shard_map/ppermute | solution.py:445
  583.3 19.3 %collective-permute-start.8 = (bf16[1024,1152]{1,0:T(8,128)(2,1)}, bf16[1024,1152]{1,0:T(8,128)(2,1)}, u32[]{:S(2)}, u32[]{:S(2)}) collective-permute-start(bf16[1024,1152]{1,0:T(8,128)(2,1)} %fusion.38), channel_id=1, source_target_pairs={{0,0},{1,8},{2,2},{3,10},{4,4},{5,12},{6,6},{7,14},{8,1},{9,9},{10... | collective-permute-start | bytes 7077896 | tf_op jit(solution)/shard_map/ppermute | solution.py:1359
  610.3 10.3 fusion.13
  620.6 8.8 fusion.186
  629.4 7.0 multiply_reduce_fusion.1
  640.2 29.9 %shard_map.157 = (f32[1152,512]{1,0:T(8,128)}, bf16[4,6,64,512]{3,2,1,0:T(8,128)(2,1)S(1)}, bf16[4,6,64,512]{3,2,1,0:T(8,128)(2,1)}) custom-call(s32[5]{0:T(128)S(1)} %pad_add_fusion.live_ref, bf16[1152,512]{1,0:T(8,128)(2,1)S(1)} %bitcast.243, bf16[1152,512]{1,0:T(8,128)(2,1)S(1)} %convolution_convert_fusion.4.do_ref, ...), custom_call_target="tpu_custom_call" | custom-call | flops 48318382080 | bytes 12582912 | tf_op jit(solution)/shard_map/pallas_call | solution.py:588
  761.9 10.7 pad_maximum_fusion.rhs_all
  772.6 13.8 %collective-permute-done.13 = bf16[512,1152]{1,0:T(8,128)(2,1)S(1)} collective-permute-done((bf16[512,1152]{1,0:T(8,128)(2,1)}, bf16[512,1152]{1,0:T(8,128)(2,1)S(1)}, u32[]{:S(2)}, u32[]{:S(2)}) %collective-permute-start.13) | collective-permute-done | bytes 1179680 | tf_op jit(solution)/shard_map/ppermute | solution.py:445
  792.6 19.2 %collective-permute-start.14 = (bf16[1024,1152]{1,0:T(8,128)(2,1)}, bf16[1024,1152]{1,0:T(8,128)(2,1)}, u32[]{:S(2)}, u32[]{:S(2)}) collective-permute-start(bf16[1024,1152]{1,0:T(8,128)(2,1)} %fusion.39), channel_id=1, source_target_pairs={{0,0},{1,8},{2,2},{3,10},{4,4},{5,12},{6,6},{7,14},{8,1},{9,9},{10... | collective-permute-start | bytes 7077896 | tf_op jit(solution)/shard_map/ppermute | solution.py:1359
  818.7 264.9 %shard_map.158 = (f32[33,72,384]{2,1,0:T(8,128)}, bf16[2,33,512,384]{3,2,1,0:T(8,128)(2,1)}) custom-call(bf16[2,5,1152,512]{3,2,1,0:T(8,128)(2,1)} %pad_maximum_fusion.1.lhs_all, bf16[2,33,512,384]{3,2,1,0:T(8,128)(2,1)} %pad_maximum_fusion.rhs_all), custom_call_target="tpu_custom_call" | custom-call | tf_op jit(solution)/shard_map/pallas_call | solution.py:1223
  (464 shorter events, 294.3 us)
Async XLA Ops:
  0.7 258.5 %copy-start.76 = (s32[1152]{0:T(1024)}, s32[1152]{0:T(1024)S(1)}, u32[]{:S(2)}) copy-start(s32[1152]{0:T(1024)S(1)} %fusion.139) | copy-start | bytes 13828
  232.8 130.0 %copy-start.30 = (f32[32,512]{1,0:T(8,128)}, f32[32,512]{1,0:T(8,128)S(1)}, u32[]{:S(2)}) copy-start(f32[32,512]{1,0:T(8,128)S(1)} %get-tuple-element.184) | copy-start | bytes 196612
  233.9 68.5 %collective-permute-start.2 = (bf16[12,64,512]{2,1,0:T(8,128)(2,1)}, bf16[12,64,512]{2,1,0:T(8,128)(2,1)}, u32[]{:S(2)}, u32[]{:S(2)}) collective-permute-start(bf16[12,64,512]{2,1,0:T(8,128)(2,1)} %pad_maximum_fusion.10), channel_id=1, source_target_pairs={{0,4},{4,0},{8,12},{12,8},{1,5},{5,1},{9,13},{13,9},{2,6},{6,2},{1... | collective-permute-start | bytes 2359304 | tf_op jit(solution)/shard_map/ppermute | solution.py:445
  233.9 69.7 %collective-permute-start.1 = (bf16[12,64,512]{2,1,0:T(8,128)(2,1)}, bf16[12,64,512]{2,1,0:T(8,128)(2,1)}, u32[]{:S(2)}, u32[]{:S(2)}) collective-permute-start(bf16[12,64,512]{2,1,0:T(8,128)(2,1)} %pad_maximum_fusion.10), channel_id=1, source_target_pairs={{0,1},{1,0},{2,3},{3,2},{4,5},{5,4},{6,7},{7,6},{8,9},{9,8},{10,11... | collective-permute-start | bytes 2359304 | tf_op jit(solution)/shard_map/ppermute | solution.py:445
  234.3 58.9 %collective-permute-start = (s32[2,2048]{1,0:T(2,128)S(1)}, s32[2,2048]{1,0:T(2,128)S(1)}, u32[]{:S(2)}, u32[]{:S(2)}) collective-permute-start(s32[2,2048]{1,0:T(2,128)S(1)} %bitcast.340), channel_id=1, source_target_pairs={{0,1},{1,0},{2,3},{3,2},{4,5},{5,4},{6,7},{7,6},{8,9},{9,8},{10,11... | collective-permute-start | bytes 49160 | tf_op jit(solution)/shard_map/ppermute | solution.py:445
  247.1 89.3 %copy-start.66 = (f32[1152]{0:T(1024)}, f32[1152]{0:T(1024)S(1)}, u32[]{:S(2)}) copy-start(f32[1152]{0:T(1024)S(1)} %convert_reduce_fusion.2) | copy-start | bytes 13828
  259.1 101.9 %copy-start.68 = (f32[1152]{0:T(1024)}, f32[1152]{0:T(1024)S(1)}, u32[]{:S(2)}) copy-start(f32[1152]{0:T(1024)S(1)} %convert_reduce_fusion.1) | copy-start | bytes 13828
  283.1 110.3 %copy-start.79 = (s32[1152]{0:T(1024)}, s32[1152]{0:T(1024)S(1)}, u32[]{:S(2)}) copy-start(s32[1152]{0:T(1024)S(1)} %fusion.143) | copy-start | bytes 13828
  302.4 2.5 collective-permute-start.3
  359.1 20.2 %collective-permute-start.5 = (bf16[12,64,512]{2,1,0:T(8,128)(2,1)}, bf16[12,64,512]{2,1,0:T(8,128)(2,1)}, u32[]{:S(2)}, u32[]{:S(2)}) collective-permute-start(bf16[12,64,512]{2,1,0:T(8,128)(2,1)} %pad_maximum_fusion.11), channel_id=1, source_target_pairs={{0,4},{4,0},{8,12},{12,8},{1,5},{5,1},{9,13},{13,9},{2,6},{6,2},{1... | collective-permute-start | bytes 2359304 | tf_op jit(solution)/shard_map/ppermute | solution.py:445
  359.1 36.1 %collective-permute-start.4 = (bf16[12,64,512]{2,1,0:T(8,128)(2,1)}, bf16[12,64,512]{2,1,0:T(8,128)(2,1)}, u32[]{:S(2)}, u32[]{:S(2)}) collective-permute-start(bf16[12,64,512]{2,1,0:T(8,128)(2,1)} %pad_maximum_fusion.11), channel_id=1, source_target_pairs={{0,1},{1,0},{2,3},{3,2},{4,5},{5,4},{6,7},{7,6},{8,9},{9,8},{10,11... | collective-permute-start | bytes 2359304 | tf_op jit(solution)/shard_map/ppermute | solution.py:445
  379.3 15.9 %collective-permute-start.6 = (bf16[12,64,512]{2,1,0:T(8,128)(2,1)}, bf16[12,64,512]{2,1,0:T(8,128)(2,1)}, u32[]{:S(2)}, u32[]{:S(2)}) collective-permute-start(bf16[12,64,512]{2,1,0:T(8,128)(2,1)} %collective-permute-done.5), channel_id=1, source_target_pairs={{0,1},{1,0},{2,3},{3,2},{4,5},{5,4},{6,7},{7,6},{8,9},{9,8},{10,11... | collective-permute-start | bytes 2359304 | tf_op jit(solution)/shard_map/ppermute | solution.py:445
  506.1 50.9 %collective-permute-start.9 = (bf16[2,12,64,512]{3,2,1,0:T(8,128)(2,1)}, bf16[2,12,64,512]{3,2,1,0:T(8,128)(2,1)}, u32[]{:S(2)}, u32[]{:S(2)}) collective-permute-start(bf16[2,12,64,512]{3,2,1,0:T(8,128)(2,1)} %pad_maximum_fusion.6), channel_id=1, source_target_pairs={{0,1},{1,0},{2,3},{3,2},{4,5},{5,4},{6,7},{7,6},{8,9},{9,8},{10,11... | collective-permute-start | bytes 4718600 | tf_op jit(solution)/shard_map/ppermute | solution.py:445
  549.4 27.3 %collective-permute-start.7 = (bf16[512,1152]{1,0:T(8,128)(2,1)}, bf16[512,1152]{1,0:T(8,128)(2,1)S(1)}, u32[]{:S(2)}, u32[]{:S(2)}) collective-permute-start(bf16[512,1152]{1,0:T(8,128)(2,1)} %get-tuple-element.202), channel_id=1, source_target_pairs={{0,16},{16,0},{1,17},{17,1},{2,18},{18,2},{3,19},{19,3},{4,20},{20... | collective-permute-start | bytes 3538952 | tf_op jit(solution)/shard_map/ppermute | solution.py:445
  556.9 26.3 %copy-start.6 = (bf16[33,512,384]{2,1,0:T(8,128)(2,1)}, bf16[33,512,384]{2,1,0:T(8,128)(2,1)S(1)}, u32[]{:S(2)}) copy-start(bf16[33,512,384]{2,1,0:T(8,128)(2,1)S(1)} %bitcast_dynamic-update-slice_fusion.1) | copy-start | bytes 38928388
  563.1 39.4 %collective-permute-start.10 = (bf16[12,64,512]{2,1,0:T(8,128)(2,1)S(1)}, bf16[12,64,512]{2,1,0:T(8,128)(2,1)S(1)}, u32[]{:S(2)}, u32[]{:S(2)}) collective-permute-start(bf16[12,64,512]{2,1,0:T(8,128)(2,1)S(1)} %fusion.119), channel_id=1, source_target_pairs={{0,4},{4,0},{8,12},{12,8},{1,5},{5,1},{9,13},{13,9},{2,6},{6,2},{1... | collective-permute-start | bytes 2359304 | tf_op jit(solution)/shard_map/ppermute | solution.py:445
  576.7 26.4 %slice-start.26 = ((s8[4718592]{0:T(1024)(128)(4,1)}), s8[4194304]{0:T(1024)(128)(4,1)S(1)}, s32[]{:S(2)}) async-start(s8[4718592]{0:T(1024)(128)(4,1)} %bitcast.299), calls=%async_computation.26 | async-start | bytes 8388608
  583.3 147.2 %collective-permute-start.8 = (bf16[1024,1152]{1,0:T(8,128)(2,1)}, bf16[1024,1152]{1,0:T(8,128)(2,1)}, u32[]{:S(2)}, u32[]{:S(2)}) collective-permute-start(bf16[1024,1152]{1,0:T(8,128)(2,1)} %fusion.38), channel_id=1, source_target_pairs={{0,0},{1,8},{2,2},{3,10},{4,4},{5,12},{6,6},{7,14},{8,1},{9,9},{10... | collective-permute-start | bytes 7077896 | tf_op jit(solution)/shard_map/ppermute | solution.py:1359
  674.0 33.1 %collective-permute-start.11 = (bf16[2,12,64,512]{3,2,1,0:T(8,128)(2,1)}, bf16[2,12,64,512]{3,2,1,0:T(8,128)(2,1)}, u32[]{:S(2)}, u32[]{:S(2)}) collective-permute-start(bf16[2,12,64,512]{3,2,1,0:T(8,128)(2,1)} %pad_maximum_fusion.7), channel_id=1, source_target_pairs={{0,1},{1,0},{2,3},{3,2},{4,5},{5,4},{6,7},{7,6},{8,9},{9,8},{10,11... | collective-permute-start | bytes 4718600 | tf_op jit(solution)/shard_map/ppermute | solution.py:445
  712.9 19.4 %collective-permute-start.12 = (bf16[12,64,512]{2,1,0:T(8,128)(2,1)}, bf16[12,64,512]{2,1,0:T(8,128)(2,1)}, u32[]{:S(2)}, u32[]{:S(2)}) collective-permute-start(bf16[12,64,512]{2,1,0:T(8,128)(2,1)} %fusion.120), channel_id=1, source_target_pairs={{0,4},{4,0},{8,12},{12,8},{1,5},{5,1},{9,13},{13,9},{2,6},{6,2},{1... | collective-permute-start | bytes 2359304 | tf_op jit(solution)/shard_map/ppermute | solution.py:445
  759.6 26.8 %collective-permute-start.13 = (bf16[512,1152]{1,0:T(8,128)(2,1)}, bf16[512,1152]{1,0:T(8,128)(2,1)S(1)}, u32[]{:S(2)}, u32[]{:S(2)}) collective-permute-start(bf16[512,1152]{1,0:T(8,128)(2,1)} %get-tuple-element.128), channel_id=1, source_target_pairs={{0,16},{16,0},{1,17},{17,1},{2,18},{18,2},{3,19},{19,3},{4,20},{20... | collective-permute-start | bytes 3538952 | tf_op jit(solution)/shard_map/ppermute | solution.py:445
  786.4 27.2 %slice-start.28 = ((s8[5898240]{0:T(1024)(128)(4,1)}), s8[4194304]{0:T(1024)(128)(4,1)S(1)}, s32[]{:S(2)}) async-start(s8[5898240]{0:T(1024)(128)(4,1)} %bitcast.302), calls=%async_computation.28 | async-start | bytes 8388608
  786.7 26.9 %slice-start.29 = ((s8[5898240]{0:T(1024)(128)(4,1)}), s8[1703936]{0:T(1024)(128)(4,1)S(1)}, s32[]{:S(2)}) async-start(s8[5898240]{0:T(1024)(128)(4,1)} %bitcast.302), calls=%async_computation.29 | async-start | bytes 3407872
  792.6 302.6 %collective-permute-start.14 = (bf16[1024,1152]{1,0:T(8,128)(2,1)}, bf16[1024,1152]{1,0:T(8,128)(2,1)}, u32[]{:S(2)}, u32[]{:S(2)}) collective-permute-start(bf16[1024,1152]{1,0:T(8,128)(2,1)} %fusion.39), channel_id=1, source_target_pairs={{0,0},{1,8},{2,2},{3,10},{4,4},{5,12},{6,6},{7,14},{8,1},{9,9},{10... | collective-permute-start | bytes 7077896 | tf_op jit(solution)/shard_map/ppermute | solution.py:1359
  (116 other events, 894.3 us)

commit v3 on v0

--- a/solution.py
+++ b/solution.py
@@ -1,6 +1,10 @@
+import functools
+
 import jax
 import jax.numpy as jnp
 from jax import lax
+from jax.experimental import pallas as pl
+from jax.experimental.pallas import tpu as pltpu
 from jax.sharding import PartitionSpec as P
 
 D = 1152
@@ -8,6 +12,7 @@
 KV = 6
 HD = 64
 FF = 3072
+SECTION, CTX, WSH = "section", "ctx", "wsh"
 
 
 NEG = -1e30
@@ -322,7 +327,7 @@
     )
 
 
-def on_device(x_in, cotangent, w_qkv, w_out, w_gate_up, w_down, gains, order, visible, seq_ids):
+def on_device_general(x_in, cotangent, w_qkv, w_out, w_gate_up, w_down, gains, order, visible, seq_ids):
     section = lax.axis_index("section")
     column = lax.axis_index("ctx")
     n_ctx = lax.axis_size("ctx")
@@ -418,6 +423,1985 @@
     )
 
 
+GROUP = H // KV
+QD = H * HD
+KD = KV * HD
+QKV = QD + 2 * KD
+SIDE = 128
+LOW = jnp.bfloat16
+
+
+def fits_pairs(mesh):
+    return mesh.shape[SECTION] == 2 and mesh.shape[CTX] == 4 and mesh.shape[WSH] == 4
+
+
+def contract(left, right, left_dim, right_dim):
+    return lax.dot_general(
+        left,
+        right,
+        (((left_dim,), (right_dim,)), ((), ())),
+        preferred_element_type=jnp.float32,
+    )
+
+
+def swap(value, axis, bit):
+    return lax.ppermute(value, axis, [(i, i ^ bit) for i in range(lax.axis_size(axis))])
+
+
+def after(value, *others):
+    return lax.optimization_barrier((value, *others))[0]
+
+
+def masked_pair(first, second):
+    return jnp.concatenate([first, second], axis=0)
+
+
+def attend(queries, masks, keys_of, values_of, key_mask_of, first, last, slot_of):
+    rows = masks.shape[1]
+    query = masked_pair(
+        jnp.concatenate(queries, axis=1), jnp.concatenate([masks] * GROUP, axis=1)
+    )
+
+    def step(i, state):
+        high, acc = state
+        slot = slot_of(i)
+        value_t = values_of(slot)
+        ones = jnp.ones((1, value_t.shape[1]), jnp.float32)
+        ones = jnp.concatenate([ones, jnp.zeros((15, value_t.shape[1]), jnp.float32)], axis=0)
+        scores = contract(masked_pair(keys_of(slot), key_mask_of(slot)), query, 0, 0)
+        top = jnp.maximum(high, jnp.max(scores, axis=0, keepdims=True))
+        terms = jnp.exp(scores - top).astype(LOW)
+        fresh = contract(masked_pair(value_t, ones.astype(LOW)), terms, 1, 0)
+        return top, acc * jnp.exp(high - top) + fresh
+
+    start = (
+        jnp.full((1, GROUP * rows), NEG, jnp.float32),
+        jnp.zeros((HD + 16, GROUP * rows), jnp.float32),
+    )
+    high, acc = lax.fori_loop(first, last, step, start)
+    total = acc[HD : HD + 1]
+    out = (acc[:HD] / total).astype(LOW)
+    log_total = high + jnp.log(total)
+    cuts = [slice(j * rows, (j + 1) * rows) for j in range(GROUP)]
+    return [out[:, c] for c in cuts], [log_total[:, c] for c in cuts]
+
+
+def forward_kernel(live_ref, q_ref, k_ref, v_ref, key_mask_ref, mask_ref, o_ref, lse_ref):
+    out, log_total = attend(
+        [q_ref[pl.ds(j * HD, HD), :] for j in range(GROUP)],
+        mask_ref[...],
+        lambda slot: k_ref[slot, 0],
+        lambda slot: v_ref[slot, 0],
+        lambda slot: key_mask_ref[slot],
+        0,
+        live_ref[0],
+        lambda i: live_ref[1 + i],
+    )
+    for j in range(GROUP):
+        o_ref[pl.ds(j * HD, HD), :] = out[j]
+        lse_ref[0, pl.ds(j, 1), :] = log_total[j]
+
+
+def backward_kernel(
+    live_ref,
+    q_ref,
+    do_ref,
+    o_ref,
+    lse_ref,
+    k_ref,
+    v_ref,
+    key_mask_ref,
+    mask_ref,
+    dq_ref,
+    dk_ref,
+    dv_ref,
+    acc_ref,
+):
+    rows = q_ref.shape[1]
+    acc_ref[...] = jnp.zeros_like(acc_ref)
+    dk_ref[...] = jnp.zeros_like(dk_ref)
+    dv_ref[...] = jnp.zeros_like(dv_ref)
+    parts = [pl.ds(j * HD, HD) for j in range(GROUP)]
+    query_t = jnp.concatenate([q_ref[part, :] for part in parts], axis=1)
+    grad_t = jnp.concatenate([do_ref[part, :] for part in parts], axis=1)
+    out_t = jnp.concatenate([o_ref[part, :] for part in parts], axis=1)
+    log_total = jnp.concatenate([lse_ref[0, pl.ds(j, 1), :] for j in range(GROUP)], axis=1)
+    both = grad_t.astype(jnp.float32) * out_t.astype(jnp.float32)
+    delta = jnp.sum(both, axis=0, keepdims=True)
+    query = masked_pair(query_t, jnp.concatenate([mask_ref[...]] * GROUP, axis=1))
+
+    def step(i, carry):
+        slot = live_ref[1 + i]
+        key_t = k_ref[slot, 0]
+        scores = contract(masked_pair(key_t, key_mask_ref[slot]), query, 0, 0)
+        probs = jnp.exp(scores - log_total)
+        grad_probs = contract(v_ref[slot, 0], grad_t, 0, 0)
+        grad_scores = (probs * (grad_probs - delta)).astype(LOW)
+        grad_v = contract(probs.astype(LOW), grad_t, 1, 1)
+        grad_k = contract(grad_scores, query_t, 1, 1)
+        acc_ref[...] += contract(key_t, grad_scores, 1, 0)
+        dk_ref[slot, 0] = jnp.transpose(grad_k).astype(LOW)
+        dv_ref[slot, 0] = jnp.transpose(grad_v).astype(LOW)
+        return carry
+
+    lax.fori_loop(0, live_ref[0], step, 0)
+    for j in range(GROUP):
+        cut = slice(j * rows, (j + 1) * rows)
+        dq_ref[parts[j], :] = acc_ref[:, cut] * HD ** (-0.5)
+
+
+def long_cost(microseconds):
+    return pl.CostEstimate(
+        flops=microseconds * 10**9, bytes_accessed=2**20, transcendentals=0
+    )
+
+
+def kernel_cost(scores, matmuls):
+    return pl.CostEstimate(
+        flops=scores * matmuls * HD * 2 * 4, bytes_accessed=12 * 2**20, transcendentals=scores
+    )
+
+
+def pair_attention_forward(info, q_t, kv_t):
+    live, key_masks, masks = info
+    slots, keys = kv_t.shape[0], kv_t.shape[3]
+    rows = q_t.shape[1]
+    return pl.pallas_call(
+        forward_kernel,
+        grid_spec=pltpu.PrefetchScalarGridSpec(
+            num_scalar_prefetch=1,
+            grid=(KV,),
+            in_specs=[
+                pl.BlockSpec((GROUP * HD, rows), lambda g, l: (g, 0)),
+                pl.BlockSpec((slots, 1, HD, keys), lambda g, l: (0, g, 0, 0)),
+                pl.BlockSpec((slots, 1, HD, keys), lambda g, l: (0, KV + g, 0, 0)),
+                pl.BlockSpec((slots, 16, keys), lambda g, l: (0, 0, 0)),
+                pl.BlockSpec((16, rows), lambda g, l: (0, 0)),
+            ],
+            out_specs=[
+                pl.BlockSpec((GROUP * HD, rows), lambda g, l: (g, 0)),
+                pl.BlockSpec((1, GROUP, rows), lambda g, l: (g, 0, 0)),
+            ],
+        ),
+        out_shape=[
+            jax.ShapeDtypeStruct(q_t.shape, LOW),
+            jax.ShapeDtypeStruct((KV, GROUP, rows), jnp.float32),
+        ],
+        compiler_params=pltpu.CompilerParams(vmem_limit_bytes=62 * 2**20),
+        cost_estimate=kernel_cost(H * rows * slots * keys, 2),
+    )(live, q_t, kv_t, kv_t, key_masks, masks)
+
+
+def pair_attention_backward(info, q_t, do_t, o_t, lse, kv_t):
+    live, key_masks, masks = info
+    slots, keys = kv_t.shape[0], kv_t.shape[3]
+    rows = q_t.shape[1]
+    q_spec = pl.BlockSpec((GROUP * HD, rows), lambda g, l: (g, 0))
+    part_spec = pl.BlockSpec((slots, 1, HD, keys), lambda g, l: (0, g, 0, 0))
+    part_shape = jax.ShapeDtypeStruct((slots, KV, HD, keys), LOW)
+    return pl.pallas_call(
+        backward_kernel,
+        grid_spec=pltpu.PrefetchScalarGridSpec(
+            num_scalar_prefetch=1,
+            grid=(KV,),
+            in_specs=[
+                q_spec,
+                q_spec,
+                q_spec,
+                pl.BlockSpec((1, GROUP, rows), lambda g, l: (g, 0, 0)),
+                part_spec,
+                pl.BlockSpec((slots, 1, HD, keys), lambda g, l: (0, KV + g, 0, 0)),
+                pl.BlockSpec((slots, 16, keys), lambda g, l: (0, 0, 0)),
+                pl.BlockSpec((16, rows), lambda g, l: (0, 0)),
+            ],
+            out_specs=[q_spec, part_spec, part_spec],
+            scratch_shapes=[pltpu.VMEM((HD, GROUP * rows), jnp.float32)],
+        ),
+        out_shape=[jax.ShapeDtypeStruct(q_t.shape, jnp.float32), part_shape, part_shape],
+        compiler_params=pltpu.CompilerParams(vmem_limit_bytes=62 * 2**20),
+        cost_estimate=kernel_cost(H * rows * slots * keys, 5),
+    )(live, q_t, do_t, o_t, lse, kv_t, kv_t, key_masks, masks)
+
+
+def turn(heads, cosine, sine):
+    half = HD // 2
+    first, second = heads[:, :half], heads[:, half:]
+    return jnp.concatenate(
+        [first * cosine - second * sine, first * sine + second * cosine], axis=1
+    )
+
+
+def pair_angles(own_block, rows):
+    positions = own_block * rows + jnp.arange(rows, dtype=jnp.int32)
+    frequency = 10000.0 ** (-(jnp.arange(HD // 2, dtype=jnp.float32) * 2.0 / HD))
+    angles = frequency[:, None] * positions.astype(jnp.float32)[None, :]
+    return jnp.cos(angles), jnp.sin(angles)
+
+
+MESH_ID = pl.DeviceIdType.MESH
+
+
+def stream_partner(column, place):
+    core = place % 2
+    moving = (column < 2) == (core == 1)
+    return moving, lax.rem(column + 2, 4), place + 1 - 2 * core
+
+
+def first_kernel(*refs):
+    x_ref, shard_refs = refs[0], refs[1:5]
+    seq_all_ref, cos_ref, sin_ref, order_ref, visible_ref = refs[5:10]
+    full_refs = refs[10:15]
+    (
+        hidden_ref,
+        q_ref,
+        kv_out,
+        o_ref,
+        lse_ref,
+        result_ref,
+        middle_ref,
+        lhs_out,
+        attended_out,
+        units_out,
+        gate_out,
+        up_out,
+        stream_ref,
+        gains_ref,
+        next_q_ref,
+        next_kv_out,
+        natural_out_ref,
+        key_mask_out,
+        mask_out,
+        live_ref,
+        natural_ref,
+    ) = refs[15:36]
+    (
+        send_sem,
+        recv_sem,
+        store_sem,
+        hold_sem,
+        local_sem,
+        ring_ref,
+        rows_ref,
+        w_in_ref,
+        w_out_ref,
+        w_mlp_ref,
+        w_down_ref,
+        units_ref,
+        gate_ref,
+        up_ref,
+        normed_ref,
+        turned_ref,
+        attended_ref,
+        acc_ref,
+        kv_ref,
+        seq_peer_ref,
+        key_mask_ref,
+        mask_ref,
+        gain_ref,
+        next_kv_ref,
+        seq_ref,
+    ) = refs[36:]
+    section = lax.axis_index(SECTION)
+    column = lax.axis_index(CTX)
+    place = lax.axis_index(WSH)
+    half = lax.rem(column, 2)
+    core = lax.rem(place, 2)
+    other = 1 - section
+    over_x = (section, column, lax.rem(place + 2, 4))
+    over_y = (other, column, place)
+    over_z = (section, column + 1 - 2 * half, place)
+    over_core = (section, column, place + 1 - 2 * core)
+    moving, partner_column, partner_place = stream_partner(column, place)
+    partner = (section, partner_column, partner_place)
+
+    barrier = pltpu.get_barrier_semaphore()
+    for target in (over_x, over_y, over_z, over_core):
+        pl.semaphore_signal(barrier, inc=1, device_id=target, device_id_type=MESH_ID)
+
+    @pl.when(moving)
+    def _():
+        pl.semaphore_signal(barrier, inc=1, device_id=partner, device_id_type=MESH_ID)
+        pl.semaphore_wait(barrier, 5)
+
+    @pl.when(jnp.logical_not(moving))
+    def _():
+        pl.semaphore_wait(barrier, 4)
+
+    seq_ref[...] = seq_all_ref[section].astype(jnp.float32)
+    in_shard, out_shard, gate_up_shard, down_shard = shard_refs
+    sources = [
+        (in_shard, 0, full_refs[0], 1024),
+        (out_shard, 0, full_refs[1], QD),
+        (gate_up_shard, 0, full_refs[2], WIDE),
+        (gate_up_shard, FF, full_refs[3], WIDE),
+        (down_shard, 0, full_refs[4], WIDE),
+    ]
+    pieces = []
+    for shard_ref, offset, full_ref, step in sources:
+        for first in range(0, full_ref.shape[2], step):
+            pieces.append((shard_ref, offset + first, full_ref, first, step))
+    count = len(pieces)
+    direct = (13, 14)
+    quarter = in_shard.shape[0]
+    mid = quarter // 2
+    rows = hidden_ref.shape[0]
+
+    def own(k):
+        shard_ref, offset, full_ref, first, step = pieces[k]
+        return shard_ref.at[:, pl.ds(offset, step)]
+
+    def own_half(k):
+        shard_ref, offset, full_ref, first, step = pieces[k]
+        return shard_ref.at[pl.ds(half * mid, mid), pl.ds(offset, step)]
+
+    def full(k, layer, block):
+        shard_ref, offset, full_ref, first, step = pieces[k]
+        return full_ref.at[layer, pl.ds(block * quarter, quarter), pl.ds(first, step)]
+
+    def full_half(k, layer, block, which):
+        shard_ref, offset, full_ref, first, step = pieces[k]
+        span = pl.ds(block * quarter + which * mid, mid)
+        return full_ref.at[layer, span, pl.ds(first, step)]
+
+    started = {}
+    arrived = set()
+
+    def remote(kind, k, source, target, device):
+        return pltpu.make_async_remote_copy(
+            src_ref=source,
+            dst_ref=target,
+            send_sem=send_sem.at[kind, k],
+            recv_sem=recv_sem.at[kind, k],
+            device_id=device,
+            device_id_type=MESH_ID,
+        )
+
+    def send(kind, k, source, target, device):
+        copy = remote(kind, k, source, target, device)
+        copy.start()
+        started[kind, k] = copy
+
+    def receive(kind, k):
+        if (kind, k) not in arrived:
+            arrived.add((kind, k))
+            started[kind, k].wait_recv()
+
+    def start_near(k):
+        if k < count:
+            send(0, k, own(k), full(k, section, 2), over_x)
+
+    def start_cross(k):
+        if k in direct:
+            send(1, k, own(k), full(k, section, 0), over_y)
+        elif k < count:
+            send(1, k, own_half(k), full_half(k, section, 0, half), over_y)
+
+    def ring(k):
+        return ring_ref.at[k % 2, :, pl.ds(0, pieces[k][4])]
+
+    def hold(k):
+        return pltpu.make_async_copy(own(k), ring(k), hold_sem.at[k % 2])
+
+    def store(k):
+        return pltpu.make_async_copy(ring(k), full(k, section, 0), store_sem.at[k])
+
+    stored_pieces = set()
+
+    def need(k):
+        for kind in range(5, 10 if k in direct else 11):
+            receive(kind, k)
+        if k not in stored_pieces:
+            stored_pieces.add(k)
+            store(k).wait()
+
+    local_copies = {}
+
+    def begin(name, source, target):
+        copy = pltpu.make_async_copy(source, target, local_sem.at[len(local_copies)])
+        local_copies[name] = copy
+        copy.start()
+
+    def finish(name):
+        local_copies[name].wait()
+
+    row_source = x_ref.at[section, 0]
+    row_move = remote(11, 0, row_source, rows_ref, partner)
+    row_copy = pltpu.make_async_copy(row_source, rows_ref, hold_sem.at[2])
+
+    def move_rows():
+        @pl.when(moving)
+        def _():
+            row_move.wait()
+
+        @pl.when(jnp.logical_not(moving))
+        def _():
+            row_copy.wait()
+
+        share = quarter // 4
+        index = lax.broadcasted_iota(jnp.int32, (D, 1), 0)
+        block, inner = index // quarter, index % quarter
+        to_core, to_side = inner // (2 * share), inner % (2 * share) // share
+        index = (block ^ place) * quarter + (2 * to_side + to_core) * share + inner % share
+        lane = lax.broadcasted_iota(jnp.int32, (D, D), 1)
+        natural_ref[...] = jnp.where(index == lane, 1.0, 0.0).astype(LOW)
+        hidden_ref[...] = contract(rows_ref[...], natural_ref[...], 1, 1).astype(LOW)
+
+    def make_masks():
+        receive(11, 1)
+        own_stream = jnp.broadcast_to(core == column // 2, seq_ref.shape)
+        stream_ref[...] = jnp.where(own_stream, seq_ref[...], seq_peer_ref[...])
+        slot = half + 2 * core
+        own_block = order_ref[section, slot]
+        alive, spans = [], []
+        for p, step in enumerate((0, 2, 1, 3)):
+            at = slot ^ step
+            span = pl.ds(pl.multiple_of(at * rows, rows), rows)
+            ids = stream_ref[:, span]
+            seen = visible_ref[own_block, order_ref[section, at]].astype(jnp.float32)
+            unseen = jnp.full((1, rows), 1.0, jnp.float32) * (1.0 - seen)
+            blank = jnp.zeros((13, rows), jnp.float32)
+            key_mask = jnp.concatenate([ids, 1.0 - ids, unseen, blank], axis=0) * NEG
+            key_mask_ref[p] = key_mask.astype(LOW)
+            spans.append((jnp.min(ids), jnp.max(ids)))
+            if p == 0:
+                ones = jnp.ones((1, rows), jnp.float32)
+                mask_ref[...] = jnp.concatenate([1.0 - ids, ids, ones, blank], axis=0).astype(LOW)
+                alive.append(jnp.int32(1))
+            else:
+                shared = (spans[p][0] <= spans[0][1]) & (spans[0][0] <= spans[p][1])
+                alive.append(jnp.where(shared & (seen > 0.5), 1, 0).astype(jnp.int32))
+        key_mask_out[...] = key_mask_ref[...]
+        mask_out[...] = mask_ref[...]
+        found = [sum(alive[:p], jnp.int32(0)) for p in range(5)]
+        live_ref[0] = found[4]
+        for j in range(4):
+            live_ref[1 + j] = sum(
+                (jnp.where((alive[p] == 1) & (found[p] == j), p, 0) for p in range(1, 4)),
+                jnp.int32(0),
+            )
+
+    def load_in(layer):
+        need(0)
+        need(1)
+        begin((0, layer), full_refs[0].at[layer], w_in_ref)
+
+    def make_keys(layer, source_ref, keys_ref, first):
+        if layer == 0:
+            finish((0, 0))
+            gain_ref[0] = w_in_ref[:, pl.ds(QKV, SIDE)].astype(jnp.float32).T[:8]
+        else:
+            finish((1, 0))
+        unit_rows, unused = norm_parts(source_ref[...].astype(jnp.float32))
+        normed = (unit_rows * gain_ref[layer, :1]).astype(LOW)
+        normed_ref[...] = normed
+        turned_ref[1] = normed.T
+        begin((1, layer), turned_ref.at[1], lhs_out.at[layer, 3])
+        for part in range(2):
+            cut = pl.ds(QD + part * KD, KD)
+            heads = jnp.dot(normed, w_in_ref[:, cut], preferred_element_type=jnp.float32).T
+            heads = heads.reshape(KV, HD, rows)
+            if part == 0:
+                heads = turn(heads, cos_ref[...], sin_ref[...])
+            keys_ref[0, pl.ds(part * KV, KV)] = heads.astype(LOW)
+        send(11, first, keys_ref.at[0], keys_ref.at[2], over_z)
+        send(11, first + 1, keys_ref.at[0], keys_ref.at[1], over_core)
+
+    def make_queries(target_ref):
+        normed = normed_ref[...]
+        for part in range(QD // KD):
+            heads = jnp.dot(
+                normed, w_in_ref[:, pl.ds(part * KD, KD)], preferred_element_type=jnp.float32
+            ).T
+            turned = turn(heads.reshape(KV, HD, rows), cos_ref[...], sin_ref[...])
+            turned = turned.astype(LOW).astype(jnp.float32) * HD ** (-0.5)
+            target_ref[pl.ds(part * KD, KD), :] = turned.astype(LOW).reshape(KD, rows)
+
+    def take_keys(layer, keys_ref, keys_out, first):
+        receive(11, first)
+        send(11, first + 2, keys_ref.at[2], keys_ref.at[3], over_core)
+        receive(11, first + 1)
+        receive(11, first + 2)
+        begin((2, layer), keys_ref, keys_out)
+
+    def attention(first, last):
+        def one(g, carry):
+            spans = [
+                pl.ds(pl.multiple_of(g * GROUP * HD + j * HD, HD), HD) for j in range(GROUP)
+            ]
+            out, log_total = attend(
+                [q_ref[span, :] for span in spans],
+                mask_ref[...],
+                lambda slot: kv_ref[slot, g],
+                lambda slot: kv_ref[slot, KV + g],
+                lambda slot: key_mask_ref[slot],
+                0,
+                4,
+                lambda i: i,
+            )
+            for j in range(GROUP):
+                o_ref[spans[j], :] = out[j]
+            lse_ref[g] = jnp.concatenate(log_total, axis=0)
+            return carry
+
+        lax.fori_loop(first, last, one, 0)
+
+    def load_out():
+        need(2)
+        begin((3, 0), full_refs[1].at[0], w_out_ref)
+
+    def make_middle():
+        attended = o_ref[...].T
+        for t in range(QD // TILE):
+            attended_ref[t] = attended[:, t * TILE : (t + 1) * TILE]
+        begin((4, 0), attended_ref, attended_out.at[0])
+        finish((3, 0))
+        added = jnp.dot(w_out_ref[...], o_ref[...], preferred_element_type=jnp.float32)
+        middle = hidden_ref[...].astype(jnp.float32) + added.T
+        middle_ref[...] = middle
+        acc_ref[...] = jnp.zeros_like(acc_ref)
+        unit_rows, unused = norm_parts(middle)
+        normed = (unit_rows * gain_ref[0, 1:2]).astype(LOW)
+        normed_ref[...] = normed
+        turned_ref[0] = normed.T
+        begin((5, 0), turned_ref.at[0], lhs_out.at[0, 2])
+
+    per = WIDE // TILE
+
+    def load_mlp(t):
+        need(3 + t)
+        need(7 + t)
+        span = pl.ds(t * WIDE, WIDE)
+        begin((6, t), full_refs[2].at[0, :, span], w_mlp_ref.at[t % 2, 0])
+        begin((7, t), full_refs[3].at[0, :, span], w_mlp_ref.at[t % 2, 1])
+
+    def make_units(t):
+        finish((6, t))
+        finish((7, t))
+        normed = normed_ref[...]
+        gate = jnp.dot(normed, w_mlp_ref[t % 2, 0], preferred_element_type=jnp.float32)
+        up = jnp.dot(normed, w_mlp_ref[t % 2, 1], preferred_element_type=jnp.float32)
+        units = (gate * sigmoid_of(gate) * up).astype(LOW)
+        gate_low, up_low = gate.astype(LOW), up.astype(LOW)
+        for i in range(per):
+            cut = slice(i * TILE, (i + 1) * TILE)
+            gate_ref[per * t + i] = gate_low[:, cut]
+            up_ref[per * t + i] = up_low[:, cut]
+            units_ref[per * t + i] = units[:, cut]
+        span = pl.ds(per * t, per)
+        begin((8, t), units_ref.at[span], units_out.at[0, span])
+        begin((9, t), gate_ref.at[span], gate_out.at[span])
+        begin((10, t), up_ref.at[span], up_out.at[span])
+
+    def load_down(t):
+        need(11 + t)
+        span = pl.ds(t * WIDE, WIDE)
+        begin((11, t), full_refs[4].at[0, :, span], w_down_ref.at[t % 2])
+
+    def add_down(t):
+        finish((11, t))
+        units = jnp.concatenate([units_ref[per * t + i] for i in range(per)], axis=1)
+        acc_ref[...] += jnp.dot(w_down_ref[t % 2], units.T, preferred_element_type=jnp.float32)
+
+    def make_late_gains():
+        finish((0, 1))
+        gain_ref[1] = w_in_ref[:, pl.ds(QKV, SIDE)].astype(jnp.float32).T[:8]
+        gains_ref[...] = gain_ref[...]
+
+    tasks = {
+        1: [make_masks],
+        2: [move_rows],
+        3: [lambda: load_in(0)],
+        4: [lambda: make_keys(0, hidden_ref, kv_ref, 2), lambda: make_queries(q_ref)],
+        6: [lambda: take_keys(0, kv_ref, kv_out, 2), lambda: attention(0, 1), load_out],
+        7: [lambda: attention(1, 2)],
+        8: [lambda: attention(2, 3)],
+        9: [lambda: attention(3, 4)],
+        10: [lambda: attention(4, 5)],
+        11: [lambda: attention(5, 6), make_middle, lambda: load_mlp(0), lambda: load_in(1)],
+        12: [lambda: load_mlp(1), lambda: make_units(0), make_late_gains],
+        13: [lambda: load_mlp(2), lambda: make_units(1)],
+        14: [lambda: load_mlp(3), lambda: make_units(2), lambda: load_down(0)],
+        15: [lambda: make_units(3)],
+        16: [lambda: load_down(1), lambda: add_down(0), lambda: load_down(2), lambda: add_down(1)],
+    }
+
+    ahead = 3
+    for k in range(ahead):
+        start_near(k)
+        start_cross(k)
+
+    @pl.when(moving)
+    def _():
+        row_move.start()
+
+    @pl.when(jnp.logical_not(moving))
+    def _():
+        row_copy.start()
+
+    send(11, 1, seq_ref, seq_peer_ref, over_core)
+    hold(0).start()
+    for k in range(count):
+        send(5, k, own(k), full(k, section, 1), over_core)
+
+    for k in range(count + 2):
+        if k < count:
+            hold(k).wait()
+            store(k).start()
+            if k + 1 < count:
+                if k >= 1 and k - 1 not in stored_pieces:
+                    stored_pieces.add(k - 1)
+                    store(k - 1).wait()
+                hold(k + 1).start()
+            receive(0, k)
+            send(6, k, full(k, section, 2), full(k, section, 3), over_core)
+            which = 1 if k in direct else half
+            mine = full_half(k, section, 2, which)
+            send(2, k, mine, mine, over_y)
+            start_near(k + ahead)
+            receive(1, k)
+            if k in direct:
+                send(3, k, full_half(k, other, 0, 0), full_half(k, other, 2, 0), over_x)
+                send(7, k, full(k, other, 0), full(k, other, 1), over_core)
+            else:
+                crossed = full_half(k, other, 0, half)
+                send(3, k, crossed, crossed, over_z)
+                send(7, k, crossed, full_half(k, other, 1, half), over_core)
+            start_cross(k + ahead)
+        j = k - 1
+        if 0 <= j < count:
+            receive(2, j)
+            if j in direct:
+                send(8, j, full_half(j, other, 2, 1), full_half(j, other, 3, 1), over_core)
+                receive(3, j)
+                send(9, j, full_half(j, other, 2, 0), full_half(j, other, 3, 0), over_core)
+            else:
+                crossed = full_half(j, other, 2, half)
+                send(4, j, crossed, crossed, over_z)
+                send(8, j, crossed, full_half(j, other, 3, half), over_core)
+                receive(3, j)
+                passed = full_half(j, other, 0, 1 - half)
+                send(9, j, passed, full_half(j, other, 1, 1 - half), over_core)
+        j = k - 2
+        if 0 <= j < count and j not in direct:
+            receive(4, j)
+            passed = full_half(j, other, 2, 1 - half)
+            send(10, j, passed, full_half(j, other, 3, 1 - half), over_core)
+        for task in tasks.get(k, []):
+            task()
+    load_down(3)
+    add_down(2)
+    add_down(3)
+    result_ref[...] = (middle_ref[...] + acc_ref[...].T).astype(LOW)
+    make_keys(1, result_ref, next_kv_ref, 5)
+    make_queries(next_q_ref)
+    turned = jnp.dot(result_ref[...], natural_ref[...], preferred_element_type=jnp.float32)
+    natural_out_ref[...] = turned.astype(LOW)
+    for k in range(count):
+        need(k)
+    take_keys(1, next_kv_ref, next_kv_out, 5)
+    for copy in started.values():
+        copy.wait_send()
+    for name in ((1, 1), (2, 0), (2, 1), (4, 0), (5, 0)):
+        finish(name)
+    for t in range(FF // WIDE):
+        for name in (8, 9, 10):
+            finish((name, t))
+
+
+def first_layer(x_in, shards, seq_ids, angles, order, visible):
+    rows = x_in.shape[2]
+    quarter = shards[0].shape[0]
+    widths = [shards[0].shape[1], QD, FF, FF, FF]
+    pieces = 15
+    tiles, head_tiles = FF // TILE, QD // TILE
+    in_vmem = pl.BlockSpec(memory_space=pltpu.VMEM)
+    in_smem = pl.BlockSpec(memory_space=pltpu.SMEM)
+
+    def low(*shape):
+        return jax.ShapeDtypeStruct(shape, LOW)
+
+    def wide(*shape):
+        return jax.ShapeDtypeStruct(shape, jnp.float32)
+
+    dma = pltpu.SemaphoreType.DMA
+    outs = pl.pallas_call(
+        first_kernel,
+        out_shape=[low(2, 4 * quarter, w) for w in widths]
+        + [
+            low(rows, D),
+            low(QD, rows),
+            low(4, 2 * KV, HD, rows),
+            low(QD, rows),
+            wide(KV, GROUP, rows),
+            low(rows, D),
+            wide(rows, D),
+            low(2, 5, D, rows),
+            low(2, head_tiles, rows, TILE),
+            low(2, tiles, rows, TILE),
+            low(tiles, rows, TILE),
+            low(tiles, rows, TILE),
+            wide(*seq_ids.shape[1:]),
+            wide(2, 8, D),
+            low(QD, rows),
+            low(4, 2 * KV, HD, rows),
+            low(rows, D),
+            low(4, 16, rows),
+            low(16, rows),
+            jax.ShapeDtypeStruct((8,), jnp.int32),
+            low(D, D),
+        ],
+        in_specs=[ANYWHERE] * 5 + [in_vmem] * 3 + [in_smem] * 2,
+        out_specs=[ANYWHERE] * 5
+        + [in_vmem, in_vmem, ANYWHERE, in_vmem, in_vmem, in_vmem, in_vmem]
+        + [ANYWHERE] * 5
+        + [in_vmem, in_vmem, in_vmem, ANYWHERE, in_vmem, in_vmem, in_vmem, in_smem, in_vmem],
+        scratch_shapes=[
+            dma((12, pieces)),
+            dma((12, pieces)),
+            dma((pieces,)),
+            dma((3,)),
+            dma((40,)),
+            pltpu.VMEM((2, quarter, QD), LOW),
+            pltpu.VMEM((rows, D), LOW),
+            pltpu.VMEM((D, widths[0]), LOW),
+            pltpu.VMEM((D, QD), LOW),
+            pltpu.VMEM((2, 2, D, WIDE), LOW),
+            pltpu.VMEM((2, D, WIDE), LOW),
+            pltpu.VMEM((tiles, rows, TILE), LOW),
+            pltpu.VMEM((tiles, rows, TILE), LOW),
+            pltpu.VMEM((tiles, rows, TILE), LOW),
+            pltpu.VMEM((rows, D), LOW),
+            pltpu.VMEM((2, D, rows), LOW),
+            pltpu.VMEM((head_tiles, rows, TILE), LOW),
+            pltpu.VMEM((D, rows), jnp.float32),
+            pltpu.VMEM((4, 2 * KV, HD, rows), LOW),
+            pltpu.VMEM(seq_ids.shape[1:], jnp.float32),
+            pltpu.VMEM((4, 16, rows), LOW),
+            pltpu.VMEM((16, rows), LOW),
+            pltpu.VMEM((2, 8, D), jnp.float32),
+            pltpu.VMEM((4, 2 * KV, HD, rows), LOW),
+            pltpu.VMEM(seq_ids.shape[1:], jnp.float32),
+        ],
+        compiler_params=pltpu.CompilerParams(
+            collective_id=1, has_side_effects=True, vmem_limit_bytes=62 * 2**20
+        ),
+        cost_estimate=long_cost(230),
+    )(x_in, *shards, seq_ids, *angles, order, visible)
+    names = ("hidden", "q_t", "kv_t", "o_t", "lse", "result", "middle")
+    saved = dict(zip(names, outs[5:12]))
+    saved.update(gate=outs[15], up=outs[16])
+    stores = dict(lhs=outs[12], attended=outs[13], units=outs[14])
+    ahead = dict(hidden=outs[10], q_t=outs[19], kv_t=outs[20])
+    info = (outs[24], outs[22], outs[23])
+    return outs[:5], saved, ahead, stores, info, outs[18], outs[21], outs[25]
+
+
+ANYWHERE = pl.BlockSpec(memory_space=pl.ANY)
+WIDE = 768
+
+
+def whole(shape, *index):
+    return pl.BlockSpec(shape, lambda s: index + (0,) * (len(shape) - len(index)))
+
+
+def sigmoid_of(value):
+    return 0.5 * jnp.tanh(0.5 * value) + 0.5
+
+
+def norm_parts(value):
+    inverse = lax.rsqrt(jnp.mean(value * value, axis=-1, keepdims=True) + EPS)
+    return value * inverse, inverse
+
+
+def norm_back(grad_rows, value, gain_row):
+    unit_rows, inverse = norm_parts(value)
+    grad_unit = grad_rows * gain_row
+    grad_gain = jnp.sum(grad_rows * unit_rows, axis=0, keepdims=True)
+    inner = jnp.mean(grad_unit * unit_rows, axis=-1, keepdims=True)
+    return inverse * (grad_unit - unit_rows * inner), grad_gain
+
+
+def stored(stores, name, shape):
+    return stores.get(name), jax.ShapeDtypeStruct(shape, LOW)
+
+
+def copies_of(sem, pairs):
+    copies = [pltpu.make_async_copy(x, y, sem.at[i]) for i, (x, y) in enumerate(pairs)]
+    for copy in copies:
+        copy.start()
+    return copies
+
+
+def mlp_forward_kernel(
+    h_ref, o_ref, w_out_ref, w_gate_ref, w_up_ref, w_down_ref, gain_ref, *refs
+):
+    (
+        result_ref,
+        middle_ref,
+        normed_t_ref,
+        attended_ref,
+        units_ref,
+        gate_ref,
+        up_ref,
+        acc_ref,
+        normed_ref,
+    ) = refs[-9:]
+    step = pl.program_id(0)
+
+    @pl.when(step == 0)
+    def _():
+        attended = o_ref[...].T
+        for t in range(attended_ref.shape[1]):
+            attended_ref[0, t] = attended[:, t * TILE : (t + 1) * TILE]
+        added = jnp.dot(w_out_ref[0], o_ref[...], preferred_element_type=jnp.float32)
+        middle = h_ref[...].astype(jnp.float32) + added.T
+        middle_ref[...] = middle
+        acc_ref[...] = jnp.zeros_like(acc_ref)
+        unit_rows, unused = norm_parts(middle)
+        normed = (unit_rows * gain_ref[0, 1:2]).astype(LOW)
+        normed_ref[...] = normed
+        normed_t_ref[0, 0] = normed.T
+
+    @pl.when(step > 0)
+    def _():
+        normed = normed_ref[...]
+        gate = jnp.dot(normed, w_gate_ref[0], preferred_element_type=jnp.float32)
+        up = jnp.dot(normed, w_up_ref[0], preferred_element_type=jnp.float32)
+        units = (gate * sigmoid_of(gate) * up).astype(LOW)
+        gate_low, up_low = gate.astype(LOW), up.astype(LOW)
+        for t in range(WIDE // TILE):
+            cut = slice(t * TILE, (t + 1) * TILE)
+            gate_ref[t] = gate_low[:, cut]
+            up_ref[t] = up_low[:, cut]
+            units_ref[0, t] = units[:, cut]
+        acc_ref[...] += jnp.dot(w_down_ref[0], units.T, preferred_element_type=jnp.float32)
+
+    @pl.when(step == pl.num_programs(0) - 1)
+    def _():
+        result_ref[...] = (middle_ref[...] + acc_ref[...].T).astype(LOW)
+
+
+def call_mlp_forward(layer, hidden, o_t, weights, gain_rows, stores):
+    w_in, w_out_t, w_gate, w_up, w_down_t = weights
+    rows = hidden.shape[0]
+    steps, per = FF // WIDE, WIDE // TILE
+    tiles, head_tiles = FF // TILE, QD // TILE
+    names = ("lhs", "attended", "units")
+    shapes = ((2, 5, D, rows), (2, head_tiles, rows, TILE), (2, tiles, rows, TILE))
+    extra, aliases, store_shapes = [], {}, []
+    for place, (name, shape) in enumerate(zip(names, shapes)):
+        value, shape = stored(stores, name, shape)
+        store_shapes.append(shape)
+        if value is not None:
+            aliases[7 + len(extra)] = 2 + place
+            extra.append(value)
+
+    def behind(s):
+        return jnp.maximum(s - 1, 0)
+
+    column = pl.BlockSpec((1, D, WIDE), lambda s: (layer, 0, behind(s)))
+    kept = pl.BlockSpec((per, rows, TILE), lambda s: (behind(s), 0, 0))
+    result, middle, lhs, attended, units, gate, up = pl.pallas_call(
+        mlp_forward_kernel,
+        grid=(steps + 1,),
+        in_specs=[
+            whole((rows, D)),
+            whole((QD, rows)),
+            whole((1, D, QD), layer),
+            column,
+            column,
+            column,
+            whole((1, 8, D), layer),
+        ]
+        + [ANYWHERE] * len(extra),
+        out_specs=[
+            whole((rows, D)),
+            whole((rows, D)),
+            whole((1, 1, D, rows), layer, 2),
+            whole((1, head_tiles, rows, TILE), layer),
+            pl.BlockSpec((1, per, rows, TILE), lambda s: (layer, behind(s), 0, 0)),
+            kept,
+            kept,
+        ],
+        out_shape=[
+            jax.ShapeDtypeStruct((rows, D), LOW),
+            jax.ShapeDtypeStruct((rows, D), jnp.float32),
+            *store_shapes,
+            jax.ShapeDtypeStruct((tiles, rows, TILE), LOW),
+            jax.ShapeDtypeStruct((tiles, rows, TILE), LOW),
+        ],
+        scratch_shapes=[pltpu.VMEM((D, rows), jnp.float32), pltpu.VMEM((rows, D), LOW)],
+        input_output_aliases=aliases,
+        compiler_params=pltpu.CompilerParams(vmem_limit_bytes=62 * 2**20),
+        cost_estimate=long_cost(25),
+    )(hidden, o_t, w_out_t, w_gate, w_up, w_down_t, gain_rows, *extra)
+    stores.update(lhs=lhs, attended=attended, units=units)
+    return result, middle, gate, up
+
+
+def pair_forward(layer, saved, weights, gain_rows, info, stores):
+    o_t, lse = pair_attention_forward(info, saved["q_t"], saved["kv_t"])
+    result, middle, gate, up = call_mlp_forward(
+        layer, saved["hidden"], o_t, weights, gain_rows, stores
+    )
+    return dict(saved, o_t=o_t, lse=lse, middle=middle, gate=gate, up=up, result=result)
+
+
+def mlp_backward_kernel(
+    layer,
+    grad_ref,
+    gate_ref,
+    up_ref,
+    w_gate_ref,
+    w_up_ref,
+    w_down_ref,
+    middle_ref,
+    gain_ref,
+    w_out_ref,
+    *refs,
+):
+    (
+        mlp_ref,
+        pair_ref,
+        grad_middle_ref,
+        do_ref,
+        gain_grad_ref,
+        acc_ref,
+        late_middle,
+        late_out,
+        late_sem,
+    ) = refs[-9:]
+    step = pl.program_id(0)
+    per = gate_ref.shape[0]
+    late = [
+        pltpu.make_async_copy(middle_ref, late_middle, late_sem.at[0]),
+        pltpu.make_async_copy(w_out_ref.at[layer], late_out, late_sem.at[1]),
+    ]
+
+    @pl.when(step == 0)
+    def _():
+        for copy in late:
+            copy.start()
+
+    gate = jnp.concatenate([gate_ref[t] for t in range(per)], axis=1).astype(jnp.float32)
+    up = jnp.concatenate([up_ref[t] for t in range(per)], axis=1).astype(jnp.float32)
+    grad_units = jnp.dot(grad_ref[...], w_down_ref[0], preferred_element_type=jnp.float32)
+    sigmoid = sigmoid_of(gate)
+    slope = grad_units * sigmoid
+    tilted = slope * gate
+    grad_gate = (up * (slope + tilted * (1.0 - sigmoid))).astype(LOW)
+    grad_up = tilted.astype(LOW)
+    for t in range(per):
+        cut = slice(t * TILE, (t + 1) * TILE)
+        mlp_ref[0, 2 * t] = grad_gate[:, cut]
+        mlp_ref[0, 2 * t + 1] = grad_up[:, cut]
+    part = jnp.dot(w_gate_ref[0], grad_gate.T, preferred_element_type=jnp.float32)
+    part = part + jnp.dot(w_up_ref[0], grad_up.T, preferred_element_type=jnp.float32)
+
+    @pl.when(step == 0)
+    def _():
+        acc_ref[...] = part
+        pair_ref[0, 0] = grad_ref[...].T
+
+    @pl.when(step > 0)
+    def _():
+        acc_ref[...] += part
+
+    @pl.when(step == pl.num_programs(0) - 1)
+    def _():
+        for copy in late:
+            copy.wait()
+        grad_norm, grad_gain = norm_back(acc_ref[...].T, late_middle[...], gain_ref[0, 1:2])
+        gain_grad_ref[...] = jnp.broadcast_to(grad_gain, gain_grad_ref.shape)
+        grad_middle = grad_ref[...].astype(jnp.float32) + grad_norm
+        grad_middle_ref[...] = grad_middle
+        grad_branch = grad_middle.astype(LOW)
+        pair_ref[0, 1] = grad_branch.T
+        grad_attended = jnp.dot(grad_branch, late_out[...], preferred_element_type=jnp.float32)
+        do_ref[...] = grad_attended.astype(LOW).T
+
+
+def call_mlp_backward(layer, grad_low, saved, weights, gain_rows, stores):
+    w_in, w_out_t, w_gate, w_up, w_down_t = weights
+    rows = grad_low.shape[0]
+    steps, per = FF // WIDE, WIDE // TILE
+    mlp, mlp_shape = stored(stores, "mlp", (2, 2 * FF // TILE, rows, TILE))
+    extra = [stores["lhs"]] if mlp is None else [stores["lhs"], mlp]
+    aliases = {9: 1} if mlp is None else {9: 1, 10: 0}
+    column = pl.BlockSpec((1, D, WIDE), lambda s: (layer, 0, s))
+    kept = pl.BlockSpec((per, rows, TILE), lambda s: (s, 0, 0))
+    mlp, lhs, grad_middle, do_t, grad_gain = pl.pallas_call(
+        functools.partial(mlp_backward_kernel, layer),
+        grid=(steps,),
+        in_specs=[
+            whole((rows, D)),
+            kept,
+            kept,
+            column,
+            column,
+            column,
+            ANYWHERE,
+            whole((1, 8, D), layer),
+            ANYWHERE,
+        ]
+        + [ANYWHERE] * len(extra),
+        out_specs=[
+            pl.BlockSpec((1, 2 * per, rows, TILE), lambda s: (layer, s, 0, 0)),
+            whole((1, 2, D, rows), layer),
+            whole((rows, D)),
+            whole((QD, rows)),
+            whole((8, D)),
+        ],
+        out_shape=[
+            mlp_shape,
+            jax.ShapeDtypeStruct(stores["lhs"].shape, LOW),
+            jax.ShapeDtypeStruct((rows, D), jnp.float32),
+            jax.ShapeDtypeStruct((QD, rows), LOW),
+            jax.ShapeDtypeStruct((8, D), jnp.float32),
+        ],
+        scratch_shapes=[
+            pltpu.VMEM((D, rows), jnp.float32),
+            pltpu.VMEM((rows, D), jnp.float32),
+            pltpu.VMEM((D, QD), LOW),
+            pltpu.SemaphoreType.DMA((2,)),
+        ],
+        input_output_aliases=aliases,
+        compiler_params=pltpu.CompilerParams(vmem_limit_bytes=62 * 2**20),
+        cost_estimate=long_cost(25),
+    )(
+        grad_low,
+        saved["gate"],
+        saved["up"],
+        w_gate,
+        w_up,
+        w_down_t,
+        saved["middle"],
+        gain_rows,
+        w_out_t,
+        *extra,
+    )
+    stores.update(lhs=lhs, mlp=mlp)
+    return grad_middle, do_t, grad_gain
+
+
+def mixed_backward_kernel(
+    layer,
+    dk_ref,
+    dv_ref,
+    gain_ref,
+    gain_grad_ref,
+    cos_ref,
+    sin_ref,
+    dq_all,
+    h_all,
+    grad_middle_all,
+    natural_all,
+    w_all,
+    *refs,
+):
+    if layer == 0:
+        outs = len(refs) - 27
+        ahead = (refs[outs - 1], refs[outs + 4], *refs[-7:])
+        refs = refs[: outs + 4] + refs[outs + 5 : -7]
+    (
+        mixed_out,
+        lhs_out,
+        result_ref,
+        natural_out_ref,
+        w_ref,
+        acc_ref,
+        tile_ref,
+        gains_ref,
+        near_ref,
+        far_ref,
+        passed_ref,
+        dq_ref,
+        h_ref,
+        grad_middle_ref,
+        natural_ref,
+        send_sem,
+        recv_sem,
+        local_sem,
+        load_sem,
+    ) = refs[-19:]
+    section = lax.axis_index(SECTION)
+    column = lax.axis_index(CTX)
+    place = lax.axis_index(WSH)
+    over_z = (section, column + 1 - 2 * lax.rem(column, 2), place)
+    over_core = (section, column, place + 1 - 2 * lax.rem(place, 2))
+    rows = result_ref.shape[0]
+    steps = QKV // TILE
+    barrier = pltpu.get_barrier_semaphore()
+    over_y = (1 - section, column, place)
+    targets = (over_z, over_core, over_y) if layer == 0 else (over_z, over_core)
+    for target in targets:
+        pl.semaphore_signal(barrier, inc=1, device_id=target, device_id_type=MESH_ID)
+    pl.semaphore_wait(barrier, len(targets))
+
+    def remote(index, source, target, device):
+        copy = pltpu.make_async_remote_copy(
+            src_ref=source,
+            dst_ref=target,
+            send_sem=send_sem.at[index],
+            recv_sem=recv_sem.at[index],
+            device_id=device,
+            device_id_type=MESH_ID,
+        )
+        copy.start()
+        return copy
+
+    crossed = [
+        remote(2 * slot + part, source.at[2 * slot + 1], near_ref.at[slot, part], over_core)
+        for slot in (1, 0)
+        for part, source in enumerate((dk_ref, dv_ref))
+    ]
+    loads = copies_of(
+        load_sem,
+        [
+            (w_all.at[layer], w_ref),
+            (dq_all, dq_ref),
+            (h_all, h_ref),
+            (grad_middle_all, grad_middle_ref),
+            (natural_all, natural_ref),
+        ],
+    )
+    for copy in crossed[:2]:
+        copy.wait_recv()
+    for part, source in enumerate((dk_ref, dv_ref)):
+        both = source[2].astype(jnp.float32) + near_ref[1, part].astype(jnp.float32)
+        far_ref[part] = both.astype(LOW)
+    passed = [remote(4 + part, far_ref.at[part], passed_ref.at[part], over_z) for part in range(2)]
+    if layer == 0:
+        finish = first_crossed(refs[0], ahead, section, place, over_core, over_y)
+    for copy in loads:
+        copy.wait()
+
+    def add(t, grad_t):
+        grad_t = grad_t.astype(LOW)
+        tile_ref[t] = grad_t.T
+        part = jnp.dot(
+            w_ref[:, pl.ds(t * TILE, TILE)], grad_t, preferred_element_type=jnp.float32
+        )
+        if t == 0:
+            acc_ref[...] = part
+        else:
+            acc_ref[...] += part
+
+    def back(heads):
+        return turn(heads, cos_ref[...], -sin_ref[...]).reshape(KD, rows)
+
+    for t in range(QD // KD):
+        add(t, back(dq_ref[pl.ds(t * KD, KD), :].reshape(KV, HD, rows)))
+    row = lax.broadcasted_iota(jnp.int32, (rows, TILE), 0)
+    lane = lax.broadcasted_iota(jnp.int32, (rows, TILE), 1)
+    tile_ref[steps] = jnp.where(row == lane, 1.0, 0.0).astype(LOW)
+    for copy in crossed[2:]:
+        copy.wait_recv()
+    for part, source in enumerate((dk_ref, dv_ref)):
+        passed[part].wait_recv()
+        own = source[0].astype(jnp.float32) + near_ref[0, part].astype(jnp.float32)
+        own = own + passed_ref[part].astype(jnp.float32)
+        add(QD // KD + part, back(own) if part == 0 else own.reshape(KD, rows))
+    tiles = pltpu.make_async_copy(tile_ref, mixed_out.at[layer], local_sem.at[1])
+    tiles.start()
+    grad_norm, grad_gain = norm_back(
+        acc_ref[...].T, h_ref[...].astype(jnp.float32), gain_ref[layer, :1]
+    )
+    both = jnp.concatenate(
+        [grad_gain, gain_grad_ref[:1], jnp.zeros((rows - 2, D), jnp.float32)], axis=0
+    )
+    gains_ref[...] = both.T.astype(LOW)
+    gains = pltpu.make_async_copy(gains_ref, lhs_out.at[layer, 4], local_sem.at[2])
+    gains.start()
+    result = (grad_middle_ref[...] + grad_norm).astype(LOW)
+    result_ref[...] = result
+    turned = jnp.dot(result, natural_ref[...], preferred_element_type=jnp.float32)
+    natural_out_ref[...] = turned.astype(LOW)
+    for copy in crossed + passed:
+        copy.wait_send()
+    tiles.wait()
+    gains.wait()
+    if layer == 0:
+        finish()
+
+
+def first_crossed(lhs_all, ahead, section, place, over_core, over_y):
+    mlp_all, given_out, lhs_ref, rhs_ref, given_ref, local_sem, near_sem, peer_sem, far_sem = ahead
+    other = 1 - section
+    core = lax.rem(place, 2)
+    tokens = lhs_all.shape[3]
+    piece = lhs_all.shape[2] // 8
+
+    def remote(send_sem, recv_sem, source, target, device):
+        copy = pltpu.make_async_remote_copy(
+            src_ref=source,
+            dst_ref=target,
+            send_sem=send_sem,
+            recv_sem=recv_sem,
+            device_id=device,
+            device_id_type=MESH_ID,
+        )
+        copy.start()
+        return copy
+
+    pairs, peers = [], []
+    for p in range(4):
+        mine = lhs_all.at[other, 2, pl.ds((2 * p + core) * piece, piece), :]
+        theirs = lhs_all.at[other, 2, pl.ds((2 * p + 1 - core) * piece, piece), :]
+        pairs.append((mine, lhs_ref.at[pl.ds(p * piece, piece), pl.ds(0, tokens)]))
+        target = lhs_ref.at[pl.ds((p ^ 1) * piece, piece), pl.ds(tokens, tokens)]
+        peers.append(remote(near_sem.at[p], peer_sem.at[p], theirs, target, over_core))
+    for t in range(2):
+        pairs.append((mlp_all.at[other, t], rhs_ref.at[t, pl.ds(0, tokens)]))
+        target = rhs_ref.at[t, pl.ds(tokens, tokens)]
+        sems = (near_sem.at[4 + t], peer_sem.at[4 + t])
+        peers.append(remote(*sems, mlp_all.at[other, t], target, over_core))
+    copies = copies_of(local_sem, pairs)
+    for copy in copies:
+        copy.wait()
+    for copy in peers:
+        copy.wait_recv()
+    sent = []
+    for t in range(2):
+        value = jnp.dot(lhs_ref[...], rhs_ref[t], preferred_element_type=jnp.float32)
+        given_ref[t] = value.astype(LOW)
+        sems = (far_sem.at[0, t], far_sem.at[1, t])
+        sent.append(remote(*sems, given_ref.at[t], given_out.at[t], over_y))
+
+    def finish():
+        for copy in peers:
+            copy.wait_send()
+        for copy in sent:
+            copy.wait()
+
+    return finish
+
+
+def call_mixed_backward(
+    layer, dq_t, dk_t, dv_t, hidden, grad_middle, grad_gain, shared, angles, stores
+):
+    weights, gain_rows, natural = shared
+    rows = hidden.shape[0]
+    steps = QKV // TILE + 1
+    mixed, mixed_shape = stored(stores, "mixed", (2, steps, rows, TILE))
+    extra = [stores["lhs"]] if mixed is None else [stores["lhs"], mixed]
+    aliases = {11: 1} if mixed is None else {11: 1, 12: 0}
+    ahead = [stores["mlp"]] if layer == 0 else []
+    half = D // 2
+    ahead_shape = [jax.ShapeDtypeStruct((2, half, TILE), LOW)] if layer == 0 else []
+    ahead_scratch = [
+        pltpu.VMEM((half, 2 * rows), LOW),
+        pltpu.VMEM((2, 2 * rows, TILE), LOW),
+        pltpu.VMEM((2, half, TILE), LOW),
+        pltpu.SemaphoreType.DMA((6,)),
+        pltpu.SemaphoreType.DMA((6,)),
+        pltpu.SemaphoreType.DMA((6,)),
+        pltpu.SemaphoreType.DMA((2, 2)),
+    ]
+    in_vmem = pl.BlockSpec(memory_space=pltpu.VMEM)
+    dma = pltpu.SemaphoreType.DMA
+    part = (2, KV, HD, rows)
+    mixed, lhs, result, turned, *given = pl.pallas_call(
+        functools.partial(mixed_backward_kernel, layer),
+        in_specs=[in_vmem] * 6 + [ANYWHERE] * (5 + len(extra) + len(ahead)),
+        out_specs=[ANYWHERE, ANYWHERE, in_vmem, in_vmem] + [ANYWHERE] * len(ahead),
+        out_shape=[
+            mixed_shape,
+            jax.ShapeDtypeStruct(stores["lhs"].shape, LOW),
+            jax.ShapeDtypeStruct((rows, D), LOW),
+            jax.ShapeDtypeStruct((rows, D), LOW),
+            *ahead_shape,
+        ],
+        scratch_shapes=[
+            pltpu.VMEM((D, weights[0].shape[2]), LOW),
+            pltpu.VMEM((D, rows), jnp.float32),
+            pltpu.VMEM((steps, rows, TILE), LOW),
+            pltpu.VMEM((D, rows), LOW),
+            pltpu.VMEM((2, *part), LOW),
+            pltpu.VMEM(part, LOW),
+            pltpu.VMEM(part, LOW),
+            pltpu.VMEM((QD, rows), jnp.float32),
+            pltpu.VMEM((rows, D), LOW),
+            pltpu.VMEM((rows, D), jnp.float32),
+            pltpu.VMEM((D, D), LOW),
+            dma((6,)),
+            dma((6,)),
+            dma((3,)),
+            dma((5,)),
+        ]
+        + ahead_scratch * len(ahead),
+        input_output_aliases=aliases,
+        compiler_params=pltpu.CompilerParams(
+            collective_id=4 + layer, has_side_effects=True, vmem_limit_bytes=62 * 2**20
+        ),
+        cost_estimate=long_cost(30),
+    )(
+        dk_t,
+        dv_t,
+        gain_rows,
+        grad_gain,
+        *angles,
+        dq_t,
+        hidden,
+        grad_middle,
+        natural,
+        weights[0],
+        *extra,
+        *ahead,
+    )
+    stores.update(lhs=lhs, mixed=mixed)
+    if given:
+        stores["given"] = given[0]
+    return result, turned
+
+
+def pair_backward(layer, grad_low, shared, saved, info, angles, stores, beside):
+    grad_middle, do_t, grad_gain = call_mlp_backward(
+        layer, grad_low, saved, shared[0], shared[1], stores
+    )
+    dq_t, dk_t, dv_t = pair_attention_backward(
+        info, saved["q_t"], do_t, saved["o_t"], saved["lse"], saved["kv_t"]
+    )
+    dq_t, beside = lax.optimization_barrier((dq_t, beside))
+    result, turned = call_mixed_backward(
+        layer, dq_t, dk_t, dv_t, saved["hidden"], grad_middle, grad_gain, shared, angles, stores
+    )
+    return result, turned, beside
+
+
+TILE = 384
+CROSSED = 22
+PLANE = 11
+
+
+def spread_kernel(
+    lhs_all,
+    mlp_all,
+    mixed_all,
+    units_all,
+    attended_all,
+    grad_ref,
+    given_all,
+    in_out,
+    head_out,
+    mlp_out,
+    down_out,
+    gains_out,
+    grad_out,
+    mlp_peer,
+    mixed_peer,
+    units_peer,
+    attended_peer,
+    lhs_ref,
+    rhs_ref,
+    given_ref,
+    sum_ref,
+    side_ref,
+    block_ref,
+    last_given,
+    last_ref,
+    hold_ref,
+    kept_ref,
+    grad_sem,
+    early_sem,
+    lhs_sem,
+    peer_send,
+    peer_recv,
+    load_sem,
+    given_send,
+    given_recv,
+    side_send,
+    side_recv,
+    block_send,
+    block_recv,
+    last_send,
+    last_recv,
+):
+    section = lax.axis_index(SECTION)
+    column = lax.axis_index(CTX)
+    place = lax.axis_index(WSH)
+    other = 1 - section
+    over_x = (section, column, lax.rem(place + 2, 4))
+    over_y = (other, column, place)
+    over_core = (section, column, place + 1 - 2 * lax.rem(place, 2))
+    flip_low = column + 1 - 2 * lax.rem(column, 2)
+    flip_high = lax.rem(column + 2, 4)
+    flip_both = lax.rem(flip_low + 2, 4)
+    over_z = [(section, c, place) for c in (flip_low, flip_high, flip_both)]
+    origin = place ^ column
+
+    barrier = pltpu.get_barrier_semaphore()
+    for target in (over_x, over_y, over_core, *over_z):
+        pl.semaphore_signal(barrier, inc=1, device_id=target, device_id_type=MESH_ID)
+    moving, partner_column, partner_place = stream_partner(column, place)
+    staying = jnp.logical_not(moving)
+
+    @pl.when(moving)
+    def _():
+        for target in (section, other):
+            pl.semaphore_signal(
+                barrier,
+                inc=1,
+                device_id=(target, partner_column, partner_place),
+                device_id_type=MESH_ID,
+            )
+        pl.semaphore_wait(barrier, 8)
+
+    @pl.when(staying)
+    def _():
+        pl.semaphore_wait(barrier, 6)
+
+    half = lhs_all.shape[2] // 2
+    tokens = lhs_all.shape[3]
+    quarter = half // 2
+    share = quarter // 4
+    layers = (section, other)
+
+    def remote(source, target, send_sem, recv_sem, device):
+        return pltpu.make_async_remote_copy(
+            src_ref=source,
+            dst_ref=target,
+            send_sem=send_sem,
+            recv_sem=recv_sem,
+            device_id=device,
+            device_id_type=MESH_ID,
+        )
+
+    core = lax.rem(place, 2)
+    side = place // 2
+    piece = half // 4
+
+    def grad_copy(slot, device):
+        return remote(
+            grad_ref, grad_out.at[slot], grad_sem.at[0], grad_sem.at[1 + slot], device
+        )
+
+    hold_in = pltpu.make_async_copy(grad_ref, hold_ref, grad_sem.at[3])
+    hold_out = pltpu.make_async_copy(hold_ref, grad_out.at[0], grad_sem.at[3])
+
+    def grad_start():
+        @pl.when(moving & (section == 0))
+        def _():
+            grad_copy(0, (0, partner_column, partner_place)).start()
+
+        @pl.when(staying & (section == 0))
+        def _():
+            hold_in.start()
+            hold_in.wait()
+            hold_out.start()
+
+    def grad_cross():
+        @pl.when(moving & (section == 1))
+        def _():
+            grad_copy(1, (0, partner_column, partner_place)).start()
+
+        @pl.when(staying & (section == 1))
+        def _():
+            grad_copy(1, over_y).start()
+
+    def grad_finish():
+        @pl.when(section == 0)
+        def _():
+            grad_copy(1, over_y).wait_recv()
+
+        @pl.when(moving & (section == 0))
+        def _():
+            grad_copy(0, over_y).wait_recv()
+
+        @pl.when(moving | (section == 1))
+        def _():
+            grad_copy(0, over_y).wait_send()
+
+        @pl.when(staying & (section == 0))
+        def _():
+            hold_out.wait()
+
+    def lhs_copies(group):
+        kinds = (pl.ds(2, 1), pl.ds(0, 1), pl.ds(1, 1), pl.ds(3, 2))[group]
+        copies = []
+        for which in (1, 0):
+            for p in range(4):
+                index = which * 4 + p
+                copies.append(
+                    pltpu.make_async_copy(
+                        lhs_all.at[layers[which], kinds, pl.ds((2 * p + core) * piece, piece), :],
+                        lhs_ref.at[which, kinds, pl.ds(p * piece, piece), pl.ds(0, tokens)],
+                        lhs_sem.at[group, 0, index],
+                    )
+                )
+                span = pl.ds((2 * p + 1 - core) * piece, piece)
+                copies.append(
+                    remote(
+                        lhs_all.at[layers[which], kinds, span, :],
+                        lhs_ref.at[
+                            which, kinds, pl.ds((p ^ 1) * piece, piece), pl.ds(tokens, tokens)
+                        ],
+                        lhs_sem.at[group, 1, index],
+                        lhs_sem.at[group, 2, index],
+                        over_core,
+                    )
+                )
+        return copies
+
+    sources = (
+        (mlp_all, mlp_peer, lambda tile: tile),
+        (mixed_all, mixed_peer, lambda tile: tile - 16),
+        (units_all, units_peer, lambda tile: tile - CROSSED),
+        (attended_all, attended_peer, lambda tile: tile - CROSSED - 8),
+    )
+
+    def peer_copy(which, tile, source):
+        mine, theirs, place_of = sources[source]
+        return remote(
+            mine.at[layers[which], place_of(tile)],
+            theirs.at[layers[which], place_of(tile)],
+            peer_send.at[which, tile],
+            peer_recv.at[which, tile],
+            over_core,
+        )
+
+    def peer_wait(which, tile):
+        return remote(
+            mlp_all.at[layers[which], 0],
+            mlp_peer.at[layers[which], 0],
+            peer_send.at[which, tile],
+            peer_recv.at[which, tile],
+            over_core,
+        )
+
+    def peer_starts(crossed, which, i):
+        for early in (True, False):
+
+            @pl.when(((i < 8) == early) & (i < PLANE))
+            def _():
+                late = 1 - early
+                if crossed:
+                    peer_copy(which, 2 * i, late).start()
+                    peer_copy(which, 2 * i + 1, late).start()
+                else:
+                    peer_copy(1, CROSSED + i, 2 + late).start()
+                    peer_copy(0, CROSSED + i, 2 + late).start()
+
+    def loads(slot, which, tile, source):
+        mine, theirs, place_of = sources[source]
+        return (
+            pltpu.make_async_copy(
+                mine.at[layers[which], place_of(tile)],
+                rhs_ref.at[slot, pl.ds(0, tokens)],
+                load_sem.at[slot, 0],
+            ),
+            pltpu.make_async_copy(
+                theirs.at[layers[which], place_of(tile)],
+                rhs_ref.at[slot, pl.ds(tokens, tokens)],
+                load_sem.at[slot, 1],
+            ),
+        )
+
+    def load_start(slot, which, tile, source, early):
+        peer_wait(which, tile).wait_recv()
+        for flag in (True, False):
+
+            @pl.when(early == flag)
+            def _():
+                for copy in loads(slot, which, tile, source + 1 - flag):
+                    copy.start()
+
+    def product(slot, which, tile, kind):
+        for copy in loads(slot, which, 0, 0):
+            copy.wait()
+        return jnp.dot(
+            lhs_ref[which, kind], rhs_ref[slot], preferred_element_type=jnp.float32
+        )
+
+    def crossed_kind(tile):
+        return jnp.where(tile < 16, 2, jnp.where(tile < 21, 3, 4))
+
+    def plane_kind(i):
+        return jnp.where(i < 8, 0, 1)
+
+    def sorted_sides(value):
+        blocks = value.reshape(4, 2, share, TILE)
+        first, second = blocks[:, 0], blocks[:, 1]
+        low = jnp.broadcast_to(side == 0, first.shape)
+        away = jnp.where(low, second, first).reshape(quarter, TILE)
+        kept = jnp.where(low, first, second).reshape(quarter, TILE)
+        return jnp.concatenate([away, kept], axis=0).astype(LOW)
+
+    def given_copy(tile):
+        slot = lax.rem(tile, 4)
+        return remote(
+            given_ref.at[slot],
+            sum_ref.at[tile],
+            given_send.at[slot],
+            given_recv.at[tile],
+            over_y,
+        )
+
+    def side_copy(unit):
+        return remote(
+            sum_ref.at[unit, pl.ds(0, quarter)],
+            side_ref.at[unit // 2, pl.ds(lax.rem(unit, 2) * quarter, quarter)],
+            side_send.at[unit],
+            side_recv.at[unit],
+            over_x,
+        )
+
+    def block_span(k):
+        return pl.ds(pl.multiple_of((origin ^ k) * 2 * share, 2 * share), 2 * share)
+
+    def block_copy(pair, k):
+        return remote(
+            side_ref.at[pair, block_span(k + 1)],
+            block_ref.at[pair, k],
+            block_send.at[pair, k],
+            block_recv.at[pair, k],
+            over_z[1 if k == 1 else 0],
+        )
+
+    def last_copy(i):
+        return remote(
+            last_given.at[i], last_ref.at[i], last_send.at[i], last_recv.at[i], over_y
+        )
+
+    def combine(pair):
+        parts = []
+        for e in range(2):
+            unit = 2 * pair + e
+            side_copy(unit).wait_recv()
+            kept = sum_ref[unit, pl.ds(quarter, quarter)].astype(jnp.float32)
+            got = side_ref[pair, pl.ds(e * quarter, quarter)].astype(jnp.float32)
+            got = jnp.concatenate([got[quarter // 2 :], got[: quarter // 2]], axis=0)
+            parts.append((kept + got).reshape(4, share, TILE))
+        both = jnp.concatenate(parts, axis=1).reshape(8 * share, TILE)
+        side_ref[pair] = both.astype(LOW)
+        block_copy(pair, 2).start()
+        block_copy(pair, 0).start()
+
+    def relay(pair):
+        for k, block in ((2, 2), (0, 0)):
+            block_copy(pair, k).wait_recv()
+            span = block_span(block)
+            total = side_ref[pair, span].astype(jnp.float32)
+            total = total + block_ref[pair, k].astype(jnp.float32)
+            side_ref[pair, span] = total.astype(LOW)
+            if k == 2:
+                block_copy(pair, 1).start()
+
+    def settle(pair):
+        block_copy(pair, 1).wait_recv()
+        total = side_ref[pair, block_span(0)].astype(jnp.float32)
+        total = total + block_ref[pair, 1].astype(jnp.float32)
+        return total[:share], total[share:]
+
+    early_copies = copies_of(early_sem, [(given_all.at[t], sum_ref.at[t]) for t in range(2)])
+    for copy in lhs_copies(0):
+        copy.start()
+    peer_starts(True, 1, 1)
+    peer_starts(False, 0, 0)
+    peer_starts(True, 0, 0)
+    for group in (1, 2, 3):
+        for copy in lhs_copies(group):
+            copy.start()
+    grad_start()
+    for copy in lhs_copies(0):
+        copy.wait()
+    for copy in early_copies:
+        copy.wait()
+
+    def within(i, low=0):
+        return (i >= low) & (i < low + PLANE)
+
+    def step(i, carry):
+        peer_starts(True, 1, i + 2)
+        peer_starts(False, 0, i + 1)
+        peer_starts(True, 0, i + 1)
+
+        for group, when in ((1, 0), (2, 6), (3, 6)):
+
+            @pl.when(i == when)
+            def _():
+                for copy in lhs_copies(group):
+                    copy.wait()
+
+        @pl.when(i + 1 < PLANE)
+        def _():
+            j = i + 1
+            load_start(0, 1, 2 * j, 0, j < 8)
+            load_start(1, 1, 2 * j + 1, 0, j < 8)
+            for e in range(2):
+                tile = 2 * j + e
+                value = product(e, 1, tile, crossed_kind(tile))
+
+                @pl.when(j >= 3)
+                def _():
+                    given_copy(tile - 4).wait_send()
+
+                given_ref[lax.rem(tile, 4)] = value.astype(LOW)
+                given_copy(tile).start()
+
+        @pl.when(i < PLANE)
+        def _():
+            load_start(2, 1, CROSSED + i, 2, i < 8)
+            load_start(0, 0, CROSSED + i, 2, i < 8)
+            for e in range(2):
+                unit = CROSSED + 2 * i + e
+                value = product(2 - 2 * e, 1 - e, CROSSED + i, plane_kind(i))
+                sum_ref[unit] = sorted_sides(value)
+                side_copy(unit).start()
+
+        @pl.when(within(i, 1))
+        def _():
+            combine(PLANE + i - 1)
+
+        @pl.when(i < PLANE)
+        def _():
+            load_start(1, 0, 2 * i, 0, i < 8)
+            load_start(2, 0, 2 * i + 1, 0, i < 8)
+            for e in range(2):
+                tile = 2 * i + e
+                value = product(1 + e, 0, tile, crossed_kind(tile))
+
+                @pl.when(i > 0)
+                def _():
+                    given_copy(tile).wait_recv()
+
+                sum_ref[tile] = sorted_sides(value + sum_ref[tile].astype(jnp.float32))
+                side_copy(tile).start()
+
+        @pl.when(i == PLANE - 1)
+        def _():
+            grad_cross()
+
+        @pl.when(within(i, 2))
+        def _():
+            j = i - 2
+            given, kept = settle(PLANE + j)
+            kept_ref[j] = kept
+            last_given[j] = jnp.concatenate(
+                [given, jnp.zeros((last_given.shape[1] - share, TILE), jnp.float32)], axis=0
+            ).astype(LOW)
+            last_copy(j).start()
+
+        @pl.when(within(i, 1))
+        def _():
+            combine(i - 1)
+            relay(PLANE + i - 1)
+            relay(i - 1)
+
+        @pl.when(within(i, 2))
+        def _():
+            j = i - 2
+            tiles = settle(j)
+
+            def columns(base):
+                return pl.ds(pl.multiple_of(base * TILE, TILE), TILE)
+
+            @pl.when(j < 8)
+            def _():
+                for e in range(2):
+                    mlp_out[:, columns(8 * e + j)] = tiles[e]
+
+            @pl.when(j >= 8)
+            def _():
+                in_out[:, columns(2 * (j - 8))] = tiles[0]
+
+            @pl.when((j >= 8) & (j < 10))
+            def _():
+                in_out[:, columns(2 * (j - 8) + 1)] = tiles[1]
+
+            @pl.when(j == 10)
+            def _():
+                gains_out[...] = tiles[1][:, :SIDE].T[:8]
+
+        @pl.when(within(i, 3))
+        def _():
+            j = i - 3
+
+            def columns(base):
+                return pl.ds(pl.multiple_of(base * TILE, TILE), TILE)
+
+            last_copy(j).wait_recv()
+            total = (kept_ref[j] + last_ref[j].astype(jnp.float32)[:share]).T
+
+            @pl.when(j < 8)
+            def _():
+                down_out[columns(j), :] = total
+
+            @pl.when(j >= 8)
+            def _():
+                head_out[columns(j - 8), :] = total
+
+        return carry
+
+    lax.fori_loop(0, PLANE + 3, step, 0)
+
+    def drain(i, carry):
+        for e in range(4):
+            side_copy(4 * i + e).wait_send()
+        for e in range(2):
+            for k in range(3):
+                block_copy(2 * i + e, k).wait_send()
+        last_copy(i).wait_send()
+        for tile in (2 * i, 2 * i + 1, CROSSED + i):
+            peer_wait(0, tile).wait_send()
+
+        @pl.when(i > 0)
+        def _():
+            for tile in (2 * i, 2 * i + 1):
+                peer_wait(1, tile).wait_send()
+
+        peer_wait(1, CROSSED + i).wait_send()
+        return carry
+
+    lax.fori_loop(0, PLANE, drain, 0)
+    grad_finish()
+    for e in range(4):
+        given_copy(2 * PLANE - 4 + e).wait_send()
+
+
+def spread_all(lhs, mlp, mixed, units, attended, given, grad):
+    tiles = 3 * PLANE
+    half = lhs.shape[2] // 2
+    share = half // 8
+    tokens = lhs.shape[3]
+    sources = (mlp, mixed, units, attended)
+    dma = pltpu.SemaphoreType.DMA
+    anywhere = pl.BlockSpec(memory_space=pl.ANY)
+    return pl.pallas_call(
+        spread_kernel,
+        out_shape=[
+            jax.ShapeDtypeStruct((share, QKV), jnp.float32),
+            jax.ShapeDtypeStruct((QD, share), jnp.float32),
+            jax.ShapeDtypeStruct((share, 2 * FF), jnp.float32),
+            jax.ShapeDtypeStruct((FF, share), jnp.float32),
+            jax.ShapeDtypeStruct((8, share), jnp.float32),
+            jax.ShapeDtypeStruct((2, *grad.shape), LOW),
+            *[jax.ShapeDtypeStruct(v.shape, LOW) for v in sources],
+        ],
+        in_specs=[anywhere] * 7,
+        out_specs=[pl.BlockSpec(memory_space=pltpu.VMEM)] * 5 + [anywhere] * 5,
+        scratch_shapes=[
+            pltpu.VMEM((2, lhs.shape[1], half, 2 * tokens), LOW),
+            pltpu.VMEM((3, 2 * tokens, TILE), LOW),
+            pltpu.VMEM((4, half, TILE), LOW),
+            pltpu.VMEM((4 * PLANE, half, TILE), LOW),
+            pltpu.VMEM((2 * PLANE, half, TILE), LOW),
+            pltpu.VMEM((2 * PLANE, 3, 2 * share, TILE), LOW),
+            pltpu.VMEM((PLANE, share + 8, TILE), LOW),
+            pltpu.VMEM((PLANE, share + 8, TILE), LOW),
+            pltpu.VMEM(grad.shape, LOW),
+            pltpu.VMEM((PLANE, share, TILE), jnp.float32),
+            dma((4,)),
+            dma((2,)),
+            dma((4, 3, 8)),
+            dma((2, tiles)),
+            dma((2, tiles)),
+            dma((3, 2)),
+            dma((4,)),
+            dma((CROSSED,)),
+            dma((4 * PLANE,)),
+            dma((4 * PLANE,)),
+            dma((2 * PLANE, 3)),
+            dma((2 * PLANE, 3)),
+            dma((PLANE,)),
+            dma((PLANE,)),
+        ],
+        compiler_params=pltpu.CompilerParams(
+            collective_id=2, has_side_effects=True, vmem_limit_bytes=62 * 2**20
+        ),
+        cost_estimate=long_cost(250),
+    )(lhs, *sources, grad, given)[:6]
+
+
+def on_device_pairs(
+    x_in, cotangent, w_qkv, w_out, w_gate_up, w_down, gains, order, visible, seq_ids
+):
+    section = lax.axis_index(SECTION)
+    column = lax.axis_index(CTX)
+    place = lax.axis_index(WSH)
+    core = place % 2
+    side = place // 2
+    rows = x_in.shape[2]
+    quarter = D // 4
+    share = quarter // 4
+    slot = column % 2 + 2 * core
+    first_section = section == 0
+
+    def partner(index):
+        z, w = index // 4, index % 4
+        if (z < 2) == (w % 2 == 1):
+            return ((z + 2) % 4) * 4 + (w ^ 1)
+        return index
+
+    pairs = [(i, partner(i)) for i in range(16)]
+    moving = (column < 2) == (core == 1)
+
+    def placed(value, layer):
+        crossing = [((1 - layer) * 16 + i, layer * 16 + j) for i, j in pairs]
+        other = lax.ppermute(value, (SECTION, CTX, WSH), crossing)
+        inside = [(layer * 16 + i, layer * 16 + j) for i, j in pairs if i != j]
+        return lax.ppermute(value, (SECTION, CTX, WSH), inside), value, other
+
+    def chosen(first, second):
+        return jnp.where(first_section, first, second)
+
+    def sorted_rows(value):
+        blocks = value.reshape(2, 2, share, value.shape[1])
+        return blocks.transpose(1, 0, 2, 3).reshape(value.shape)
+
+    gain_columns = jnp.concatenate(
+        [gains[0].T, jnp.zeros((quarter, SIDE - gains.shape[1]), LOW)], axis=1
+    )
+    shards = [
+        sorted_rows(jnp.concatenate([w_qkv[0], gain_columns], axis=1)),
+        sorted_rows(w_out[0].T),
+        sorted_rows(w_gate_up[0]),
+        sorted_rows(w_down[0].T),
+    ]
+    angles = pair_angles(order[section, slot], rows)
+    weights, saved_one, ahead, stores, info, gain_rows, early, natural = first_layer(
+        x_in, shards, seq_ids, angles, order, visible
+    )
+    upstream = cotangent[section, 0]
+    crossing = [(i, j) for i, j in pairs if i != j]
+    upstream, early = lax.optimization_barrier((upstream, early))
+    upstream = jnp.where(moving, lax.ppermute(upstream, (CTX, WSH), crossing), upstream)
+    grad_low = contract(upstream, natural, 1, 1).astype(LOW)
+    saved_two = pair_forward(1, ahead, weights, gain_rows, info, stores)
+    late = contract(saved_two["result"], natural, 1, 0).astype(LOW)
+
+    own, away = chosen(early, late), chosen(late, early)
+    swaps = [(s * 16 + i, (1 - s) * 16 + j) for s in range(2) for i, j in pairs]
+    other = lax.ppermute(away, (SECTION, CTX, WSH), swaps)
+    mine = lax.ppermute(own, (CTX, WSH), crossing)
+    shared = (weights, gain_rows, natural)
+    grad_two, turned, unused = pair_backward(
+        1, grad_low, shared, saved_two, info, angles, stores, early
+    )
+    grad_two, turned, mine, other = lax.optimization_barrier((grad_two, turned, mine, other))
+    mine = jnp.where(moving, mine, own)
+    activations = jnp.stack([chosen(mine, other), chosen(other, mine)])
+    later = placed(turned, 1)
+    grad_one, turned, later = pair_backward(
+        0, grad_two, shared, saved_one, info, angles, stores, later
+    )
+    names = ("lhs", "mlp", "mixed", "units", "attended", "given")
+    *shares, earlier = spread_all(*[stores[k] for k in names], turned)
+    later = (later[2], jnp.where(moving, later[0], later[1]))
+    input_grads = jnp.stack([chosen(earlier[m], later[m]).astype(jnp.float32) for m in range(2)])
+
+    share_in, share_head, share_mlp, share_down, share_gains = shares
+    return (
+        activations[None, :, None],
+        input_grads[None, :, None],
+        share_in[None],
+        share_head[None],
+        share_mlp[None],
+        share_down[None],
+        share_gains[None, :2],
+    )
+
+
 def solution(mesh):
     in_specs = (
         P(None, "wsh", "ctx", None),
@@ -440,6 +2424,7 @@
         P("section", None, ("ctx", "wsh")),
         P("section", None, ("ctx", "wsh")),
     )
+    body = on_device_pairs if fits_pairs(mesh) else on_device_general
     return jax.shard_map(
-        on_device, mesh=mesh, in_specs=in_specs, out_specs=out_specs, check_vma=False
-    )
+        body, mesh=mesh, in_specs=in_specs, out_specs=out_specs, check_vma=False
+    )

time: 2620 us -> 785 us (0.30)
  matrix products: 1320 us -> 10.4 us
  Pallas kernels: 0 us -> 724 us
  waiting for transfers between devices: 580 us -> 0.01 us
  other arithmetic: 408 us -> 9.51 us
  local copies, waits for them, and re-layouts: 202 us -> 20.1 us
  blocking collectives: 42.3 us -> 0 us
  between operations: 32.7 us -> 1.78 us
    dot_general x153 -> x2, matrix products: 1320 us -> 10.4 us  [contract(): lax.dot_general(left, right, (((left_dim,), (right_dim,)), ((), ())), pre...]
    pallas_call x0 -> x10, Pallas kernels: none -> 724 us  [the longest x1 281 us: spread_all(): pl.pallas_call(spread_kernel, out_shape=[jax.ShapeDtypeStruct((share, QKV...]
    reduce_scatter x8 -> x0, waiting for transfers between devices: 381 us -> none  [the longest x1 274 us: on_device(): lax.psum_scatter(term_gate_up, ('ctx', 'wsh'), scatter_dimension=0, tiled...]
    reduce_sum x29 -> x0, other arithmetic: 269 us -> none  [the longest x24 264 us: lse_step(): return ((top, total * jnp.exp(high - top) + jnp.sum(terms, axis=-1)), None)]
    all_gather x16 -> x0, waiting for transfers between devices: 133 us -> none  [the longest x6 64.1 us: layer_forward(): lax.all_gather(key_own, 'ctx', axis=0, tiled=True)]
    ppermute x4 -> x5, waiting for transfers between devices: 64.1 us -> 0.01 us  [the longest x1 0.01 us: on_device_pairs(): other = lax.ppermute(away, (SECTION, CTX, WSH), swaps)]
    slice x38 -> x0, local copies, waits for them, and re-layouts: 49.3 us -> none  [the longest x13 27.5 us: layer_forward(): mixed[:, :query_width].reshape(rows, H, HD)]
    unnamed x1 -> x0, blocking collectives: 33.4 us -> none
  transfers between devices with their start and end apart: 30 -> 5, of which waited for: 13 -> 0; matrix products, arithmetic and copies ran while one was open for 49% -> 2% of each run, Pallas kernels for 0% -> 23%
where the time goes in v3:
time: 785 us; the launch traced here: 776 us
  Pallas kernels  724 us (92%)
  local copies, waits for them, and re-layouts  20.1 us (3%)
  starting transfers between devices  10.6 us (1%)
  matrix products  10.4 us (1%)
  other arithmetic  9.51 us (1%)
    pallas_call x1, Pallas kernels, spread_all(): pl.pallas_call(spread_kernel, out_shape=[jax.ShapeDtypeStruct((share, QKV...  281 us
    pallas_call x1, Pallas kernels, first_layer(): pl.pallas_call(first_kernel, out_shape=[low(2, 4 * quarter, w) for w in w...  231 us
    pallas_call x2, Pallas kernels, call_mixed_backward(): pl.pallas_call(functools.partial(mixed_backward_kernel, layer), in_specs=...  60.5 us
    pallas_call x2, Pallas kernels, pair_attention_backward(): pl.pallas_call(backward_kernel, grid_spec=pltpu.PrefetchScalarGridSpec(nu...  58.8 us
    pallas_call x2, Pallas kernels, call_mlp_backward(): pl.pallas_call(functools.partial(mlp_backward_kernel, layer), grid=(steps...  49.6 us
    pallas_call x1, Pallas kernels, call_mlp_forward(): pl.pallas_call(mlp_forward_kernel, grid=(steps + 1,), in_specs=[whole((ro...  23.9 us
    pallas_call x1, Pallas kernels, pair_attention_forward(): pl.pallas_call(forward_kernel, grid_spec=pltpu.PrefetchScalarGridSpec(num...  18.9 us
  transfers between devices with their start and end apart: 5, of which 0 were waited for; matrix products, arithmetic and copies ran while one was open for 2% of the time, Pallas kernels for 23%

profile of v3, /device:TPU:0, one launch (start us, length us, event | category | flops | bytes accessed | tf_op | source)
XLA Modules:
  0.0 776.2 jit_solution(11089455294573402031)
XLA Ops:
  0.7 1.4 copy.26
  3.2 4.3 copy.29
  12.3 1.8 concatenate.10
  14.0 230.8 %shard_map.153 = (bf16[2,1152,2048]{2,1,0:T(8,128)(2,1)}, bf16[2,1152,1152]{2,1,0:T(8,128)(2,1)}, bf16[2,1152,3072]{2,1,0:T(8,128)(2,1)}, bf16[2,1152,3072]{2,1,...) custom-call(bf16[2,1,512,1152]{3,2,1,0:T(8,128)(2,1)} %refs_0_.1, ...), custom_call_target="tpu_custom_call" | custom-call | flops 230000001024 | bytes 1048576 | tf_op jit(solution)/shard_map/pallas_call | solution.py:1127
  244.9 1.7 collective-permute-start
  246.6 18.9 %shard_map.154 = (bf16[1152,512]{1,0:T(8,128)(2,1)}, f32[6,3,512]{2,1,0:T(4,128)}) custom-call(s32[8]{0:T(128)} %get-tuple-element.82.live_ref, bf16[1152,512]{1,0:T(8,128)(2,1)} %get-tuple-element.83.q_ref, bf16[4,12,64,512]{3,2,1,0:T(8,128)(2,1)} %get-tuple-element.88.k_ref.v_ref, bf16[4,12,64,512]{3,2,1,0:T(8,128)(2,1)} %get-tuple-element.88.k_ref.v_ref, ...), custom_call_target="tpu_custom_call" | custom-call | flops 19327352832 | bytes 12582912 | tf_op jit(solution)/shard_map/pallas_call | solution.py:569
  265.5 23.9 %shard_map.155 = (bf16[512,1152]{1,0:T(8,128)(2,1)}, f32[512,1152]{1,0:T(8,128)}, bf16[2,5,1152,512]{3,2,1,0:T(8,128)(2,1)}, bf16[2,3,512,384]{3,2,1,0:T(8,128)(...) custom-call(bf16[512,1152]{1,0:T(8,128)(2,1)} %get-tuple-element.87., ...), custom_call_target="tpu_custom_call", output_to_operand_aliasing={{2}: (7, {}), {3}: (8, {}), {4}: (9, {})} | custom-call | flops 24999999488 | bytes 1048576 | tf_op jit(solution)/shard_map/pallas_call | solution.py:1304
  289.3 5.7 broadcast_select_fusion.1
  295.0 1.7 collective-permute-start.1
  296.7 3.5 collective-permute-start.2
  300.2 4.7 convolution_convert_fusion.1.grad_ref
  304.9 24.9 %shard_map.156 = (bf16[2,16,512,384]{3,2,1,0:T(8,128)(2,1)}, bf16[2,5,1152,512]{3,2,1,0:T(8,128)(2,1)}, f32[512,1152]{1,0:T(8,128)}, bf16[1152,512]{1,0:T(8,128)(2,1)}, f32[8,1152]{1,0:T(8,128)}) custom-call(bf16[512,1152]{1,0:T(8,128)(2,1)} %convolution_convert_fusion.1.grad_ref, ...), custom_call_target="tpu_custom_call", output_to_operand_aliasing={{1}: (9, {})} | custom-call | flops 24999999488 | bytes 1048576 | tf_op jit(solution)/shard_map/pallas_call | solution.py:1433
  329.8 29.5 %shard_map.157 = (f32[1152,512]{1,0:T(8,128)}, bf16[4,6,64,512]{3,2,1,0:T(8,128)(2,1)}, bf16[4,6,64,512]{3,2,1,0:T(8,128)(2,1)}) custom-call(s32[8]{0:T(128)} %get-tuple-element.82.live_ref, bf16[1152,512]{1,0:T(8,128)(2,1)} %get-tuple-element.83.q_ref, bf16[1152,512]{1,0:T(8,128)(2,1)} %get-tuple-element.104.do_ref, ...), custom_call_target="tpu_custom_call" | custom-call | flops 48318382080 | bytes 12582912 | tf_op jit(solution)/shard_map/pallas_call | solution.py:602
  359.3 28.0 %shard_map.158 = (bf16[2,6,512,384]{3,2,1,0:T(8,128)(2,1)}, bf16[2,5,1152,512]{3,2,1,0:T(8,128)(2,1)}, bf16[512,1152]{1,0:T(8,128)(2,1)}, bf16[512,1152]{1,0:T(8,128)(2,1)}) custom-call(bf16[4,6,64,512]{3,2,1,0:T(8,128)(2,1)} %get-tuple-element.106.dk_ref, bf16[4,6,64,512]{3,2,1,0:T(8,128)(2,1)} %get-tuple-element.107.dv_ref, ...), custom_call_target="tpu_custom_call", output_to_operand_aliasing={{1}: (11, {})} | custom-call | flops 30000001024 | bytes 1048576 | tf_op jit(solution)/shard_map/pallas_call | solution.py:1704
  388.1 2.9 collective-permute-start.4
  391.0 24.8 %shard_map.159 = (bf16[2,16,512,384]{3,2,1,0:T(8,128)(2,1)}, bf16[2,5,1152,512]{3,2,1,0:T(8,128)(2,1)}, f32[512,1152]{1,0:T(8,128)}, bf16[1152,512]{1,0:T(8,128)(2,1)}, f32[8,1152]{1,0:T(8,128)}) custom-call(bf16[512,1152]{1,0:T(8,128)(2,1)} %get-tuple-element.121.grad_ref, ...), custom_call_target="tpu_custom_call", output_to_operand_aliasing={{1}: (9, {}), {0}: (10, {})} | custom-call | flops 24999999488 | bytes 1048576 | tf_op jit(solution)/shard_map/pallas_call | solution.py:1433
  415.8 29.3 %shard_map.160 = (f32[1152,512]{1,0:T(8,128)}, bf16[4,6,64,512]{3,2,1,0:T(8,128)(2,1)}, bf16[4,6,64,512]{3,2,1,0:T(8,128)(2,1)}) custom-call(s32[8]{0:T(128)} %get-tuple-element.82.live_ref, bf16[1152,512]{1,0:T(8,128)(2,1)} %get-tuple-element.120.q_ref, bf16[1152,512]{1,0:T(8,128)(2,1)} %get-tuple-element.127.do_ref, ...), custom_call_target="tpu_custom_call" | custom-call | flops 48318382080 | bytes 12582912 | tf_op jit(solution)/shard_map/pallas_call | solution.py:602
  445.1 3.3 select_bitcast_fusion.1
  448.5 32.4 %shard_map.161 = (bf16[2,6,512,384]{3,2,1,0:T(8,128)(2,1)}, bf16[2,5,1152,512]{3,2,1,0:T(8,128)(2,1)}, bf16[512,1152]{1,0:T(8,128)(2,1)}, bf16[512,1152]{1,0:T(8,128)(2,1)}, bf16[2,576,384]{2,1,0:T(8,128)(2,1)}) custom-call(bf16[4,6,64,512]{3,2,1,0:T(8,128)(2,1)} %get-tuple-element.131.dk_ref, ...), custom_call_target="tpu_custom_call", output_to_operand_aliasing={{1}: (11, {}), {0}: (12, {})} | custom-call | flops 30000001024 | bytes 1048576 | tf_op jit(solution)/shard_map/pallas_call | solution.py:1704
  480.9 281.3 %shard_map.162 = (f32[72,1920]{1,0:T(8,128)}, f32[1152,72]{1,0:T(8,128)}, f32[72,6144]{1,0:T(8,128)}, f32[3072,72]{1,0:T(8,128)}, f32[8,72]{1,0:T(8,128)}, /*ind...) custom-call(bf16[2,5,1152,512]{3,2,1,0:T(8,128)(2,1)} %get-tuple-ele, ...), custom_call_target="tpu_custom_call" | custom-call | flops 249999998976 | bytes 1048576 | tf_op jit(solution)/shard_map/pallas_call | solution.py:2270
  762.2 2.2 copy.33
  764.4 2.8 copy.34
  768.4 1.7 fusion.2
  770.4 3.5 maximum_bitcast_fusion
  (43 shorter events, 9.5 us)
Async XLA Ops:
  0.6 1.5 copy-start.10
  0.6 1.7 copy-start.7
  3.2 4.3 copy-start.3
  7.5 1.3 copy-start.11
  7.5 2.6 copy-start.8
  14.0 230.8 %copy-start.6 = (bf16[512,1152]{1,0:T(8,128)(2,1)S(1)}, bf16[512,1152]{1,0:T(8,128)(2,1)}, u32[]{:S(2)}) copy-start(bf16[512,1152]{1,0:T(8,128)(2,1)} %dynamic-slice_bitcast_fusion) | copy-start | bytes 3538948
  244.9 55.3 %collective-permute-start = (bf16[512,1152]{1,0:T(8,128)(2,1)S(1)}, bf16[512,1152]{1,0:T(8,128)(2,1)}, u32[]{:S(2)}, u32[]{:S(2)}) collective-permute-start(bf16[512,1152]{1,0:T(8,128)(2,1)S(1)} %copy-done.6), channel_id=1, source_target_pairs={{1,8},{3,10},{5,12},{7,14},{8,1},{10,3},{12,5},{14,7},{17,24},{19,... | collective-permute-start | bytes 3538952 | tf_op jit(solution)/shard_map/ppermute | solution.py:2368
  295.0 92.3 %collective-permute-start.1 = (bf16[512,1152]{1,0:T(8,128)(2,1)}, bf16[512,1152]{1,0:T(8,128)(2,1)}, u32[]{:S(2)}, u32[]{:S(2)}) collective-permute-start(bf16[512,1152]{1,0:T(8,128)(2,1)} %get-tuple-element.169), channel_id=1, source_target_pairs={{1,8},{3,10},{5,12},{7,14},{8,1},{10,3},{12,5},{14,7},{17,24},{19,... | collective-permute-start | bytes 3538952 | tf_op jit(solution)/shard_map/ppermute | solution.py:2376
  296.7 90.6 %collective-permute-start.2 = (bf16[512,1152]{1,0:T(8,128)(2,1)}, bf16[512,1152]{1,0:T(8,128)(2,1)}, u32[]{:S(2)}, u32[]{:S(2)}) collective-permute-start(bf16[512,1152]{1,0:T(8,128)(2,1)} %get-tuple-element.168), channel_id=1, source_target_pairs={{0,16},{1,24},{2,18},{3,26},{4,20},{5,28},{6,22},{7,30},{8,17},{9,... | collective-permute-start | bytes 3538952 | tf_op jit(solution)/shard_map/ppermute | solution.py:2375
  387.3 61.1 %collective-permute-start.3 = (bf16[512,1152]{1,0:T(8,128)(2,1)}, bf16[512,1152]{1,0:T(8,128)(2,1)S(1)}, u32[]{:S(2)}, u32[]{:S(2)}) collective-permute-start(bf16[512,1152]{1,0:T(8,128)(2,1)} %get-tuple-element.151), channel_id=1, source_target_pairs={{17,24},{19,26},{21,28},{23,30},{24,17},{26,19},{28,21},{30,23}} | collective-permute-start | bytes 3538952 | tf_op jit(solution)/shard_map/ppermute | solution.py:2343
  388.1 60.4 %collective-permute-start.4 = (bf16[512,1152]{1,0:T(8,128)(2,1)}, bf16[512,1152]{1,0:T(8,128)(2,1)}, u32[]{:S(2)}, u32[]{:S(2)}) collective-permute-start(bf16[512,1152]{1,0:T(8,128)(2,1)} %get-tuple-element.151), channel_id=1, source_target_pairs={{0,16},{1,24},{2,18},{3,26},{4,20},{5,28},{6,22},{7,30},{8,17},{9,... | collective-permute-start | bytes 3538952 | tf_op jit(solution)/shard_map/ppermute | solution.py:2341
  448.4 32.5 %copy-start.5 = (bf16[512,1152]{1,0:T(8,128)(2,1)}, bf16[512,1152]{1,0:T(8,128)(2,1)S(1)}, u32[]{:S(2)}) copy-start(bf16[512,1152]{1,0:T(8,128)(2,1)S(1)} %collective-permute-done.3) | copy-start | bytes 3538948
  762.2 6.2 copy-start.2
  768.4 1.7 copy-start
  768.4 2.0 copy-start.1
  770.4 3.5 copy-start.9
  770.4 4.3 copy-start.4
